TPU v7x, 128 devices: a whole 4x4x4 slice. The times are simulated.
128 devices in a mesh: pair: 32 (over z, y, core), aux: 4 (over x).
Axes of the slice: x: 4, y: 4, z: 4, core: 2. Of those that a mesh axis runs over, the one named last changes fastest.
Arguments:
- ac_factors: bfloat16 [9600, 128], P('aux'), may hold values from -6 to 6
- bd_factors: bfloat16 [2400, 4, 38400], P('pair', 'aux'), may hold values from -0.0625 to 0.0625
- amplitudes: float32 [24576, 8, 2400], P(('pair', 'aux')), may hold values from -0.046875 to 0.046875
Outputs:
- ladder: float32 [24576, 256], P(('pair', 'aux'))
All inputs are finite; a program needn't handle non-finite values.
Results may differ from a plain program's by a relative error of at most 0.0003.
Values sent between devices are 32-bit elements; how exact they have to be, the bound alone decides.
No kernel may reach another device: no remote copies, remote signals or barrier semaphores. Data moves between devices by JAX's collectives and lax.ppermute only.
A program may use at most 192 MiB of HBM per device.

v0:
```python
import jax
import jax.numpy as jnp
from jax import lax
from jax.sharding import PartitionSpec as P


def contract(integrals, amps):
    count_c = amps.shape[1]
    count_a = integrals.shape[0] // count_c
    shaped = integrals.reshape(count_a, count_c, integrals.shape[1], integrals.shape[2])
    return jnp.einsum("pcd,acbd->pab", amps, shaped, precision=lax.Precision.HIGHEST)


def body(ac_factors, bd_factors, amplitudes):
    local_rows = ac_factors.shape[0]
    columns_ac = ac_factors.shape[1]
    count_c = amplitudes.shape[1]
    count_a = columns_ac // count_c
    width_d = bd_factors.shape[0]
    block_b = bd_factors.shape[2] // local_rows
    own_pairs = amplitudes.shape[0]
    flat = bd_factors.reshape(width_d * block_b, local_rows)
    partial_ints = jnp.dot(flat, ac_factors, preferred_element_type=jnp.float32)
    partial_ints = partial_ints.reshape(width_d, block_b, columns_ac).transpose(2, 1, 0)
    summed = lax.psum(partial_ints, "aux")
    result = contract(lax.all_gather(summed, "pair", axis=2, tiled=True), amplitudes)
    return result.reshape(own_pairs, count_a * block_b)


def solution(mesh):
    placed = (P("aux", None), P("pair", "aux", None), P(("pair", "aux"), None, None))
    return jax.shard_map(
        body, mesh=mesh, in_specs=placed, out_specs=P(("pair", "aux"), None), check_vma=False
    )
```

profile of v0, /device:TPU:1, one launch (start us, length us, event | category | flops | bytes accessed | tf_op | source)
XLA Modules:
  0.0 204.5 jit_solution(8155947865148196963)
XLA Ops:
  6.5 0.0 copy-start
  6.5 0.0 all-reduce.2.cloned.1.call-start
  6.5 12.8 %dot_general.10 = bf16[75,16,2400]{2,1,0:T(8,128)(2,1)} reshape(bf16[75,1,38400]{2,0,1:T(8,128)(2,1)} %param.4) | data formatting | bytes 11520000 | tf_op jit(solution)/shard_map/dot_general | solution.py:23
  19.3 0.0 copy-done
  19.3 5.3 %convolution_bitcast_fusion = f32[128,16,75]{0,1,2:T(8,128)} fusion(bf16[75,16,2400]{2,1,0:T(8,128)(2,1)} %dot_general.10, bf16[2400,128]{1,0:T(8,128)(2,1)S(1)} %copy-done), kind=kOutput, calls=%fused_computation.3 | convolution fusion | flops 737280000 | bytes 6988800 | tf_op jit(solution)/shard_map/dot_general | solution.py:23
  24.6 0.0 all-reduce.2.cloned.1.call-update
  24.6 0.0 all-gather.2.cloned.1.call-start
  24.6 44.6 %all-reduce.2.cloned.1.call-done = f32[128,16,75]{0,1,2:T(8,128)} async-done(((f32[128,16,75]{0,1,2:T(8,128)}), f32[128,16,75]{0,1,2:T(8,128)}) %all-reduce.2.cloned.1.call-update) | async-done | bytes 614416 | tf_op jit(solution)/shard_map/psum | solution.py:25
  69.3 0.0 all-gather.2.cloned.1.call-update
  69.3 84.9 %all-gather.2.cloned.1.call-done = f32[128,16,2400]{0,1,2:T(8,128)} async-done(((f32[128,16,75]{0,1,2:T(8,128)}), f32[128,16,2400]{0,1,2:T(8,128)}) %all-gather.2.cloned.1.call-update) | async-done | bytes 19660816 | tf_op jit(solution)/shard_map/all_gather | solution.py:26
  154.2 19.8 %copy.10 = f32[128,16,2400]{2,1,0:T(8,128)} copy(f32[128,16,2400]{0,1,2:T(8,128)} %all-gather.2.cloned.1.call-done) | data formatting | bytes 39321600 | tf_op jit(solution)/shard_map/all_gather | solution.py:26
  174.0 0.0 copy-start.1
  174.0 22.8 %fusion = f32[16,16,192,1]{2,1,3,0:T(8,128)S(1)} fusion(f32[16,8,16,2400]{3,2,1,0:T(8,128)} %bitcast.19, f32[192,8,2400]{2,1,0:T(8,128)} %param.5), kind=kOutput, calls=%fused_computation | convolution fusion | flops 11324620800 | bytes 34603008 | tf_op jit(solution)/shard_map/pcd,acbd->pab/dot_general | solution.py:11
  196.8 0.8 copy.12
  197.6 0.0 copy-done.1
Async XLA Ops:
  6.5 12.8 %copy-start = (bf16[2400,128]{1,0:T(8,128)(2,1)S(1)}, bf16[2400,128]{1,0:T(8,128)(2,1)}, u32[]{:S(2)}) copy-start(bf16[2400,128]{1,0:T(8,128)(2,1)} %param.3) | copy-start | bytes 1843204
  6.5 62.7 %all-reduce.2.cloned.1.call-start = ((), (), s32[]{:S(2)}) async-start(), calls=%async_computation | async-start | bytes 1228800 | tf_op jit(solution)/shard_map/psum | solution.py:25
  24.6 129.6 %all-gather.2.cloned.1.call-start = ((), (), s32[]{:S(2)}) async-start(), calls=%async_computation.1 | async-start | bytes 20275200 | tf_op jit(solution)/shard_map/all_gather | solution.py:26
  174.0 23.6 %copy-start.1 = (bf16[2400,128]{1,0:T(8,128)(2,1)S(1)}, bf16[2400,128]{1,0:T(8,128)(2,1)}, u32[]{:S(2)}) copy-start(bf16[2400,128]{1,0:T(8,128)(2,1)} %param.3) | copy-start | bytes 1843204
Sparse Core Ops, SparseCore 0:
  24.7 44.5 all-reduce.1
  71.5 82.6 all-gather.1
where the time goes:
time: 205 us; the launch traced here: 204 us
  waiting for transfers between devices  130 us (63%)
  local copies, waits for them, and re-layouts  33.4 us (16%)
  matrix products  28.1 us (14%)
  between operations  13.4 us (7%)
    all_gather x1, waiting for transfers between devices, body(): lax.all_gather(summed, 'pair', axis=2, tiled=True)  84.9 us
    psum x1, waiting for transfers between devices, body(): summed = lax.psum(partial_ints, 'aux')  44.6 us
    dot_general x1, matrix products, contract(): jnp.einsum('pcd,acbd->pab', amps, shaped, precision=lax.Precision.HIGHEST)  22.8 us
    all_gather x1, local copies, waits for them, and re-layouts, body(): lax.all_gather(summed, 'pair', axis=2, tiled=True)  19.8 us
    dot_general x1, local copies, waits for them, and re-layouts, body(): partial_ints = jnp.dot(flat, ac_factors, preferred_element_type=jnp.float32)  12.8 us
    dot_general x1, matrix products, body(): partial_ints = jnp.dot(flat, ac_factors, preferred_element_type=jnp.float32)  5.26 us
  transfers between devices with their start and end apart: 2, of which 2 were waited for; matrix products, arithmetic and copies ran while one was open for 0% of the time, Pallas kernels for 0%

commit v1 on v0

v1 whole, which is shorter than its diff:
```python
import functools

import jax
import jax.numpy as jnp
from jax import lax
from jax.experimental import pallas as pl
from jax.experimental.pallas import tpu as pltpu
from jax.sharding import PartitionSpec as P

AXES = ("pair", "aux")
SIDE = 4
CORES = 2
CHIP_ROWS = 150
FRAME = 152
PARTS = ((0, 48, "xyz"), (48, 96, "yzx"), (96, 152, "zxy"))
WIDE = 16 * 56
REL = (0, 1, 3, 2)


def place(z, y, core, x):
    return (((z % SIDE) * SIDE + y % SIDE) * CORES + core) * SIDE + x % SIDE


def permute(value, step, axis, signed=True):
    pairs = []
    for z in range(SIDE):
        for y in range(SIDE):
            for core in range(CORES):
                for x in range(SIDE):
                    s = -step if signed and core else step
                    to = dict(z=z, y=y, core=core, x=x)
                    if axis == "core":
                        to["core"] = 1 - core
                    else:
                        to[axis] += s
                    pairs.append((place(z, y, core, x), place(**to)))
    return lax.ppermute(value, AXES, pairs)


def partial_kernel(slot_ref, bd_ref, ac_ref, swap_ref, out_ref, shifted):
    rows = ac_ref.shape[0]
    count_d = bd_ref.shape[0]
    block_b = bd_ref.shape[1] // rows
    ordered = jnp.dot(ac_ref[...], swap_ref[...], preferred_element_type=jnp.float32).astype(jnp.bfloat16)
    shifted[...] = jnp.zeros_like(shifted)
    for k in range(4):
        shifted[k, pl.ds((rows * k) % 128, rows), :] = ordered
    products = []
    for b in range(block_b):
        offset = (rows * b) % 128
        start = rows * b - offset
        length = -(-(offset + rows) // 128) * 128
        products.append(jnp.dot(bd_ref[:, start:start + length], shifted[b % 4, :length, :],
                                preferred_element_type=jnp.float32))
    out_ref[...] = jnp.zeros_like(out_ref)
    core = slot_ref[8]
    slabs = [jnp.concatenate([p[:, 16 * c:16 * c + 16] for p in products], axis=1) for c in range(8)]
    for which in range(CORES):
        @pl.when(core == which)
        def _():
            for c in range(8):
                out_ref[slot_ref[c], which * count_d:(which + 1) * count_d, :] = slabs[c]


def partial_integrals(slots, bd, ac, swap):
    rows = ac.shape[0]
    return pl.pallas_call(
        partial_kernel,
        out_shape=jax.ShapeDtypeStruct((8, FRAME, 256), jnp.float32),
        in_specs=[pl.BlockSpec(memory_space=pltpu.SMEM)] + [pl.BlockSpec(memory_space=pltpu.VMEM)] * 3,
        out_specs=pl.BlockSpec(memory_space=pltpu.VMEM),
        scratch_shapes=[pltpu.VMEM((4, -(-(rows + 96) // 128) * 128, 128), jnp.bfloat16)],
        compiler_params=pltpu.CompilerParams(vmem_limit_bytes=40 * 2**20),
        cost_estimate=pl.CostEstimate(flops=10**9, bytes_accessed=8 * 10**6, transcendentals=0),
    )(slots, bd, ac, swap)


def arrange_kernel(amp_ref, out_ref):
    for c in range(8):
        half, x = divmod(c, SIDE)
        row = amp_ref[:, c, :]
        row = jnp.concatenate([row, jnp.zeros((row.shape[0], 32), jnp.float32)], axis=1)
        for z in range(SIDE):
            for y in range(SIDE):
                at = dict(x=x, y=y, z=z)
                for j, (first, last, order) in enumerate(PARTS):
                    inner = (at[order[1]] * SIDE + at[order[0]]) * (last - first)
                    begin = CHIP_ROWS * (z * SIDE + y) + first
                    out_ref[half, SIDE * j + at[order[2]], :, inner:inner + last - first] = row[:, begin:begin + last - first]


def arrange(amps):
    pairs = amps.shape[0]
    step = 16
    return pl.pallas_call(
        arrange_kernel,
        grid=(pairs // step,),
        out_shape=jax.ShapeDtypeStruct((2, 12, pairs, WIDE), jnp.float32),
        in_specs=[pl.BlockSpec((step,) + amps.shape[1:], lambda i: (i, 0, 0))],
        out_specs=pl.BlockSpec((2, 12, step, WIDE), lambda i: (0, 0, i, 0)),
        compiler_params=pltpu.CompilerParams(vmem_limit_bytes=40 * 2**20),
        cost_estimate=pl.CostEstimate(flops=10**6, bytes_accessed=30 * 10**6, transcendentals=0),
    )(amps)


def split(value):
    high = value.astype(jnp.bfloat16)
    return high, (value - high.astype(jnp.float32)).astype(jnp.bfloat16)


def ladder_kernel(piece_ref, own_ref, other_ref, order_ref, *refs):
    pieces, out_ref, total = refs[:15], refs[15], refs[16]
    step = pl.program_id(0)

    @pl.when(step == 0)
    def _():
        total[...] = jnp.zeros_like(total)

    for k in range(12):
        @pl.when(step == k)
        def _():
            j, kind = divmod(k, 4)
            if kind < 3:
                block = pieces[5 * j + kind][...]
            else:
                block = jnp.concatenate([pieces[5 * j + 3][...], pieces[5 * j + 4][...]], axis=0)
            high, low = split(block)
            depth = block.shape[0]
            for r, amp_ref in enumerate((own_ref, other_ref)):
                ahigh, alow = split(amp_ref[:, :depth])
                dot = functools.partial(jnp.dot, preferred_element_type=jnp.float32)
                total[r] += dot(ahigh, high) + (dot(ahigh, low) + dot(alow, high))

    @pl.when(step == 11)
    def _():
        for r in range(2):
            out_ref[r] = jnp.dot(total[r], order_ref[...], precision=lax.Precision.HIGHEST,
                                 preferred_element_type=jnp.float32)


def ladder(ids, own, other, order, pieces):
    pairs = own.shape[1]
    amp_spec = pl.BlockSpec((None, pairs, WIDE), lambda k, ids: (ids[k], 0, 0))
    whole = pl.BlockSpec(memory_space=pltpu.VMEM)
    return pl.pallas_call(
        ladder_kernel,
        grid_spec=pltpu.PrefetchScalarGridSpec(
            num_scalar_prefetch=1,
            grid=(12,),
            in_specs=[amp_spec, amp_spec, whole] + [whole] * 15,
            out_specs=whole,
            scratch_shapes=[pltpu.VMEM((2, pairs, 256), jnp.float32)],
        ),
        out_shape=jax.ShapeDtypeStruct((2, pairs, 256), jnp.float32),
        compiler_params=pltpu.CompilerParams(vmem_limit_bytes=40 * 2**20),
        cost_estimate=pl.CostEstimate(flops=6 * 10**9, bytes_accessed=25 * 10**6, transcendentals=0),
    )(ids, own, other, order, *pieces)


def gather(value, axis, coord, sign):
    rows = value.shape[0]
    got = ((coord, value), (coord - sign, permute(value, 1, axis)), (coord + sign, permute(value, -1, axis)),
           (coord + 2, permute(value, 2, axis)))
    whole = jnp.zeros((SIDE * rows, value.shape[1]), jnp.float32)
    for at, block in got:
        whole = lax.dynamic_update_slice(whole, block, ((at % SIDE) * rows, 0))
    return whole


def body(ac_factors, bd_factors, amplitudes):
    pair, x = lax.axis_index("pair"), lax.axis_index("aux")
    core = pair % CORES
    at = dict(x=x, y=(pair // CORES) % SIDE, z=pair // (CORES * SIDE))
    sign = 1 - 2 * core
    column = jnp.arange(128)
    swap = (column[:, None] % 8 * 16 + column[:, None] // 8 == column[None, :]).astype(jnp.bfloat16)
    column = jnp.arange(256)
    order = (column[:, None] % 16 * 16 + column[:, None] // 16 == column[None, :]).astype(jnp.float32)
    c = jnp.arange(8)
    ahead = (c % SIDE - x) % SIDE
    slot = jnp.where(ahead == 2, 3, jnp.where(ahead == 3, 2, ahead)) + jnp.where(c // SIDE == core, 0, 4)
    slots = jnp.concatenate([slot, core[None]]).astype(jnp.int32)

    bd = bd_factors.reshape(bd_factors.shape[0], bd_factors.shape[2])
    ints = partial_integrals(slots, bd, ac_factors, swap)
    chip = ints[:4] + permute(ints[4:], 0, "core")
    shard = chip[0] + permute(chip[1], 1, "x", False) + permute(chip[2], -1, "x", False) + permute(chip[3], 2, "x", False)

    arranged = arrange(amplitudes)
    own = lax.dynamic_index_in_dim(arranged, core, 0, False)
    other = permute(lax.dynamic_index_in_dim(arranged, 1 - core, 0, False), 0, "core")

    values = [shard[first:last] for first, last, _ in PARTS]
    values = [gather(v, order_[0], at[order_[0]], sign) for v, (_, _, order_) in zip(values, PARTS)]
    values = [gather(v, order_[1], at[order_[1]], sign) for v, (_, _, order_) in zip(values, PARTS)]
    ups = [permute(v, 1, order_[2]) for v, (_, _, order_) in zip(values, PARTS)]
    downs = [permute(v, -1, order_[2]) for v, (_, _, order_) in zip(values, PARTS)]
    half = [v.shape[0] // 2 for v in values]
    far_up = [permute(v[:h], 1, order_[2]) for v, h, (_, _, order_) in zip(ups, half, PARTS)]
    far_down = [permute(v[h:], -1, order_[2]) for v, h, (_, _, order_) in zip(downs, half, PARTS)]
    pieces, ids = [], []
    for j, (_, _, order_) in enumerate(PARTS):
        pieces += [values[j], ups[j], downs[j], far_up[j], far_down[j]]
        mine = at[order_[2]]
        ids += [4 * j + (mine + s) % SIDE for s in (0, -sign, sign, 2)]
    both = ladder(jnp.stack(ids).astype(jnp.int32), own, other, order, pieces)
    return both[0] + permute(both[1], 0, "core")


def solution(mesh):
    placed = (P("aux", None), P("pair", "aux", None), P(("pair", "aux"), None, None))
    return jax.shard_map(
        body, mesh=mesh, in_specs=placed, out_specs=P(("pair", "aux"), None), check_vma=False
    )
```

time: 205 us -> 190 us (0.927)
  waiting for transfers between devices: 130 us -> 68.4 us
  starting transfers between devices: 0.04 us -> 51.9 us
  Pallas kernels: 0 us -> 38.4 us
  matrix products: 28.1 us -> 0 us
  between operations: 13.4 us -> 0.42 us
  local copies, waits for them, and re-layouts: 33.4 us -> 28.4 us
    all_gather x1 -> x0, waiting for transfers between devices: 84.9 us -> none  [body(): lax.all_gather(summed, 'pair', axis=2, tiled=True)]
    ppermute x0 -> x36, waiting for transfers between devices: none -> 68.4 us  [permute(): return lax.ppermute(value, AXES, pairs)]
    ppermute x0 -> x36, starting transfers between devices: none -> 51.9 us  [permute(): return lax.ppermute(value, AXES, pairs)]
    psum x1 -> x0, waiting for transfers between devices: 44.6 us -> none  [body(): summed = lax.psum(partial_ints, 'aux')]
    pallas_call x0 -> x3, Pallas kernels: none -> 38.4 us  [the longest x1 19.7 us: arrange(): pl.pallas_call(arrange_kernel, grid=(pairs // step,), out_shape=jax.Shape...]
    dot_general x2 -> x0, matrix products: 28.1 us -> none  [the longest x1 22.8 us: contract(): jnp.einsum('pcd,acbd->pab', amps, shaped, precision=lax.Precision.HIGHEST)]
    all_gather x1 -> x0, local copies, waits for them, and re-layouts: 19.8 us -> none  [body(): lax.all_gather(summed, 'pair', axis=2, tiled=True)]
    unnamed x4 -> x32, local copies, waits for them, and re-layouts: 0.01 us -> 12.9 us
  transfers between devices with their start and end apart: 2 -> 36, of which waited for: 2 -> 13; matrix products, arithmetic and copies ran while one was open for 0% -> 2% of each run, Pallas kernels for 0% -> 2%
where the time goes in v1:
time: 190 us; the launch traced here: 189 us
  waiting for transfers between devices  68.4 us (36%)
  starting transfers between devices  51.9 us (27%)
  Pallas kernels  38.4 us (20%)
  local copies, waits for them, and re-layouts  28.4 us (15%)
    ppermute x36, waiting for transfers between devices, permute(): return lax.ppermute(value, AXES, pairs)  68.4 us
    ppermute x36, starting transfers between devices, permute(): return lax.ppermute(value, AXES, pairs)  51.9 us
    pallas_call x1, Pallas kernels, arrange(): pl.pallas_call(arrange_kernel, grid=(pairs // step,), out_shape=jax.Shape...  19.7 us
    pallas_call x1, Pallas kernels, ladder(): pl.pallas_call(ladder_kernel, grid_spec=pltpu.PrefetchScalarGridSpec(num_...  15 us
    unnamed x32, local copies, waits for them, and re-layouts  12.9 us
    squeeze x1, local copies, waits for them, and re-layouts, body(): lax.dynamic_index_in_dim(arranged, 1 - core, 0, False)  11.6 us
  transfers between devices with their start and end apart: 36, of which 13 were waited for; matrix products, arithmetic and copies ran while one was open for 2% of the time, Pallas kernels for 2%

profile of v1, /device:TPU:1, one launch (start us, length us, event | category | flops | bytes accessed | tf_op | source)
XLA Modules:
  0.0 188.6 jit_solution(12053546843033203923)
XLA Ops:
  0.0 19.7 %shard_map.37 = f32[2,12,192,896]{3,2,1,0:T(8,128)} custom-call(f32[192,8,2400]{2,1,0:T(8,128)} %amp_ref.1), custom_call_target="tpu_custom_call" | custom-call | flops 1000000 | bytes 30000000 | tf_op jit(solution)/shard_map/pallas_call | solution.py:95
  19.7 11.6 %dynamic-slice_bitcast_fusion = (f32[12,192,896]{2,1,0:T(8,128)}, f32[12,192,896]{2,1,0:T(8,128)}) fusion(f32[2,12,192,896]{3,2,1,0:T(8,128)} %shard_map.37, s32[]{:T(128)S(6)} %select_n.284, s32[]{:T(128)S(6)} %select_n.283), kind=kLoop, calls=%fused_computation | loop fusion | bytes 33030152 | tf_op jit(solution)/shard_map/jit(dynamic_index_in_dim)/squeeze | solution.py:191
  31.3 1.4 collective-permute-start
  32.9 2.7 %copy-done = bf16[75,1,38400]{2,0,1:T(8,128)(2,1)S(1)} copy-done((bf16[75,1,38400]{2,0,1:T(8,128)(2,1)S(1)}, bf16[75,1,38400]{2,0,1:T(8,128)(2,1)}, u32[]{:S(2)}) %copy-start) | copy-done | bytes 5760024
  35.6 3.7 %shard_map.38 = f32[8,152,256]{2,1,0:T(8,128)S(1)} custom-call(s32[9]{0:T(128)S(1)} %pad_add_fusion.slot_ref, bf16[75,38400]{1,0:T(8,128)(2,1)S(1)} %bitcast.38, bf16[2400,128]{1,0:T(8,128)(2,1)S(1)} %copy-done.11, bf16[128,128]{1,0:T(8,128)(2,1)S(1)} %fusion.5.swap_ref), custom_call_target="tpu_custom_call" | custom-call | flops 1000000000 | bytes 8000000 | tf_op jit(solution)/shard_map/pallas_call | solution.py:67
  39.4 0.1 collective-permute-start.1
  39.4 6.7 %collective-permute-done.1 = f32[4,152,256]{2,1,0:T(8,128)S(1)} collective-permute-done((f32[4,152,256]{2,1,0:T(8,128)S(1)}, f32[4,152,256]{2,1,0:T(8,128)S(1)}, u32[]{:S(2)}, u32[]{:S(2)}) %collective-permute-start.1) | collective-permute-done | bytes 622624 | tf_op jit(solution)/shard_map/ppermute | solution.py:37
  46.3 2.9 %collective-permute-start.4 = (f32[152,256]{1,0:T(8,128)S(1)}, f32[152,256]{1,0:T(8,128)S(1)}, u32[]{:S(2)}, u32[]{:S(2)}) collective-permute-start(f32[152,256]{1,0:T(8,128)S(1)} %get-tuple-element.8), channel_id=1, source_target_pairs={{0,2},{1,3},{2,0},{3,1},{4,6},{5,7},{6,4},{7,5},{8,10},{9,11},{10,... | collective-permute-start | bytes 466952 | tf_op jit(solution)/shard_map/ppermute | solution.py:37
  49.2 0.9 collective-permute-start.3
  50.1 0.6 collective-permute-start.2
  50.7 2.4 %collective-permute-done.4 = f32[152,256]{1,0:T(8,128)S(1)} collective-permute-done((f32[152,256]{1,0:T(8,128)S(1)}, f32[152,256]{1,0:T(8,128)S(1)}, u32[]{:S(2)}, u32[]{:S(2)}) %collective-permute-start.4) | collective-permute-done | bytes 155680 | tf_op jit(solution)/shard_map/ppermute | solution.py:37
  53.1 3.5 %collective-permute-done.3 = f32[152,256]{1,0:T(8,128)S(1)} collective-permute-done((f32[152,256]{1,0:T(8,128)S(1)}, f32[152,256]{1,0:T(8,128)S(1)}, u32[]{:S(2)}, u32[]{:S(2)}) %collective-permute-start.3) | collective-permute-done | bytes 155680 | tf_op jit(solution)/shard_map/ppermute | solution.py:37
  56.7 3.1 %collective-permute-start.5 = (f32[48,256]{1,0:T(8,128)S(1)}, f32[48,256]{1,0:T(8,128)S(1)}, u32[]{:S(2)}, u32[]{:S(2)}) collective-permute-start(f32[48,256]{1,0:T(8,128)S(1)} %get-tuple-element.14), channel_id=1, source_target_pairs={{0,1},{1,2},{2,3},{3,0},{4,7},{5,4},{6,5},{7,6},{8,9},{9,10},{10,1... | collective-permute-start | bytes 147464 | tf_op jit(solution)/shard_map/ppermute | solution.py:37
  59.9 1.7 collective-permute-start.7
  61.6 2.7 %collective-permute-start.15 = (f32[48,256]{1,0:T(8,128)S(1)}, f32[48,256]{1,0:T(8,128)S(1)}, u32[]{:S(2)}, u32[]{:S(2)}) collective-permute-start(f32[48,256]{1,0:T(8,128)S(1)} %get-tuple-element.12), channel_id=1, source_target_pairs={{0,8},{1,9},{2,10},{3,11},{4,28},{5,29},{6,30},{7,31},{8,16},{9,17... | collective-permute-start | bytes 147464 | tf_op jit(solution)/shard_map/ppermute | solution.py:37
  64.6 2.9 %collective-permute-start.17 = (f32[48,256]{1,0:T(8,128)S(1)}, f32[48,256]{1,0:T(8,128)S(1)}, u32[]{:S(2)}, u32[]{:S(2)}) collective-permute-start(f32[48,256]{1,0:T(8,128)S(1)} %get-tuple-element.12), channel_id=1, source_target_pairs={{0,16},{1,17},{2,18},{3,19},{4,20},{5,21},{6,22},{7,23},{8,24},{9,... | collective-permute-start | bytes 147464 | tf_op jit(solution)/shard_map/ppermute | solution.py:37
  67.5 3.8 %collective-permute-start.25 = (f32[56,256]{1,0:T(8,128)S(1)}, f32[56,256]{1,0:T(8,128)S(1)}, u32[]{:S(2)}, u32[]{:S(2)}) collective-permute-start(f32[56,256]{1,0:T(8,128)S(1)} %get-tuple-element.10), channel_id=1, source_target_pairs={{0,32},{1,33},{2,34},{3,35},{4,100},{5,101},{6,102},{7,103},{8,40}... | collective-permute-start | bytes 172040 | tf_op jit(solution)/shard_map/ppermute | solution.py:37
  71.5 1.4 collective-permute-start.27
  72.9 0.8 collective-permute-start.8
  73.8 0.8 collective-permute-start.9
  74.5 1.8 collective-permute-done.26
  76.3 0.4 collective-permute-start.10
  76.8 2.0 %collective-permute-start.18 = (f32[192,256]{1,0:T(8,128)S(1)}, f32[192,256]{1,0:T(8,128)S(1)}, u32[]{:S(2)}, u32[]{:S(2)}) collective-permute-start(f32[192,256]{1,0:T(8,128)S(1)} %constant_dynamic-update-slice_fusion.12), channel_id=1, source_target_pairs={{0,32},{1,33},{2,34},{3,35},{4,100},{5,101},{6,102},{7,103},{8,40}... | collective-permute-start | bytes 589832 | tf_op jit(solution)/shard_map/ppermute | solution.py:37
  78.9 1.1 collective-permute-start.28
  80.0 0.5 collective-permute-done.9
  80.5 6.7 %collective-permute-start.29 = (f32[224,256]{1,0:T(8,128)S(1)}, f32[224,256]{1,0:T(8,128)S(1)}, u32[]{:S(2)}, u32[]{:S(2)}) collective-permute-start(f32[224,256]{1,0:T(8,128)S(1)} %constant_dynamic-update-slice_fusion.4), channel_id=1, source_target_pairs={{0,3},{1,0},{2,1},{3,2},{4,5},{5,6},{6,7},{7,4},{8,11},{9,8},{10,9... | collective-permute-start | bytes 688136 | tf_op jit(solution)/shard_map/ppermute | solution.py:37
  87.3 1.3 collective-permute-start.30
  88.7 2.0 %collective-permute-start.11 = (f32[768,256]{1,0:T(8,128)S(1)}, f32[768,256]{1,0:T(8,128)S(1)}, u32[]{:S(2)}, u32[]{:S(2)}) collective-permute-start(f32[768,256]{1,0:T(8,128)S(1)} %constant_dynamic-update-slice_fusion.16.refs_0_), channel_id=1, source_target_pairs={{0,32},{1,33},{2,34},{3,35},{4,100},{5,101},{6,102},{7,103},{8,40}... | collective-permute-start | bytes 2359304 | tf_op jit(solution)/shard_map/ppermute | solution.py:37
  90.6 0.2 collective-permute-start.12
  90.8 0.7 collective-permute-done.29
  91.5 4.2 %collective-permute-start.19 = (f32[192,256]{1,0:T(8,128)S(1)}, f32[192,256]{1,0:T(8,128)S(1)}, u32[]{:S(2)}, u32[]{:S(2)}) collective-permute-start(f32[192,256]{1,0:T(8,128)S(1)} %constant_dynamic-update-slice_fusion.12), channel_id=1, source_target_pairs={{0,96},{1,97},{2,98},{3,99},{4,36},{5,37},{6,38},{7,39},{8,104},{9... | collective-permute-start | bytes 589832 | tf_op jit(solution)/shard_map/ppermute | solution.py:37
  95.8 2.2 %collective-permute-done.30 = f32[224,256]{1,0:T(8,128)S(1)} collective-permute-done((f32[224,256]{1,0:T(8,128)S(1)}, f32[224,256]{1,0:T(8,128)S(1)}, u32[]{:S(2)}, u32[]{:S(2)}) %collective-permute-start.30) | collective-permute-done | bytes 229408 | tf_op jit(solution)/shard_map/ppermute | solution.py:37
  97.9 2.4 %collective-permute-start.20 = (f32[192,256]{1,0:T(8,128)S(1)}, f32[192,256]{1,0:T(8,128)S(1)}, u32[]{:S(2)}, u32[]{:S(2)}) collective-permute-start(f32[192,256]{1,0:T(8,128)S(1)} %constant_dynamic-update-slice_fusion.12), channel_id=1, source_target_pairs={{0,64},{1,65},{2,66},{3,67},{4,68},{5,69},{6,70},{7,71},{8,72},{9,... | collective-permute-start | bytes 589832 | tf_op jit(solution)/shard_map/ppermute | solution.py:37
  100.3 17.1 %collective-permute-done.19 = f32[192,256]{1,0:T(8,128)S(1)} collective-permute-done((f32[192,256]{1,0:T(8,128)S(1)}, f32[192,256]{1,0:T(8,128)S(1)}, u32[]{:S(2)}, u32[]{:S(2)}) %collective-permute-start.19) | collective-permute-done | bytes 196640 | tf_op jit(solution)/shard_map/ppermute | solution.py:37
  117.4 1.5 collective-permute-start.32
  119.1 0.9 collective-permute-start.21
  120.0 0.6 collective-permute-start.22
  120.7 18.6 %collective-permute-done.31.refs_11_ = f32[896,256]{1,0:T(8,128)S(1)} collective-permute-done((f32[896,256]{1,0:T(8,128)S(1)}, f32[896,256]{1,0:T(8,128)S(1)}, u32[]{:S(2)}, u32[]{:S(2)}) %collective-permute-start.31) | collective-permute-done | bytes 917536 | tf_op jit(solution)/shard_map/ppermute | solution.py:37
  139.3 1.5 collective-permute-start.14
  140.9 0.8 slice.81
  141.7 0.8 slice.82
  142.5 0.4 collective-permute-start.33
  142.9 1.1 collective-permute-start.34
  144.0 0.8 slice.78
  144.8 0.9 copy-done.7
  145.8 0.8 slice.79
  146.5 2.4 %collective-permute-done.13.refs_3_ = f32[384,256]{1,0:T(8,128)S(1)} collective-permute-done((f32[384,256]{1,0:T(8,128)S(1)}, f32[384,256]{1,0:T(8,128)S(1)}, u32[]{:S(2)}, u32[]{:S(2)}) %collective-permute-start.13) | collective-permute-done | bytes 393248 | tf_op jit(solution)/shard_map/ppermute | solution.py:37
  149.0 0.7 copy-done.12
  149.7 2.1 %collective-permute-start.23 = (f32[384,256]{1,0:T(8,128)}, f32[384,256]{1,0:T(8,128)}, u32[]{:S(2)}, u32[]{:S(2)}) collective-permute-start(f32[384,256]{1,0:T(8,128)} %slice.78), channel_id=1, source_target_pairs={{0,1},{1,2},{2,3},{3,0},{4,7},{5,4},{6,5},{7,6},{8,9},{9,10},{10,1... | collective-permute-start | bytes 1179656 | tf_op jit(solution)/shard_map/ppermute | solution.py:37
  151.8 0.7 copy-done.14
  152.5 0.1 stack.51.piece_ref
  152.6 0.1 fusion.order_ref
  152.7 6.0 %collective-permute-done.23.refs_8_ = f32[384,256]{1,0:T(8,128)} collective-permute-done((f32[384,256]{1,0:T(8,128)}, f32[384,256]{1,0:T(8,128)}, u32[]{:S(2)}, u32[]{:S(2)}) %collective-permute-start.23) | collective-permute-done | bytes 393248 | tf_op jit(solution)/shard_map/ppermute | solution.py:37
  158.8 4.8 %collective-permute-done.24.refs_9_ = f32[384,256]{1,0:T(8,128)} collective-permute-done((f32[384,256]{1,0:T(8,128)}, f32[384,256]{1,0:T(8,128)}, u32[]{:S(2)}, u32[]{:S(2)}) %collective-permute-start.24) | collective-permute-done | bytes 393248 | tf_op jit(solution)/shard_map/ppermute | solution.py:37
  163.6 1.2 copy-done.2
  164.8 1.1 copy-done.4
  165.9 1.1 copy-done.6
  167.0 1.1 copy-done.8
  168.2 1.1 copy-done.10
  169.3 1.0 copy-done.13
  170.3 1.0 copy-done.15
  171.3 15.0 %shard_map.39 = f32[2,192,256]{2,1,0:T(8,128)S(1)} custom-call(s32[12]{0:T(128)S(1)} %stack.51.piece_ref, f32[12,192,896]{2,1,0:T(8,128)} %get-tuple-element.6.own_ref, f32[12,192,896]{2,1,0:T(8,128)} %collective-permute-done.other_ref, f32[256,256]{1,0:T(8,128)S(1)} %fusion.order_ref, f32[768,256]{1,0:T(8,128)S(1)} %constant_dynamic-update-slice_fusion.16.refs_0_, ...), custom_call_target="tpu_custom_call" | custom-call | flops 6000000000 | bytes 25000000 | tf_op jit(solution)/shard_map/pallas_call | solution.py:145
  186.4 1.4 collective-permute-done.35
  187.9 0.7 fusion.1
  (93 shorter events, 1.4 us)
Async XLA Ops:
  19.7 13.2 %copy-start.11 = (bf16[2400,128]{1,0:T(8,128)(2,1)S(1)}, bf16[2400,128]{1,0:T(8,128)(2,1)}, u32[]{:S(2)}) copy-start(bf16[2400,128]{1,0:T(8,128)(2,1)} %ac_ref.1) | copy-start | bytes 1843204
  31.3 132.3 %collective-permute-start = (f32[12,192,896]{2,1,0:T(8,128)}, f32[12,192,896]{2,1,0:T(8,128)}, u32[]{:S(2)}, u32[]{:S(2)}) collective-permute-start(f32[12,192,896]{2,1,0:T(8,128)} %get-tuple-element.5), channel_id=1, source_target_pairs={{0,4},{1,5},{2,6},{3,7},{4,0},{5,1},{6,2},{7,3},{8,12},{9,13},{10,... | collective-permute-start | bytes 24772616 | tf_op jit(solution)/shard_map/ppermute | solution.py:37
  32.9 2.7 %copy-start = (bf16[75,1,38400]{2,0,1:T(8,128)(2,1)S(1)}, bf16[75,1,38400]{2,0,1:T(8,128)(2,1)}, u32[]{:S(2)}) copy-start(bf16[75,1,38400]{2,0,1:T(8,128)(2,1)} %param.4) | copy-start | bytes 17280004
  39.4 6.8 %collective-permute-start.1 = (f32[4,152,256]{2,1,0:T(8,128)S(1)}, f32[4,152,256]{2,1,0:T(8,128)S(1)}, u32[]{:S(2)}, u32[]{:S(2)}) collective-permute-start(f32[4,152,256]{2,1,0:T(8,128)S(1)} %slice.69), channel_id=1, source_target_pairs={{0,4},{1,5},{2,6},{3,7},{4,0},{5,1},{6,2},{7,3},{8,12},{9,13},{10,... | collective-permute-start | bytes 1867784 | tf_op jit(solution)/shard_map/ppermute | solution.py:37
  46.3 6.8 %collective-permute-start.4 = (f32[152,256]{1,0:T(8,128)S(1)}, f32[152,256]{1,0:T(8,128)S(1)}, u32[]{:S(2)}, u32[]{:S(2)}) collective-permute-start(f32[152,256]{1,0:T(8,128)S(1)} %get-tuple-element.8), channel_id=1, source_target_pairs={{0,2},{1,3},{2,0},{3,1},{4,6},{5,7},{6,4},{7,5},{8,10},{9,11},{10,... | collective-permute-start | bytes 466952 | tf_op jit(solution)/shard_map/ppermute | solution.py:37
  49.2 7.4 %collective-permute-start.3 = (f32[152,256]{1,0:T(8,128)S(1)}, f32[152,256]{1,0:T(8,128)S(1)}, u32[]{:S(2)}, u32[]{:S(2)}) collective-permute-start(f32[152,256]{1,0:T(8,128)S(1)} %get-tuple-element.9), channel_id=1, source_target_pairs={{0,3},{1,0},{2,1},{3,2},{4,7},{5,4},{6,5},{7,6},{8,11},{9,8},{10,9... | collective-permute-start | bytes 466952 | tf_op jit(solution)/shard_map/ppermute | solution.py:37
  50.1 6.6 %collective-permute-start.2 = (f32[152,256]{1,0:T(8,128)S(1)}, f32[152,256]{1,0:T(8,128)S(1)}, u32[]{:S(2)}, u32[]{:S(2)}) collective-permute-start(f32[152,256]{1,0:T(8,128)S(1)} %get-tuple-element.7), channel_id=1, source_target_pairs={{0,1},{1,2},{2,3},{3,0},{4,5},{5,6},{6,7},{7,4},{8,9},{9,10},{10,1... | collective-permute-start | bytes 466952 | tf_op jit(solution)/shard_map/ppermute | solution.py:37
  56.7 7.7 %collective-permute-start.5 = (f32[48,256]{1,0:T(8,128)S(1)}, f32[48,256]{1,0:T(8,128)S(1)}, u32[]{:S(2)}, u32[]{:S(2)}) collective-permute-start(f32[48,256]{1,0:T(8,128)S(1)} %get-tuple-element.14), channel_id=1, source_target_pairs={{0,1},{1,2},{2,3},{3,0},{4,7},{5,4},{6,5},{7,6},{8,9},{9,10},{10,1... | collective-permute-start | bytes 147464 | tf_op jit(solution)/shard_map/ppermute | solution.py:37
  59.9 4.7 %collective-permute-start.6 = (f32[48,256]{1,0:T(8,128)S(1)}, f32[48,256]{1,0:T(8,128)S(1)}, u32[]{:S(2)}, u32[]{:S(2)}) collective-permute-start(f32[48,256]{1,0:T(8,128)S(1)} %get-tuple-element.14), channel_id=1, source_target_pairs={{0,3},{1,0},{2,1},{3,2},{4,5},{5,6},{6,7},{7,4},{8,11},{9,8},{10,9... | collective-permute-start | bytes 147464 | tf_op jit(solution)/shard_map/ppermute | solution.py:37
  59.9 7.6 %collective-permute-start.7 = (f32[48,256]{1,0:T(8,128)S(1)}, f32[48,256]{1,0:T(8,128)S(1)}, u32[]{:S(2)}, u32[]{:S(2)}) collective-permute-start(f32[48,256]{1,0:T(8,128)S(1)} %get-tuple-element.14), channel_id=1, source_target_pairs={{0,2},{1,3},{2,0},{3,1},{4,6},{5,7},{6,4},{7,5},{8,10},{9,11},{10,... | collective-permute-start | bytes 147464 | tf_op jit(solution)/shard_map/ppermute | solution.py:37
  61.6 9.8 %collective-permute-start.15 = (f32[48,256]{1,0:T(8,128)S(1)}, f32[48,256]{1,0:T(8,128)S(1)}, u32[]{:S(2)}, u32[]{:S(2)}) collective-permute-start(f32[48,256]{1,0:T(8,128)S(1)} %get-tuple-element.12), channel_id=1, source_target_pairs={{0,8},{1,9},{2,10},{3,11},{4,28},{5,29},{6,30},{7,31},{8,16},{9,17... | collective-permute-start | bytes 147464 | tf_op jit(solution)/shard_map/ppermute | solution.py:37
  64.4 7.1 %collective-permute-start.16 = (f32[48,256]{1,0:T(8,128)S(1)}, f32[48,256]{1,0:T(8,128)S(1)}, u32[]{:S(2)}, u32[]{:S(2)}) collective-permute-start(f32[48,256]{1,0:T(8,128)S(1)} %get-tuple-element.12), channel_id=1, source_target_pairs={{0,24},{1,25},{2,26},{3,27},{4,12},{5,13},{6,14},{7,15},{8,0},{9,1... | collective-permute-start | bytes 147464 | tf_op jit(solution)/shard_map/ppermute | solution.py:37
  64.6 8.3 %collective-permute-start.17 = (f32[48,256]{1,0:T(8,128)S(1)}, f32[48,256]{1,0:T(8,128)S(1)}, u32[]{:S(2)}, u32[]{:S(2)}) collective-permute-start(f32[48,256]{1,0:T(8,128)S(1)} %get-tuple-element.12), channel_id=1, source_target_pairs={{0,16},{1,17},{2,18},{3,19},{4,20},{5,21},{6,22},{7,23},{8,24},{9,... | collective-permute-start | bytes 147464 | tf_op jit(solution)/shard_map/ppermute | solution.py:37
  67.5 6.3 %collective-permute-start.25 = (f32[56,256]{1,0:T(8,128)S(1)}, f32[56,256]{1,0:T(8,128)S(1)}, u32[]{:S(2)}, u32[]{:S(2)}) collective-permute-start(f32[56,256]{1,0:T(8,128)S(1)} %get-tuple-element.10), channel_id=1, source_target_pairs={{0,32},{1,33},{2,34},{3,35},{4,100},{5,101},{6,102},{7,103},{8,40}... | collective-permute-start | bytes 172040 | tf_op jit(solution)/shard_map/ppermute | solution.py:37
  71.4 4.9 %collective-permute-start.26 = (f32[56,256]{1,0:T(8,128)S(1)}, f32[56,256]{1,0:T(8,128)S(1)}, u32[]{:S(2)}, u32[]{:S(2)}) collective-permute-start(f32[56,256]{1,0:T(8,128)S(1)} %get-tuple-element.10), channel_id=1, source_target_pairs={{0,96},{1,97},{2,98},{3,99},{4,36},{5,37},{6,38},{7,39},{8,104},{9... | collective-permute-start | bytes 172040 | tf_op jit(solution)/shard_map/ppermute | solution.py:37
  71.5 5.2 %collective-permute-start.27 = (f32[56,256]{1,0:T(8,128)S(1)}, f32[56,256]{1,0:T(8,128)S(1)}, u32[]{:S(2)}, u32[]{:S(2)}) collective-permute-start(f32[56,256]{1,0:T(8,128)S(1)} %get-tuple-element.10), channel_id=1, source_target_pairs={{0,64},{1,65},{2,66},{3,67},{4,68},{5,69},{6,70},{7,71},{8,72},{9,... | collective-permute-start | bytes 172040 | tf_op jit(solution)/shard_map/ppermute | solution.py:37
  72.9 6.0 %collective-permute-start.8 = (f32[192,256]{1,0:T(8,128)S(1)}, f32[192,256]{1,0:T(8,128)S(1)}, u32[]{:S(2)}, u32[]{:S(2)}) collective-permute-start(f32[192,256]{1,0:T(8,128)S(1)} %constant_dynamic-update-slice_fusion.20), channel_id=1, source_target_pairs={{0,8},{1,9},{2,10},{3,11},{4,28},{5,29},{6,30},{7,31},{8,16},{9,17... | collective-permute-start | bytes 589832 | tf_op jit(solution)/shard_map/ppermute | solution.py:37
  73.8 6.8 %collective-permute-start.9 = (f32[192,256]{1,0:T(8,128)S(1)}, f32[192,256]{1,0:T(8,128)S(1)}, u32[]{:S(2)}, u32[]{:S(2)}) collective-permute-start(f32[192,256]{1,0:T(8,128)S(1)} %constant_dynamic-update-slice_fusion.20), channel_id=1, source_target_pairs={{0,24},{1,25},{2,26},{3,27},{4,12},{5,13},{6,14},{7,15},{8,0},{9,1... | collective-permute-start | bytes 589832 | tf_op jit(solution)/shard_map/ppermute | solution.py:37
  76.3 10.9 %collective-permute-start.10 = (f32[192,256]{1,0:T(8,128)S(1)}, f32[192,256]{1,0:T(8,128)S(1)}, u32[]{:S(2)}, u32[]{:S(2)}) collective-permute-start(f32[192,256]{1,0:T(8,128)S(1)} %constant_dynamic-update-slice_fusion.20), channel_id=1, source_target_pairs={{0,16},{1,17},{2,18},{3,19},{4,20},{5,21},{6,22},{7,23},{8,24},{9,... | collective-permute-start | bytes 589832 | tf_op jit(solution)/shard_map/ppermute | solution.py:37
  76.8 11.9 %collective-permute-start.18 = (f32[192,256]{1,0:T(8,128)S(1)}, f32[192,256]{1,0:T(8,128)S(1)}, u32[]{:S(2)}, u32[]{:S(2)}) collective-permute-start(f32[192,256]{1,0:T(8,128)S(1)} %constant_dynamic-update-slice_fusion.12), channel_id=1, source_target_pairs={{0,32},{1,33},{2,34},{3,35},{4,100},{5,101},{6,102},{7,103},{8,40}... | collective-permute-start | bytes 589832 | tf_op jit(solution)/shard_map/ppermute | solution.py:37
  78.9 11.7 %collective-permute-start.28 = (f32[224,256]{1,0:T(8,128)S(1)}, f32[224,256]{1,0:T(8,128)S(1)}, u32[]{:S(2)}, u32[]{:S(2)}) collective-permute-start(f32[224,256]{1,0:T(8,128)S(1)} %constant_dynamic-update-slice_fusion.4), channel_id=1, source_target_pairs={{0,1},{1,2},{2,3},{3,0},{4,7},{5,4},{6,5},{7,6},{8,9},{9,10},{10,1... | collective-permute-start | bytes 688136 | tf_op jit(solution)/shard_map/ppermute | solution.py:37
  80.5 11.0 %collective-permute-start.29 = (f32[224,256]{1,0:T(8,128)S(1)}, f32[224,256]{1,0:T(8,128)S(1)}, u32[]{:S(2)}, u32[]{:S(2)}) collective-permute-start(f32[224,256]{1,0:T(8,128)S(1)} %constant_dynamic-update-slice_fusion.4), channel_id=1, source_target_pairs={{0,3},{1,0},{2,1},{3,2},{4,5},{5,6},{6,7},{7,4},{8,11},{9,8},{10,9... | collective-permute-start | bytes 688136 | tf_op jit(solution)/shard_map/ppermute | solution.py:37
  87.3 10.6 %collective-permute-start.30 = (f32[224,256]{1,0:T(8,128)S(1)}, f32[224,256]{1,0:T(8,128)S(1)}, u32[]{:S(2)}, u32[]{:S(2)}) collective-permute-start(f32[224,256]{1,0:T(8,128)S(1)} %constant_dynamic-update-slice_fusion.4), channel_id=1, source_target_pairs={{0,2},{1,3},{2,0},{3,1},{4,6},{5,7},{6,4},{7,5},{8,10},{9,11},{10,... | collective-permute-start | bytes 688136 | tf_op jit(solution)/shard_map/ppermute | solution.py:37
  88.7 30.4 %collective-permute-start.11 = (f32[768,256]{1,0:T(8,128)S(1)}, f32[768,256]{1,0:T(8,128)S(1)}, u32[]{:S(2)}, u32[]{:S(2)}) collective-permute-start(f32[768,256]{1,0:T(8,128)S(1)} %constant_dynamic-update-slice_fusion.16.refs_0_), channel_id=1, source_target_pairs={{0,32},{1,33},{2,34},{3,35},{4,100},{5,101},{6,102},{7,103},{8,40}... | collective-permute-start | bytes 2359304 | tf_op jit(solution)/shard_map/ppermute | solution.py:37
  90.6 29.4 %collective-permute-start.12 = (f32[768,256]{1,0:T(8,128)S(1)}, f32[768,256]{1,0:T(8,128)S(1)}, u32[]{:S(2)}, u32[]{:S(2)}) collective-permute-start(f32[768,256]{1,0:T(8,128)S(1)} %constant_dynamic-update-slice_fusion.16.refs_0_), channel_id=1, source_target_pairs={{0,96},{1,97},{2,98},{3,99},{4,36},{5,37},{6,38},{7,39},{8,104},{9... | collective-permute-start | bytes 2359304 | tf_op jit(solution)/shard_map/ppermute | solution.py:37
  91.5 25.9 %collective-permute-start.19 = (f32[192,256]{1,0:T(8,128)S(1)}, f32[192,256]{1,0:T(8,128)S(1)}, u32[]{:S(2)}, u32[]{:S(2)}) collective-permute-start(f32[192,256]{1,0:T(8,128)S(1)} %constant_dynamic-update-slice_fusion.12), channel_id=1, source_target_pairs={{0,96},{1,97},{2,98},{3,99},{4,36},{5,37},{6,38},{7,39},{8,104},{9... | collective-permute-start | bytes 589832 | tf_op jit(solution)/shard_map/ppermute | solution.py:37
  97.9 19.5 %collective-permute-start.20 = (f32[192,256]{1,0:T(8,128)S(1)}, f32[192,256]{1,0:T(8,128)S(1)}, u32[]{:S(2)}, u32[]{:S(2)}) collective-permute-start(f32[192,256]{1,0:T(8,128)S(1)} %constant_dynamic-update-slice_fusion.12), channel_id=1, source_target_pairs={{0,64},{1,65},{2,66},{3,67},{4,68},{5,69},{6,70},{7,71},{8,72},{9,... | collective-permute-start | bytes 589832 | tf_op jit(solution)/shard_map/ppermute | solution.py:37
  117.4 21.9 %collective-permute-start.31 = (f32[896,256]{1,0:T(8,128)S(1)}, f32[896,256]{1,0:T(8,128)S(1)}, u32[]{:S(2)}, u32[]{:S(2)}) collective-permute-start(f32[896,256]{1,0:T(8,128)S(1)} %constant_dynamic-update-slice_fusion.refs_10_), channel_id=1, source_target_pairs={{0,8},{1,9},{2,10},{3,11},{4,28},{5,29},{6,30},{7,31},{8,16},{9,17... | collective-permute-start | bytes 2752520 | tf_op jit(solution)/shard_map/ppermute | solution.py:37
  117.4 21.9 %collective-permute-start.32 = (f32[896,256]{1,0:T(8,128)S(1)}, f32[896,256]{1,0:T(8,128)S(1)}, u32[]{:S(2)}, u32[]{:S(2)}) collective-permute-start(f32[896,256]{1,0:T(8,128)S(1)} %constant_dynamic-update-slice_fusion.refs_10_), channel_id=1, source_target_pairs={{0,24},{1,25},{2,26},{3,27},{4,12},{5,13},{6,14},{7,15},{8,0},{9,1... | collective-permute-start | bytes 2752520 | tf_op jit(solution)/shard_map/ppermute | solution.py:37
  119.1 20.3 %copy-start.3 = (f32[768,256]{1,0:T(8,128)}, f32[768,256]{1,0:T(8,128)S(1)}, u32[]{:S(2)}) copy-start(f32[768,256]{1,0:T(8,128)S(1)} %collective-permute-done.11.refs_1_) | copy-start | bytes 2359300
  119.1 23.4 %collective-permute-start.21 = (f32[768,256]{1,0:T(8,128)S(1)}, f32[768,256]{1,0:T(8,128)S(1)}, u32[]{:S(2)}, u32[]{:S(2)}) collective-permute-start(f32[768,256]{1,0:T(8,128)S(1)} %constant_dynamic-update-slice_fusion.8.refs_5_), channel_id=1, source_target_pairs={{0,1},{1,2},{2,3},{3,0},{4,7},{5,4},{6,5},{7,6},{8,9},{9,10},{10,1... | collective-permute-start | bytes 2359304 | tf_op jit(solution)/shard_map/ppermute | solution.py:37
  120.0 19.3 %copy-start.5 = (f32[768,256]{1,0:T(8,128)}, f32[768,256]{1,0:T(8,128)S(1)}, u32[]{:S(2)}) copy-start(f32[768,256]{1,0:T(8,128)S(1)} %collective-permute-done.12.refs_2_) | copy-start | bytes 2359300
  120.0 22.9 %collective-permute-start.22 = (f32[768,256]{1,0:T(8,128)S(1)}, f32[768,256]{1,0:T(8,128)S(1)}, u32[]{:S(2)}, u32[]{:S(2)}) collective-permute-start(f32[768,256]{1,0:T(8,128)S(1)} %constant_dynamic-update-slice_fusion.8.refs_5_), channel_id=1, source_target_pairs={{0,3},{1,0},{2,1},{3,2},{4,5},{5,6},{6,7},{7,4},{8,11},{9,8},{10,9... | collective-permute-start | bytes 2359304 | tf_op jit(solution)/shard_map/ppermute | solution.py:37
  139.3 9.6 %collective-permute-start.13 = (f32[384,256]{1,0:T(8,128)S(1)}, f32[384,256]{1,0:T(8,128)S(1)}, u32[]{:S(2)}, u32[]{:S(2)}) collective-permute-start(f32[384,256]{1,0:T(8,128)S(1)} %slice.75), channel_id=1, source_target_pairs={{0,32},{1,33},{2,34},{3,35},{4,100},{5,101},{6,102},{7,103},{8,40}... | collective-permute-start | bytes 1179656 | tf_op jit(solution)/shard_map/ppermute | solution.py:37
  139.3 3.6 %copy-start.1 = (f32[896,256]{1,0:T(8,128)}, f32[896,256]{1,0:T(8,128)S(1)}, u32[]{:S(2)}) copy-start(f32[896,256]{1,0:T(8,128)S(1)} %collective-permute-done.32.refs_12_) | copy-start | bytes 2752516
  139.3 12.4 %collective-permute-start.14 = (f32[384,256]{1,0:T(8,128)S(1)}, f32[384,256]{1,0:T(8,128)S(1)}, u32[]{:S(2)}, u32[]{:S(2)}) collective-permute-start(f32[384,256]{1,0:T(8,128)S(1)} %slice.76), channel_id=1, source_target_pairs={{0,96},{1,97},{2,98},{3,99},{4,36},{5,37},{6,38},{7,39},{8,104},{9... | collective-permute-start | bytes 1179656 | tf_op jit(solution)/shard_map/ppermute | solution.py:37
  142.5 21.1 %collective-permute-start.33 = (f32[448,256]{1,0:T(8,128)}, f32[448,256]{1,0:T(8,128)}, u32[]{:S(2)}, u32[]{:S(2)}) collective-permute-start(f32[448,256]{1,0:T(8,128)} %slice.81), channel_id=1, source_target_pairs={{0,8},{1,9},{2,10},{3,11},{4,28},{5,29},{6,30},{7,31},{8,16},{9,17... | collective-permute-start | bytes 1376264 | tf_op jit(solution)/shard_map/ppermute | solution.py:37
  142.9 1.9 %copy-start.9 = (f32[768,256]{1,0:T(8,128)}, f32[768,256]{1,0:T(8,128)S(1)}, u32[]{:S(2)}) copy-start(f32[768,256]{1,0:T(8,128)S(1)} %collective-permute-done.22.refs_7_) | copy-start | bytes 2359300
  142.9 20.7 %collective-permute-start.34 = (f32[448,256]{1,0:T(8,128)}, f32[448,256]{1,0:T(8,128)}, u32[]{:S(2)}, u32[]{:S(2)}) collective-permute-start(f32[448,256]{1,0:T(8,128)} %slice.82), channel_id=1, source_target_pairs={{0,24},{1,25},{2,26},{3,27},{4,12},{5,13},{6,14},{7,15},{8,0},{9,1... | collective-permute-start | bytes 1376264 | tf_op jit(solution)/shard_map/ppermute | solution.py:37
  144.8 0.9 copy-start.7
  149.0 0.7 copy-start.12
  149.7 9.0 %collective-permute-start.23 = (f32[384,256]{1,0:T(8,128)}, f32[384,256]{1,0:T(8,128)}, u32[]{:S(2)}, u32[]{:S(2)}) collective-permute-start(f32[384,256]{1,0:T(8,128)} %slice.78), channel_id=1, source_target_pairs={{0,1},{1,2},{2,3},{3,0},{4,7},{5,4},{6,5},{7,6},{8,9},{9,10},{10,1... | collective-permute-start | bytes 1179656 | tf_op jit(solution)/shard_map/ppermute | solution.py:37
  151.8 0.7 copy-start.14
  152.5 11.1 %collective-permute-start.24 = (f32[384,256]{1,0:T(8,128)}, f32[384,256]{1,0:T(8,128)}, u32[]{:S(2)}, u32[]{:S(2)}) collective-permute-start(f32[384,256]{1,0:T(8,128)} %slice.79), channel_id=1, source_target_pairs={{0,3},{1,0},{2,1},{3,2},{4,5},{5,6},{6,7},{7,4},{8,11},{9,8},{10,9... | collective-permute-start | bytes 1179656 | tf_op jit(solution)/shard_map/ppermute | solution.py:37
  163.6 1.2 copy-start.2
  164.8 1.1 copy-start.4
  165.9 1.1 copy-start.6
  167.0 1.1 copy-start.8
  168.2 1.1 copy-start.10
  169.3 1.0 copy-start.13
  170.3 1.0 copy-start.15
  186.3 1.5 collective-permute-start.35

commit v2 on v0

v2 whole, which is shorter than its diff:
```python
import functools

import jax
import jax.numpy as jnp
from jax import lax
from jax.experimental import pallas as pl
from jax.experimental.pallas import tpu as pltpu
from jax.sharding import PartitionSpec as P

AXES = ("pair", "aux")
SIDE = 4
CORES = 2
CHIP_ROWS = 150
FRAME = 152
STEPS = ("yx", "zy", "xz")
WIDE = 2432


def place(z, y, core, x):
    return (((z % SIDE) * SIDE + y % SIDE) * CORES + core) * SIDE + x % SIDE


def permute(value, step, axes):
    pairs = []
    for z in range(SIDE):
        for y in range(SIDE):
            for core in range(CORES):
                for x in range(SIDE):
                    to = dict(z=z, y=y, core=core, x=x)
                    if step:
                        to[axes[core]] += step
                    else:
                        to["core"] = 1 - core
                    pairs.append((place(z, y, core, x), place(**to)))
    return lax.ppermute(value, AXES, pairs)


def where():
    pair = lax.axis_index("pair")
    return pair % CORES, dict(x=lax.axis_index("aux"), y=(pair // CORES) % SIDE, z=pair // (CORES * SIDE))


def reorder(size, across):
    row = lax.broadcasted_iota(jnp.int32, (size, size), 0)
    column = lax.broadcasted_iota(jnp.int32, (size, size), 1)
    return (row % across) * (size // across) + row // across == column


def partial_kernel(first_ref, second_ref, ac_ref, own_ref, other_ref, shifted, products):
    rows = ac_ref.shape[0]
    count_d = first_ref.shape[0]
    group = pl.program_id(0)

    @pl.when(group == 0)
    def _():
        ordered = jnp.dot(ac_ref[...], reorder(128, 8).astype(jnp.bfloat16), preferred_element_type=jnp.float32)
        shifted[...] = jnp.zeros_like(shifted)
        for k in range(4):
            shifted[k, pl.ds((rows * k) % 128, rows), :] = ordered.astype(jnp.bfloat16)

    for k in range(4):
        offset = (rows * k) % 128
        start = rows * k - offset
        length = -(-(offset + rows) // 128) * 128
        for j, bd_ref in enumerate((first_ref, second_ref)):
            products[8 * group + 4 * j + k] = jnp.dot(bd_ref[:, start:start + length], shifted[k, :length, :],
                                                      preferred_element_type=jnp.float32)

    @pl.when(group == pl.num_programs(0) - 1)
    def _():
        core, at = where()
        own_ref[...] = jnp.zeros_like(own_ref)
        other_ref[...] = jnp.zeros_like(other_ref)
        blocks = [products[b] for b in range(16)]
        slabs = [jnp.concatenate([p[:, 16 * c:16 * c + 16] for p in blocks], axis=1) for c in range(8)]
        for which in range(CORES):
            @pl.when(core == which)
            def _():
                for c in range(8):
                    ref = own_ref if c // SIDE == which else other_ref
                    ref[(c - at["x"]) % SIDE, which * count_d:(which + 1) * count_d, :] = slabs[c]


def partial_integrals(bd, ac):
    rows = ac.shape[0]
    out = jax.ShapeDtypeStruct((SIDE, FRAME, 256), jnp.float32)
    whole = pl.BlockSpec(memory_space=pltpu.VMEM)
    return pl.pallas_call(
        partial_kernel,
        grid=(2,),
        out_shape=(out, out),
        in_specs=[pl.BlockSpec((bd.shape[0], 4 * rows), lambda g: (0, 2 * g)),
                  pl.BlockSpec((bd.shape[0], 4 * rows), lambda g: (0, 2 * g + 1)), whole],
        out_specs=(whole, whole),
        scratch_shapes=[pltpu.VMEM((4, -(-(rows + 96) // 128) * 128, 128), jnp.bfloat16),
                        pltpu.VMEM((16, bd.shape[0], 128), jnp.float32)],
        compiler_params=pltpu.CompilerParams(vmem_limit_bytes=48 * 2**20),
        cost_estimate=pl.CostEstimate(flops=10**9, bytes_accessed=8 * 10**6, transcendentals=0),
    )(bd, bd, ac)


def split(value):
    high = value.astype(jnp.bfloat16)
    return high, (value - high.astype(jnp.float32)).astype(jnp.bfloat16)


def arrange_kernel(*refs):
    sources, (high_ref, low_ref, amp, sems) = refs[:-4], refs[-4:]
    step, steps = pl.program_id(0), pl.num_programs(0)
    slots, rows, _, width = amp.shape
    cut = rows // sems.shape[1]
    core, _ = where()

    def each(block, act):
        slot = lax.rem(block, slots)
        first = 0
        for source in sources:
            count = source.shape[0] // rows

            @pl.when(jnp.logical_and(block >= first, block < first + count))
            def _():
                part = source.at[pl.ds((block - first) * rows, rows), pl.ds(SIDE * core, SIDE)]
                for k in range(sems.shape[1]):
                    act(pltpu.make_async_copy(part.at[pl.ds(k * cut, cut)], amp.at[slot, pl.ds(k * cut, cut)],
                                              sems.at[slot, k]))
            first += count

    @pl.when(step == 0)
    def _():
        for block in range(slots - 1):
            each(step + block, lambda copy: copy.start())

    @pl.when(step + slots - 1 < steps)
    def _():
        each(step + slots - 1, lambda copy: copy.start())

    each(step, lambda copy: copy.wait())
    pad = jnp.zeros((rows, WIDE - width), jnp.float32)
    for c in range(SIDE):
        high_ref[c], low_ref[c] = split(jnp.concatenate([amp[lax.rem(step, slots), :, c, :], pad], axis=1))


def arrange(*amps):
    pairs, width = sum(a.shape[0] for a in amps), amps[0].shape[2]
    rows, slots, cuts = 32, 3, 4
    out = jax.ShapeDtypeStruct((SIDE, pairs, WIDE), jnp.bfloat16)
    return pl.pallas_call(
        arrange_kernel,
        grid=(pairs // rows,),
        out_shape=(out, out),
        in_specs=[pl.BlockSpec(memory_space=pl.ANY)] * len(amps),
        out_specs=(pl.BlockSpec((SIDE, rows, WIDE), lambda i: (0, i, 0)),) * 2,
        scratch_shapes=[pltpu.VMEM((slots, rows, SIDE, width), jnp.float32), pltpu.SemaphoreType.DMA((slots, cuts))],
        compiler_params=pltpu.CompilerParams(vmem_limit_bytes=52 * 2**20),
        cost_estimate=pl.CostEstimate(flops=10**6, bytes_accessed=30 * 10**6, transcendentals=0),
    )(*amps)


def product(high, low, matrix):
    mhigh, mlow = split(matrix)
    dot = functools.partial(jnp.dot, preferred_element_type=jnp.float32)
    return dot(high, mhigh) + (dot(high, mlow) + dot(low, mhigh))


def slot(at, coord):
    ahead = (at - coord + SIDE) % SIDE
    return jnp.where(ahead == 0, 0, jnp.where(ahead == SIDE - 1, 1, ahead + 1))


def run_of(c, z, y):
    core, at = where()
    c, z, y = slot(c, at["x"]), slot(z, at["z"]), slot(y, at["y"])
    return jnp.where(core == 0, 16 * c + SIDE * z + y, 16 * z + SIDE * y + c)


def early_kernel(high_ref, low_ref, *refs):
    pieces, out_ref = refs[:6], refs[6]
    blocks, matrix, sems = refs[7:]
    c = pl.program_id(0)

    @pl.when(c == 0)
    def _():
        copies = [pltpu.make_async_copy(piece, blocks.at[pl.ds(8 * k, 8)], sems.at[k]) for k, piece in enumerate(pieces)]
        for copy in copies:
            copy.start()
        out_ref[...] = jnp.zeros_like(out_ref)
        matrix[WIDE - 32:, :] = jnp.zeros((32, 256), jnp.float32)
        blocks[48:] = jnp.zeros((16,) + blocks.shape[1:], jnp.float32)
        for copy in copies:
            copy.wait()

    for z in range(SIDE):
        for y in range(SIDE):
            begin = CHIP_ROWS * (z * SIDE + y)
            matrix[begin:begin + FRAME, :] = blocks[run_of(c, z, y)]
    out_ref[...] += product(high_ref[...], low_ref[...], matrix[...])


def early_ladder(high, low, pieces):
    pairs = high.shape[1]
    amp_spec = pl.BlockSpec((None, pairs, WIDE), lambda c: (c, 0, 0))
    return pl.pallas_call(
        early_kernel,
        grid=(SIDE,),
        in_specs=[amp_spec] * 2 + [pl.BlockSpec(memory_space=pl.ANY)] * len(pieces),
        out_specs=pl.BlockSpec(memory_space=pltpu.VMEM),
        scratch_shapes=[pltpu.VMEM((64, FRAME, 256), jnp.float32), pltpu.VMEM((WIDE, 256), jnp.float32),
                        pltpu.SemaphoreType.DMA((len(pieces),))],
        out_shape=jax.ShapeDtypeStruct((pairs, 256), jnp.float32),
        compiler_params=pltpu.CompilerParams(vmem_limit_bytes=52 * 2**20),
        cost_estimate=pl.CostEstimate(flops=6 * 10**9, bytes_accessed=25 * 10**6, transcendentals=0),
    )(high, low, *pieces)


def late_kernel(high_ref, low_ref, up_ref, down_ref, total_ref, own_ref, other_ref, high, low, matrix, far, sems):
    pairs = total_ref.shape[0] // 2
    core, at = where()
    sources = ((high_ref, high), (low_ref, low))
    size = matrix.shape[0] // SIDE
    matrix[...] = jnp.zeros_like(matrix)
    far[:8] = up_ref[...]
    far[8:] = down_ref[...]

    @pl.when(core == 0)
    def _():
        c = (at["x"] + 2) % SIDE
        copies = [pltpu.make_async_copy(source.at[c], to.at[:, pl.ds(0, WIDE)], sems.at[k])
                  for k, (source, to) in enumerate(sources)]
        for copy in copies:
            copy.start()
        for to in (high, low):
            to[:, WIDE:] = jnp.zeros((2 * pairs, matrix.shape[0] - WIDE), jnp.bfloat16)
        for z in range(SIDE):
            for y in range(SIDE):
                begin = CHIP_ROWS * (z * SIDE + y)
                matrix[begin:begin + FRAME, :] = far[SIDE * slot(z, at["z"]) + slot(y, at["y"])]
        for copy in copies:
            copy.wait()

    @pl.when(core == 1)
    def _():
        z = (at["z"] + 2) % SIDE
        start = jnp.minimum(SIDE * CHIP_ROWS * z // 128, (WIDE - size) // 128) * 128
        copies = [pltpu.make_async_copy(source.at[c, :, pl.ds(pl.multiple_of(start, 128), size)],
                                        to.at[:, pl.ds(size * c, size)], sems.at[2 * c + k])
                  for c in range(SIDE) for k, (source, to) in enumerate(sources)]
        for copy in copies:
            copy.start()
        for which in range(SIDE):
            @pl.when(z == which)
            def _():
                first = SIDE * CHIP_ROWS * which
                offset = first - min(first // 128, (WIDE - size) // 128) * 128
                for c in range(SIDE):
                    for y in range(SIDE):
                        to = size * c + offset + CHIP_ROWS * y
                        matrix[to:to + FRAME, :] = far[SIDE * slot(y, at["y"]) + slot(c, at["x"])]
        for copy in copies:
            copy.wait()

    result = jnp.dot(total_ref[...] + product(high[...], low[...], matrix[...]),
                     reorder(256, 16).astype(jnp.float32), precision=lax.Precision.HIGHEST,
                     preferred_element_type=jnp.float32)
    own_ref[...] = result[:pairs]
    other_ref[...] = result[pairs:]


def late_ladder(high, low, up, down, total):
    pairs = high.shape[1] // 2
    out = jax.ShapeDtypeStruct((pairs, 256), jnp.float32)
    whole = pl.BlockSpec(memory_space=pltpu.VMEM)
    wide = SIDE * 768
    return pl.pallas_call(
        late_kernel,
        in_specs=[pl.BlockSpec(memory_space=pl.ANY)] * 2 + [whole] * 3,
        out_specs=(whole, whole),
        scratch_shapes=[pltpu.VMEM((2 * pairs, wide), jnp.bfloat16)] * 2 + [
            pltpu.VMEM((wide, 256), jnp.float32), pltpu.VMEM((16,) + up.shape[1:], jnp.float32),
            pltpu.SemaphoreType.DMA((8,))],
        out_shape=(out, out),
        compiler_params=pltpu.CompilerParams(vmem_limit_bytes=40 * 2**20),
        cost_estimate=pl.CostEstimate(flops=2 * 10**9, bytes_accessed=8 * 10**6, transcendentals=0),
    )(high, low, up, down, total)


def fetch(value, axes):
    far = permute(value, 2, axes)
    return [value, permute(value, 1, axes), permute(value, -1, axes), far]


def body(ac_factors, bd_factors, amplitudes):
    barrier = lax.optimization_barrier
    bd = bd_factors.reshape(bd_factors.shape[0], bd_factors.shape[2])
    mine, sent = partial_integrals(bd, ac_factors)
    chip = mine + permute(sent, 0, None)
    amplitudes, chip = barrier((amplitudes, chip))
    other = permute(amplitudes, 0, None)
    shard = chip[0] + permute(chip[2], 2, "xx") + permute(chip[1], 1, "xx") + permute(chip[3], -1, "xx")

    line = jnp.concatenate(fetch(shard, STEPS[0]), axis=0)
    plane = fetch(line, STEPS[1])
    first, second = jnp.concatenate(plane[:2], axis=0), jnp.concatenate(plane[2:], axis=0)
    first, second, amplitudes, other = barrier((first, second, amplitudes, other))
    up_first, down_second = permute(first, 1, STEPS[2]), permute(second, -1, STEPS[2])
    up_second, down_first = permute(second, 1, STEPS[2]), permute(first, -1, STEPS[2])
    high, low = arrange(amplitudes, other)
    up_first, down_second, high, low = barrier((up_first, down_second, high, low))
    far_up, far_down = permute(up_first, 1, STEPS[2]), permute(down_second, -1, STEPS[2])

    def runs(value):
        return value.reshape(-1, FRAME, 256)

    total = early_ladder(high, low, [runs(v) for v in (first, second, up_first, up_second, down_first, down_second)])
    kept, given = late_ladder(high, low, runs(far_up), runs(far_down), total)
    return kept + permute(given, 0, None)


def solution(mesh):
    placed = (P("aux", None), P("pair", "aux", None), P(("pair", "aux"), None, None))
    return jax.shard_map(
        body, mesh=mesh, in_specs=placed, out_specs=P(("pair", "aux"), None), check_vma=False
    )
```

time: 205 us -> 112 us (0.55)
  waiting for transfers between devices: 130 us -> 37.3 us
  Pallas kernels: 0 us -> 37.1 us
  starting transfers between devices: 0.04 us -> 29.8 us
  matrix products: 28.1 us -> 0 us
  local copies, waits for them, and re-layouts: 33.4 us -> 6.53 us
  between operations: 13.4 us -> 0.18 us
    all_gather x1 -> x0, waiting for transfers between devices: 84.9 us -> none  [body(): lax.all_gather(summed, 'pair', axis=2, tiled=True)]
    psum x1 -> x0, waiting for transfers between devices: 44.6 us -> none  [body(): summed = lax.psum(partial_ints, 'aux')]
    ppermute x0 -> x18, waiting for transfers between devices: none -> 37.3 us  [permute(): return lax.ppermute(value, AXES, pairs)]
    pallas_call x0 -> x4, Pallas kernels: none -> 37.1 us  [the longest x1 13.8 us: early_ladder(): pl.pallas_call(early_kernel, grid=(SIDE,), in_specs=[amp_spec] * 2 + [pl....]
    ppermute x0 -> x18, starting transfers between devices: none -> 29.8 us  [permute(): return lax.ppermute(value, AXES, pairs)]
    dot_general x2 -> x0, matrix products: 28.1 us -> none  [the longest x1 22.8 us: contract(): jnp.einsum('pcd,acbd->pab', amps, shaped, precision=lax.Precision.HIGHEST)]
    all_gather x1 -> x0, local copies, waits for them, and re-layouts: 19.8 us -> none  [body(): lax.all_gather(summed, 'pair', axis=2, tiled=True)]
    dot_general x1 -> x0, local copies, waits for them, and re-layouts: 12.8 us -> none  [body(): partial_ints = jnp.dot(flat, ac_factors, preferred_element_type=jnp.float32)]
  transfers between devices with their start and end apart: 2 -> 18, of which waited for: 2 -> 11; matrix products, arithmetic and copies ran while one was open for 0% -> 0% of each run, Pallas kernels for 0% -> 23%
where the time goes in v2:
time: 112 us
  waiting for transfers between devices  37.3 us (33%)
  Pallas kernels  37.1 us (33%)
  starting transfers between devices  29.8 us (27%)
  local copies, waits for them, and re-layouts  6.53 us (6%)
    ppermute x18, waiting for transfers between devices, permute(): return lax.ppermute(value, AXES, pairs)  37.3 us
    ppermute x18, starting transfers between devices, permute(): return lax.ppermute(value, AXES, pairs)  29.8 us
    pallas_call x1, Pallas kernels, early_ladder(): pl.pallas_call(early_kernel, grid=(SIDE,), in_specs=[amp_spec] * 2 + [pl....  13.8 us
    pallas_call x1, Pallas kernels, arrange(): pl.pallas_call(arrange_kernel, grid=(pairs // rows,), out_shape=(out, out...  12.1 us
    unnamed x17, local copies, waits for them, and re-layouts  6.45 us
    pallas_call x1, Pallas kernels, partial_integrals(): pl.pallas_call(partial_kernel, grid=(2,), out_shape=(out, out), in_specs=...  5.94 us
    pallas_call x1, Pallas kernels, late_ladder(): pl.pallas_call(late_kernel, in_specs=[pl.BlockSpec(memory_space=pl.ANY)]...  5.27 us
  transfers between devices with their start and end apart: 18, of which 11 were waited for; matrix products, arithmetic and copies ran while one was open for 0% of the time, Pallas kernels for 23%

profile of v2, /device:TPU:1, one launch (start us, length us, event | category | flops | bytes accessed | tf_op | source)
XLA Modules:
  0.0 111.9 jit_solution(16028354157325921724)
XLA Ops:
  0.0 0.0 copy-start
  0.0 1.1 copy-done
  1.1 5.9 %shard_map.37 = (f32[4,152,256]{2,1,0:T(8,128)S(1)}, f32[4,152,256]{2,1,0:T(8,128)S(1)}) custom-call(bf16[75,38400]{1,0:T(8,128)(2,1)} %bitcast.27, bf16[75,38400]{1,0:T(8,128)(2,1)} %bitcast.28, bf16[2400,128]{1,0:T(8,128)(2,1)S(1)} %copy-done), custom_call_target="tpu_custom_call" | custom-call | flops 1000000000 | bytes 8000000 | tf_op jit(solution)/shard_map/pallas_call | solution.py:88
  7.0 1.5 %collective-permute-start = (f32[4,152,256]{2,1,0:T(8,128)S(1)}, f32[4,152,256]{2,1,0:T(8,128)S(1)}, u32[]{:S(2)}, u32[]{:S(2)}) collective-permute-start(f32[4,152,256]{2,1,0:T(8,128)S(1)} %get-tuple-element.22), channel_id=1, source_target_pairs={{0,4},{1,5},{2,6},{3,7},{4,0},{5,1},{6,2},{7,3},{8,12},{9,13},{10,... | collective-permute-start | bytes 1867784 | tf_op jit(solution)/shard_map/ppermute | solution.py:35
  8.5 1.7 %collective-permute-done = f32[4,152,256]{2,1,0:T(8,128)S(1)} collective-permute-done((f32[4,152,256]{2,1,0:T(8,128)S(1)}, f32[4,152,256]{2,1,0:T(8,128)S(1)}, u32[]{:S(2)}, u32[]{:S(2)}) %collective-permute-start) | collective-permute-done | bytes 622624 | tf_op jit(solution)/shard_map/ppermute | solution.py:35
  10.2 0.1 add.15
  10.3 0.5 collective-permute-start.10
  10.8 2.9 %collective-permute-start.1 = (f32[152,256]{1,0:T(8,128)S(1)}, f32[152,256]{1,0:T(8,128)S(1)}, u32[]{:S(2)}, u32[]{:S(2)}) collective-permute-start(f32[152,256]{1,0:T(8,128)S(1)} %get-tuple-element.39), channel_id=1, source_target_pairs={{0,2},{1,3},{2,0},{3,1},{4,6},{5,7},{6,4},{7,5},{8,10},{9,11},{10,... | collective-permute-start | bytes 466952 | tf_op jit(solution)/shard_map/ppermute | solution.py:35
  13.7 0.9 collective-permute-start.3
  14.5 0.6 collective-permute-start.2
  15.1 2.7 %collective-permute-done.1 = f32[152,256]{1,0:T(8,128)S(1)} collective-permute-done((f32[152,256]{1,0:T(8,128)S(1)}, f32[152,256]{1,0:T(8,128)S(1)}, u32[]{:S(2)}, u32[]{:S(2)}) %collective-permute-start.1) | collective-permute-done | bytes 155680 | tf_op jit(solution)/shard_map/ppermute | solution.py:35
  17.8 3.5 %collective-permute-done.3 = f32[152,256]{1,0:T(8,128)S(1)} collective-permute-done((f32[152,256]{1,0:T(8,128)S(1)}, f32[152,256]{1,0:T(8,128)S(1)}, u32[]{:S(2)}, u32[]{:S(2)}) %collective-permute-start.3) | collective-permute-done | bytes 155680 | tf_op jit(solution)/shard_map/ppermute | solution.py:35
  21.4 0.0 collective-permute-done.2
  21.4 3.1 %collective-permute-start.6 = (f32[152,256]{1,0:T(8,128)S(1)}, f32[152,256]{1,0:T(8,128)S(1)}, u32[]{:S(2)}, u32[]{:S(2)}) collective-permute-start(f32[152,256]{1,0:T(8,128)S(1)} %get-tuple-element.38), channel_id=1, source_target_pairs={{0,16},{1,17},{2,18},{3,19},{4,6},{5,7},{6,4},{7,5},{8,24},{9,25},... | collective-permute-start | bytes 466952 | tf_op jit(solution)/shard_map/ppermute | solution.py:35
  24.6 0.9 collective-permute-start.5
  25.5 0.6 collective-permute-start.4
  26.1 1.4 %collective-permute-done.6 = f32[152,256]{1,0:T(8,128)S(1)} collective-permute-done((f32[152,256]{1,0:T(8,128)S(1)}, f32[152,256]{1,0:T(8,128)S(1)}, u32[]{:S(2)}, u32[]{:S(2)}) %collective-permute-start.6) | collective-permute-done | bytes 155680 | tf_op jit(solution)/shard_map/ppermute | solution.py:35
  27.5 2.0 %collective-permute-done.5 = f32[152,256]{1,0:T(8,128)S(1)} collective-permute-done((f32[152,256]{1,0:T(8,128)S(1)}, f32[152,256]{1,0:T(8,128)S(1)}, u32[]{:S(2)}, u32[]{:S(2)}) %collective-permute-start.5) | collective-permute-done | bytes 155680 | tf_op jit(solution)/shard_map/ppermute | solution.py:35
  29.5 1.3 %collective-permute-done.4 = f32[152,256]{1,0:T(8,128)S(1)} collective-permute-done((f32[152,256]{1,0:T(8,128)S(1)}, f32[152,256]{1,0:T(8,128)S(1)}, u32[]{:S(2)}, u32[]{:S(2)}) %collective-permute-start.4) | collective-permute-done | bytes 155680 | tf_op jit(solution)/shard_map/ppermute | solution.py:35
  30.8 1.4 %collective-permute-start.7 = (f32[608,256]{1,0:T(8,128)S(1)}, f32[608,256]{1,0:T(8,128)S(1)}, u32[]{:S(2)}, u32[]{:S(2)}) collective-permute-start(f32[608,256]{1,0:T(8,128)S(1)} %pad_maximum_fusion.1), channel_id=1, source_target_pairs={{0,32},{1,33},{2,34},{3,35},{4,12},{5,13},{6,14},{7,15},{8,40},{9,... | collective-permute-start | bytes 1867784 | tf_op jit(solution)/shard_map/ppermute | solution.py:35
  32.2 2.6 %collective-permute-start.9 = (f32[608,256]{1,0:T(8,128)S(1)}, f32[608,256]{1,0:T(8,128)S(1)}, u32[]{:S(2)}, u32[]{:S(2)}) collective-permute-start(f32[608,256]{1,0:T(8,128)S(1)} %pad_maximum_fusion.1), channel_id=1, source_target_pairs={{0,64},{1,65},{2,66},{3,67},{4,20},{5,21},{6,22},{7,23},{8,72},{9,... | collective-permute-start | bytes 1867784 | tf_op jit(solution)/shard_map/ppermute | solution.py:35
  34.8 1.1 collective-permute-start.8
  35.9 5.6 %collective-permute-done.7 = f32[608,256]{1,0:T(8,128)S(1)} collective-permute-done((f32[608,256]{1,0:T(8,128)S(1)}, f32[608,256]{1,0:T(8,128)S(1)}, u32[]{:S(2)}, u32[]{:S(2)}) %collective-permute-start.7) | collective-permute-done | bytes 622624 | tf_op jit(solution)/shard_map/ppermute | solution.py:35
  41.6 7.8 %collective-permute-done.9 = f32[608,256]{1,0:T(8,128)S(1)} collective-permute-done((f32[608,256]{1,0:T(8,128)S(1)}, f32[608,256]{1,0:T(8,128)S(1)}, u32[]{:S(2)}, u32[]{:S(2)}) %collective-permute-start.9) | collective-permute-done | bytes 622624 | tf_op jit(solution)/shard_map/ppermute | solution.py:35
  49.4 0.0 collective-permute-done.8
  49.4 0.1 pad_maximum_fusion
  49.5 0.0 copy-start.2
  49.5 0.0 collective-permute-done.10.refs_1_
  49.5 0.0 copy-start.1
  49.5 1.4 %collective-permute-start.11 = (f32[1216,256]{1,0:T(8,128)S(1)}, f32[1216,256]{1,0:T(8,128)}, u32[]{:S(2)}, u32[]{:S(2)}) collective-permute-start(f32[1216,256]{1,0:T(8,128)S(1)} %constant_dynamic-update-slice_fusion), channel_id=1, source_target_pairs={{0,1},{1,2},{2,3},{3,0},{4,36},{5,37},{6,38},{7,39},{8,9},{9,10},{... | collective-permute-start | bytes 3735560 | tf_op jit(solution)/shard_map/ppermute | solution.py:35
  50.9 3.9 %copy-done.1 = f32[192,8,2400]{2,1,0:T(8,128)} copy-done((f32[192,8,2400]{2,1,0:T(8,128)}, f32[192,8,2400]{2,1,0:T(8,128)S(1)}, u32[]{:S(2)}) %copy-start.1) | copy-done | bytes 14745624
  54.8 3.5 %collective-permute-start.12 = (f32[1216,256]{1,0:T(8,128)S(1)}, f32[1216,256]{1,0:T(8,128)}, u32[]{:S(2)}, u32[]{:S(2)}) collective-permute-start(f32[1216,256]{1,0:T(8,128)S(1)} %pad_maximum_fusion), channel_id=1, source_target_pairs={{0,3},{1,0},{2,1},{3,2},{4,100},{5,101},{6,102},{7,103},{8,11},{9,... | collective-permute-start | bytes 3735560 | tf_op jit(solution)/shard_map/ppermute | solution.py:35
  58.3 0.1 collective-permute-start.16
  58.4 1.3 %collective-permute-start.15 = (f32[1216,256]{1,0:T(8,128)S(1)}, f32[1216,256]{1,0:T(8,128)S(1)}, u32[]{:S(2)}, u32[]{:S(2)}) collective-permute-start(f32[1216,256]{1,0:T(8,128)S(1)} %pad_maximum_fusion), channel_id=1, source_target_pairs={{0,1},{1,2},{2,3},{3,0},{4,36},{5,37},{6,38},{7,39},{8,9},{9,10},{... | collective-permute-start | bytes 3735560 | tf_op jit(solution)/shard_map/ppermute | solution.py:35
  59.7 12.1 %shard_map.38 = (bf16[4,384,2432]{2,1,0:T(8,128)(2,1)}, bf16[4,384,2432]{2,1,0:T(8,128)(2,1)}) custom-call(f32[192,8,2400]{2,1,0:T(8,128)} %refs_0_, f32[192,8,2400]{2,1,0:T(8,128)} %copy-done.1), custom_call_target="tpu_custom_call" | custom-call | flops 1000000 | bytes 30000000 | tf_op jit(solution)/shard_map/pallas_call | solution.py:147
  71.8 0.0 copy-done.2
  71.9 0.0 collective-permute-done.11
  71.9 0.2 collective-permute-done.12
  72.1 0.4 collective-permute-start.13
  72.5 3.1 %collective-permute-start.14 = (f32[1216,256]{1,0:T(8,128)}, f32[1216,256]{1,0:T(8,128)S(1)}, u32[]{:S(2)}, u32[]{:S(2)}) collective-permute-start(f32[1216,256]{1,0:T(8,128)} %collective-permute-done.12), channel_id=1, source_target_pairs={{0,3},{1,0},{2,1},{3,2},{4,100},{5,101},{6,102},{7,103},{8,11},{9,... | collective-permute-start | bytes 3735560 | tf_op jit(solution)/shard_map/ppermute | solution.py:35
  75.5 9.9 %collective-permute-done.16 = f32[1216,256]{1,0:T(8,128)S(1)} collective-permute-done((f32[1216,256]{1,0:T(8,128)S(1)}, f32[1216,256]{1,0:T(8,128)S(1)}, u32[]{:S(2)}, u32[]{:S(2)}) %collective-permute-start.16) | collective-permute-done | bytes 1245216 | tf_op jit(solution)/shard_map/ppermute | solution.py:35
  85.5 0.0 copy-start.3
  85.5 0.0 collective-permute-done.15
  85.5 0.0 copy-start.4
  85.5 1.0 copy-done.3
  86.5 0.4 copy-done.4
  86.9 0.0 slice-start
  86.9 0.0 slice-start.1
  86.9 13.8 %shard_map.39.total_ref = f32[384,256]{1,0:T(8,128)S(1)} custom-call(bf16[4,384,2432]{2,1,0:T(8,128)(2,1)} %get-tuple-element.31.high_ref, bf16[4,384,2432]{2,1,0:T(8,128)(2,1)} %get-tuple-element.32.low_ref, f32[8,152,256]{2,1,0:T(8,128)S(1)} %bitcast.24, f32[8,152,256]{2,1,0:T(8,128)} %bitcast.29, f32[8,152,256]{2,1,0:T(8,128)} %bitcast.9.refs_2_, ...), custom_call_target="tpu_custom_call" | custom-call | flops 6000000000 | bytes 25000000 | tf_op jit(solution)/shard_map/pallas_call | solution.py:202
  100.7 0.0 collective-permute-done.13
  100.7 0.0 collective-permute-done.14
  100.7 0.0 slice-done
  100.7 0.0 slice-done.1
  100.7 5.3 %shard_map.40 = (f32[192,256]{1,0:T(8,128)S(1)}, f32[192,256]{1,0:T(8,128)S(1)}) custom-call(bf16[4,384,2432]{2,1,0:T(8,128)(2,1)S(1)} %bitcast.23, bf16[4,384,2432]{2,1,0:T(8,128)(2,1)} %get-tuple-element.32.low_ref, f32[8,152,256]{2,1,0:T(8,128)S(1)} %bitcast.25, f32[8,152,256]{2,1,0:T(8,128)S(1)} %bitcast.26, f32[384,256]{1,0:T(8,128)S(1)} %shard_map.39.total_ref), custom_call_target="tpu_custom_call" | custom-call | flops 2000000000 | bytes 8000000 | tf_op jit(solution)/shard_map/pallas_call | solution.py:273
  106.0 4.1 %collective-permute-start.17 = (f32[192,256]{1,0:T(8,128)S(1)}, f32[192,256]{1,0:T(8,128)S(1)}, u32[]{:S(2)}, u32[]{:S(2)}) collective-permute-start(f32[192,256]{1,0:T(8,128)S(1)} %get-tuple-element.36), channel_id=1, source_target_pairs={{0,4},{1,5},{2,6},{3,7},{4,0},{5,1},{6,2},{7,3},{8,12},{9,13},{10,... | collective-permute-start | bytes 589832 | tf_op jit(solution)/shard_map/ppermute | solution.py:35
  110.1 1.1 collective-permute-done.17
  111.2 0.7 add.19
  (8 shorter events, 0.2 us)
Async XLA Ops:
  0.0 1.1 copy-start
  7.0 3.2 %collective-permute-start = (f32[4,152,256]{2,1,0:T(8,128)S(1)}, f32[4,152,256]{2,1,0:T(8,128)S(1)}, u32[]{:S(2)}, u32[]{:S(2)}) collective-permute-start(f32[4,152,256]{2,1,0:T(8,128)S(1)} %get-tuple-element.22), channel_id=1, source_target_pairs={{0,4},{1,5},{2,6},{3,7},{4,0},{5,1},{6,2},{7,3},{8,12},{9,13},{10,... | collective-permute-start | bytes 1867784 | tf_op jit(solution)/shard_map/ppermute | solution.py:35
  10.3 39.2 %collective-permute-start.10 = (f32[192,8,2400]{2,1,0:T(8,128)}, f32[192,8,2400]{2,1,0:T(8,128)S(1)}, u32[]{:S(2)}, u32[]{:S(2)}) collective-permute-start(f32[192,8,2400]{2,1,0:T(8,128)} %refs_0_), channel_id=1, source_target_pairs={{0,4},{1,5},{2,6},{3,7},{4,0},{5,1},{6,2},{7,3},{8,12},{9,13},{10,... | collective-permute-start | bytes 44236808 | tf_op jit(solution)/shard_map/ppermute | solution.py:35
  10.8 7.1 %collective-permute-start.1 = (f32[152,256]{1,0:T(8,128)S(1)}, f32[152,256]{1,0:T(8,128)S(1)}, u32[]{:S(2)}, u32[]{:S(2)}) collective-permute-start(f32[152,256]{1,0:T(8,128)S(1)} %get-tuple-element.39), channel_id=1, source_target_pairs={{0,2},{1,3},{2,0},{3,1},{4,6},{5,7},{6,4},{7,5},{8,10},{9,11},{10,... | collective-permute-start | bytes 466952 | tf_op jit(solution)/shard_map/ppermute | solution.py:35
  13.7 7.7 %collective-permute-start.3 = (f32[152,256]{1,0:T(8,128)S(1)}, f32[152,256]{1,0:T(8,128)S(1)}, u32[]{:S(2)}, u32[]{:S(2)}) collective-permute-start(f32[152,256]{1,0:T(8,128)S(1)} %get-tuple-element.40), channel_id=1, source_target_pairs={{0,3},{1,0},{2,1},{3,2},{4,7},{5,4},{6,5},{7,6},{8,11},{9,8},{10,9... | collective-permute-start | bytes 466952 | tf_op jit(solution)/shard_map/ppermute | solution.py:35
  14.5 6.9 %collective-permute-start.2 = (f32[152,256]{1,0:T(8,128)S(1)}, f32[152,256]{1,0:T(8,128)S(1)}, u32[]{:S(2)}, u32[]{:S(2)}) collective-permute-start(f32[152,256]{1,0:T(8,128)S(1)} %get-tuple-element.41), channel_id=1, source_target_pairs={{0,1},{1,2},{2,3},{3,0},{4,5},{5,6},{6,7},{7,4},{8,9},{9,10},{10,1... | collective-permute-start | bytes 466952 | tf_op jit(solution)/shard_map/ppermute | solution.py:35
  21.4 6.1 %collective-permute-start.6 = (f32[152,256]{1,0:T(8,128)S(1)}, f32[152,256]{1,0:T(8,128)S(1)}, u32[]{:S(2)}, u32[]{:S(2)}) collective-permute-start(f32[152,256]{1,0:T(8,128)S(1)} %get-tuple-element.38), channel_id=1, source_target_pairs={{0,16},{1,17},{2,18},{3,19},{4,6},{5,7},{6,4},{7,5},{8,24},{9,25},... | collective-permute-start | bytes 466952 | tf_op jit(solution)/shard_map/ppermute | solution.py:35
  24.6 4.9 %collective-permute-start.5 = (f32[152,256]{1,0:T(8,128)S(1)}, f32[152,256]{1,0:T(8,128)S(1)}, u32[]{:S(2)}, u32[]{:S(2)}) collective-permute-start(f32[152,256]{1,0:T(8,128)S(1)} %get-tuple-element.38), channel_id=1, source_target_pairs={{0,24},{1,25},{2,26},{3,27},{4,7},{5,4},{6,5},{7,6},{8,0},{9,1},{1... | collective-permute-start | bytes 466952 | tf_op jit(solution)/shard_map/ppermute | solution.py:35
  25.5 5.3 %collective-permute-start.4 = (f32[152,256]{1,0:T(8,128)S(1)}, f32[152,256]{1,0:T(8,128)S(1)}, u32[]{:S(2)}, u32[]{:S(2)}) collective-permute-start(f32[152,256]{1,0:T(8,128)S(1)} %get-tuple-element.38), channel_id=1, source_target_pairs={{0,8},{1,9},{2,10},{3,11},{4,5},{5,6},{6,7},{7,4},{8,16},{9,17},{1... | collective-permute-start | bytes 466952 | tf_op jit(solution)/shard_map/ppermute | solution.py:35
  30.8 10.7 %collective-permute-start.7 = (f32[608,256]{1,0:T(8,128)S(1)}, f32[608,256]{1,0:T(8,128)S(1)}, u32[]{:S(2)}, u32[]{:S(2)}) collective-permute-start(f32[608,256]{1,0:T(8,128)S(1)} %pad_maximum_fusion.1), channel_id=1, source_target_pairs={{0,32},{1,33},{2,34},{3,35},{4,12},{5,13},{6,14},{7,15},{8,40},{9,... | collective-permute-start | bytes 1867784 | tf_op jit(solution)/shard_map/ppermute | solution.py:35
  32.2 17.2 %collective-permute-start.9 = (f32[608,256]{1,0:T(8,128)S(1)}, f32[608,256]{1,0:T(8,128)S(1)}, u32[]{:S(2)}, u32[]{:S(2)}) collective-permute-start(f32[608,256]{1,0:T(8,128)S(1)} %pad_maximum_fusion.1), channel_id=1, source_target_pairs={{0,64},{1,65},{2,66},{3,67},{4,20},{5,21},{6,22},{7,23},{8,72},{9,... | collective-permute-start | bytes 1867784 | tf_op jit(solution)/shard_map/ppermute | solution.py:35
  34.8 14.6 %collective-permute-start.8 = (f32[608,256]{1,0:T(8,128)S(1)}, f32[608,256]{1,0:T(8,128)S(1)}, u32[]{:S(2)}, u32[]{:S(2)}) collective-permute-start(f32[608,256]{1,0:T(8,128)S(1)} %pad_maximum_fusion.1), channel_id=1, source_target_pairs={{0,96},{1,97},{2,98},{3,99},{4,28},{5,29},{6,30},{7,31},{8,104},{9... | collective-permute-start | bytes 1867784 | tf_op jit(solution)/shard_map/ppermute | solution.py:35
  49.5 22.4 %copy-start.2 = (f32[1216,256]{1,0:T(8,128)}, f32[1216,256]{1,0:T(8,128)S(1)}, u32[]{:S(2)}) copy-start(f32[1216,256]{1,0:T(8,128)S(1)} %pad_maximum_fusion) | copy-start | bytes 3735556
  49.5 5.3 %copy-start.1 = (f32[192,8,2400]{2,1,0:T(8,128)}, f32[192,8,2400]{2,1,0:T(8,128)S(1)}, u32[]{:S(2)}) copy-start(f32[192,8,2400]{2,1,0:T(8,128)S(1)} %collective-permute-done.10.refs_1_) | copy-start | bytes 44236804
  49.5 22.4 %collective-permute-start.11 = (f32[1216,256]{1,0:T(8,128)S(1)}, f32[1216,256]{1,0:T(8,128)}, u32[]{:S(2)}, u32[]{:S(2)}) collective-permute-start(f32[1216,256]{1,0:T(8,128)S(1)} %constant_dynamic-update-slice_fusion), channel_id=1, source_target_pairs={{0,1},{1,2},{2,3},{3,0},{4,36},{5,37},{6,38},{7,39},{8,9},{9,10},{... | collective-permute-start | bytes 3735560 | tf_op jit(solution)/shard_map/ppermute | solution.py:35
  54.8 17.3 %collective-permute-start.12 = (f32[1216,256]{1,0:T(8,128)S(1)}, f32[1216,256]{1,0:T(8,128)}, u32[]{:S(2)}, u32[]{:S(2)}) collective-permute-start(f32[1216,256]{1,0:T(8,128)S(1)} %pad_maximum_fusion), channel_id=1, source_target_pairs={{0,3},{1,0},{2,1},{3,2},{4,100},{5,101},{6,102},{7,103},{8,11},{9,... | collective-permute-start | bytes 3735560 | tf_op jit(solution)/shard_map/ppermute | solution.py:35
  58.3 27.2 %collective-permute-start.16 = (f32[1216,256]{1,0:T(8,128)S(1)}, f32[1216,256]{1,0:T(8,128)S(1)}, u32[]{:S(2)}, u32[]{:S(2)}) collective-permute-start(f32[1216,256]{1,0:T(8,128)S(1)} %constant_dynamic-update-slice_fusion), channel_id=1, source_target_pairs={{0,3},{1,0},{2,1},{3,2},{4,100},{5,101},{6,102},{7,103},{8,11},{9,... | collective-permute-start | bytes 3735560 | tf_op jit(solution)/shard_map/ppermute | solution.py:35
  58.4 27.1 %collective-permute-start.15 = (f32[1216,256]{1,0:T(8,128)S(1)}, f32[1216,256]{1,0:T(8,128)S(1)}, u32[]{:S(2)}, u32[]{:S(2)}) collective-permute-start(f32[1216,256]{1,0:T(8,128)S(1)} %pad_maximum_fusion), channel_id=1, source_target_pairs={{0,1},{1,2},{2,3},{3,0},{4,36},{5,37},{6,38},{7,39},{8,9},{9,10},{... | collective-permute-start | bytes 3735560 | tf_op jit(solution)/shard_map/ppermute | solution.py:35
  72.1 28.6 %collective-permute-start.13 = (f32[1216,256]{1,0:T(8,128)}, f32[1216,256]{1,0:T(8,128)S(1)}, u32[]{:S(2)}, u32[]{:S(2)}) collective-permute-start(f32[1216,256]{1,0:T(8,128)} %collective-permute-done.11), channel_id=1, source_target_pairs={{0,1},{1,2},{2,3},{3,0},{4,36},{5,37},{6,38},{7,39},{8,9},{9,10},{... | collective-permute-start | bytes 3735560 | tf_op jit(solution)/shard_map/ppermute | solution.py:35
  72.5 28.2 %collective-permute-start.14 = (f32[1216,256]{1,0:T(8,128)}, f32[1216,256]{1,0:T(8,128)S(1)}, u32[]{:S(2)}, u32[]{:S(2)}) collective-permute-start(f32[1216,256]{1,0:T(8,128)} %collective-permute-done.12), channel_id=1, source_target_pairs={{0,3},{1,0},{2,1},{3,2},{4,100},{5,101},{6,102},{7,103},{8,11},{9,... | collective-permute-start | bytes 3735560 | tf_op jit(solution)/shard_map/ppermute | solution.py:35
  85.5 1.0 copy-start.3
  85.5 1.4 %copy-start.4 = (f32[1216,256]{1,0:T(8,128)}, f32[1216,256]{1,0:T(8,128)S(1)}, u32[]{:S(2)}) copy-start(f32[1216,256]{1,0:T(8,128)S(1)} %collective-permute-done.15) | copy-start | bytes 3735556
  86.9 13.8 %slice-start = ((s8[7471104]{0:T(1024)(128)(4,1)}), s8[4194304]{0:T(1024)(128)(4,1)S(1)}, s32[]{:S(2)}) async-start(s8[7471104]{0:T(1024)(128)(4,1)} %bitcast.22), calls=%async_computation | async-start | bytes 8388608
  86.9 13.8 %slice-start.1 = ((s8[7471104]{0:T(1024)(128)(4,1)}), s8[3276800]{0:T(1024)(128)(4,1)S(1)}, s32[]{:S(2)}) async-start(s8[7471104]{0:T(1024)(128)(4,1)} %bitcast.22), calls=%async_computation.1 | async-start | bytes 6553600
  106.0 5.2 %collective-permute-start.17 = (f32[192,256]{1,0:T(8,128)S(1)}, f32[192,256]{1,0:T(8,128)S(1)}, u32[]{:S(2)}, u32[]{:S(2)}) collective-permute-start(f32[192,256]{1,0:T(8,128)S(1)} %get-tuple-element.36), channel_id=1, source_target_pairs={{0,4},{1,5},{2,6},{3,7},{4,0},{5,1},{6,2},{7,3},{8,12},{9,13},{10,... | collective-permute-start | bytes 589832 | tf_op jit(solution)/shard_map/ppermute | solution.py:35

commit v3 on v2

v3 whole, which is shorter than its diff:
```python
import functools

import jax
import jax.numpy as jnp
from jax import lax
from jax.experimental import pallas as pl
from jax.experimental.pallas import tpu as pltpu
from jax.sharding import PartitionSpec as P

AXES = ("pair", "aux")
SIDE = 4
CORES = 2
CHIP_ROWS = 150
FRAME = 152
STEPS = ("yx", "zy", "xz")
WINDOW = 768
WIDE = 2432


def place(z, y, core, x):
    return (((z % SIDE) * SIDE + y % SIDE) * CORES + core) * SIDE + x % SIDE


def permute(value, step, axes):
    pairs = []
    for z in range(SIDE):
        for y in range(SIDE):
            for core in range(CORES):
                for x in range(SIDE):
                    to = dict(z=z, y=y, core=core, x=x)
                    if step:
                        to[axes[core]] += step
                    else:
                        to["core"] = 1 - core
                    pairs.append((place(z, y, core, x), place(**to)))
    return lax.ppermute(value, AXES, pairs)


def where():
    pair = lax.axis_index("pair")
    return pair % CORES, dict(x=lax.axis_index("aux"), y=(pair // CORES) % SIDE, z=pair // (CORES * SIDE))


def reorder(size, across):
    row = lax.broadcasted_iota(jnp.int32, (size, size), 0)
    column = lax.broadcasted_iota(jnp.int32, (size, size), 1)
    return (row % across) * (size // across) + row // across == column


def partial_kernel(first_ref, second_ref, ac_ref, own_ref, other_ref, shifted, products):
    rows = ac_ref.shape[0]
    count_d = products.shape[1]
    group = pl.program_id(0)

    @pl.when(group == 0)
    def _():
        ordered = jnp.dot(ac_ref[...], reorder(128, 8).astype(jnp.bfloat16), preferred_element_type=jnp.float32)
        shifted[...] = jnp.zeros_like(shifted)
        for k in range(4):
            shifted[k, pl.ds((rows * k) % 128, rows), :] = ordered.astype(jnp.bfloat16)

    height = first_ref.shape[0]
    for k in range(4):
        offset = (rows * k) % 128
        start = rows * k - offset
        length = -(-(offset + rows) // 128) * 128
        both = jnp.concatenate([ref[:, start:start + length] for ref in (first_ref, second_ref)], axis=0)
        both = jnp.dot(both, shifted[k, :length, :], preferred_element_type=jnp.float32)
        products[8 * group + k] = both[:count_d]
        products[8 * group + 4 + k] = both[height:height + count_d]

    @pl.when(group == pl.num_programs(0) - 1)
    def _():
        core, at = where()
        own_ref[...] = jnp.zeros_like(own_ref)
        other_ref[...] = jnp.zeros_like(other_ref)
        column = lax.broadcasted_iota(jnp.int32, (count_d, 128), 1) // 16
        turned = [pltpu.roll(products[b], 16 * (b % 8), axis=1) if b % 8 else products[b] for b in range(16)]
        slabs = []
        for c in range(8):
            sides = []
            for side in (turned[:8], turned[8:]):
                picked = side[0]
                for b in range(1, 8):
                    picked = jnp.where(column == (c + b) % 8, side[b], picked)
                sides.append(pltpu.roll(picked, 128 - 16 * c, axis=1) if c else picked)
            slabs.append(jnp.concatenate(sides, axis=1))
        for which in range(CORES):
            @pl.when(core == which)
            def _():
                for c in range(8):
                    ref = own_ref if c // SIDE == which else other_ref
                    ref[(c - at["x"]) % SIDE, which * count_d:(which + 1) * count_d, :] = slabs[c]


def partial_integrals(bd, ac):
    rows = ac.shape[0]
    height = -(-bd.shape[0] // 16) * 16
    out = jax.ShapeDtypeStruct((SIDE, FRAME, 256), jnp.float32)
    whole = pl.BlockSpec(memory_space=pltpu.VMEM)
    return pl.pallas_call(
        partial_kernel,
        grid=(2,),
        out_shape=(out, out),
        in_specs=[pl.BlockSpec((height, 4 * rows), lambda g: (0, 2 * g)),
                  pl.BlockSpec((height, 4 * rows), lambda g: (0, 2 * g + 1)), whole],
        out_specs=(whole, whole),
        scratch_shapes=[pltpu.VMEM((4, -(-(rows + 96) // 128) * 128, 128), jnp.bfloat16),
                        pltpu.VMEM((16, bd.shape[0], 128), jnp.float32)],
        compiler_params=pltpu.CompilerParams(vmem_limit_bytes=48 * 2**20),
        cost_estimate=pl.CostEstimate(flops=10**9, bytes_accessed=8 * 10**6, transcendentals=0),
    )(bd, bd, ac)


def split(value):
    high = value.astype(jnp.bfloat16)
    return high, (value - high.astype(jnp.float32)).astype(jnp.bfloat16)


def arrange_kernel(amp_ref, high_ref, low_ref, amp, sems):
    step, steps = pl.program_id(0), pl.num_programs(0)
    slots, rows, _, width = amp.shape
    cut = rows // sems.shape[1]
    core, _ = where()

    def fetch(block):
        source = amp_ref.at[pl.ds(block * rows, rows), pl.ds(SIDE * core, SIDE)]
        slot = lax.rem(block, slots)
        return [pltpu.make_async_copy(source.at[pl.ds(k * cut, cut)], amp.at[slot, pl.ds(k * cut, cut)], sems.at[slot, k])
                for k in range(sems.shape[1])]

    @pl.when(step == 0)
    def _():
        for block in range(slots - 1):
            for copy in fetch(step + block):
                copy.start()

    @pl.when(step + slots - 1 < steps)
    def _():
        for copy in fetch(step + slots - 1):
            copy.start()

    for copy in fetch(step):
        copy.wait()
    pad = jnp.zeros((rows, WIDE - width), jnp.float32)
    for c in range(SIDE):
        high_ref[c], low_ref[c] = split(jnp.concatenate([amp[lax.rem(step, slots), :, c, :], pad], axis=1))


def arrange(amps, room):
    pairs, _, width = amps.shape
    rows, slots, cuts = 32, 3, 4
    out = jax.ShapeDtypeStruct((SIDE, pairs, WIDE), jnp.bfloat16)
    return pl.pallas_call(
        arrange_kernel,
        grid=(pairs // rows,),
        out_shape=(out, out),
        in_specs=[pl.BlockSpec(memory_space=pl.ANY)],
        out_specs=(pl.BlockSpec((SIDE, rows, WIDE), lambda i: (0, i, 0)),) * 2,
        scratch_shapes=[pltpu.VMEM((slots, rows, SIDE, width), jnp.float32), pltpu.SemaphoreType.DMA((slots, cuts))],
        compiler_params=pltpu.CompilerParams(vmem_limit_bytes=room * 2**20),
        cost_estimate=pl.CostEstimate(flops=10**6, bytes_accessed=15 * 10**6, transcendentals=0),
    )(amps)


def product(high, low, matrix):
    mhigh, mlow = split(matrix)
    dot = functools.partial(jnp.dot, preferred_element_type=jnp.float32)
    return dot(high, mhigh) + (dot(high, mlow) + dot(low, mhigh))


def slot(at, coord):
    ahead = (at - coord + SIDE) % SIDE
    return jnp.where(ahead == 0, 0, jnp.where(ahead == SIDE - 1, 1, ahead + 1))


def run_of(c, z, y):
    core, at = where()
    c, z, y = slot(c, at["x"]), slot(z, at["z"]), slot(y, at["y"])
    return jnp.where(core == 0, 16 * c + SIDE * z + y, 16 * z + SIDE * y + c)


def early_kernel(own_high, own_low, other_high, other_low, *refs):
    pieces, (out_ref, far_high, far_low, blocks, matrix, sems) = refs[:-6], refs[-6:]
    c = pl.program_id(0)

    @pl.when(c == 0)
    def _():
        copies, filled = [], 0
        for k, piece in enumerate(pieces):
            copies.append(pltpu.make_async_copy(piece, blocks.at[pl.ds(filled, piece.shape[0])], sems.at[k]))
            filled += piece.shape[0]
        for copy in copies:
            copy.start()
        out_ref[...] = jnp.zeros_like(out_ref)
        matrix[WIDE - 32:, :] = jnp.zeros((32, 256), jnp.float32)
        blocks[48:] = jnp.zeros((16,) + blocks.shape[1:], jnp.float32)
        for copy in copies:
            copy.wait()

    for z in range(SIDE):
        for y in range(SIDE):
            begin = CHIP_ROWS * (z * SIDE + y)
            matrix[begin:begin + FRAME, :] = blocks[run_of(c, z, y)]
    high = jnp.concatenate([own_high[...], other_high[...]], axis=0)
    low = jnp.concatenate([own_low[...], other_low[...]], axis=0)
    out_ref[...] += product(high, low, matrix[...])

    core, at = where()
    size = far_high.shape[1] // SIDE

    @pl.when(jnp.logical_and(core == 0, (at["x"] + 2) % SIDE == c))
    def _():
        for to, (one, two) in ((far_high, (own_high, other_high)), (far_low, (own_low, other_low))):
            to[:, :WIDE] = jnp.concatenate([one[...], two[...]], axis=0)
            to[:, WIDE:] = jnp.zeros((to.shape[0], SIDE * size - WIDE), jnp.bfloat16)

    @pl.when(core == 1)
    def _():
        start = jnp.minimum(SIDE * CHIP_ROWS * ((at["z"] + 2) % SIDE) // 128, (WIDE - size) // 128) * 128
        window = pl.ds(pl.multiple_of(start, 128), size)
        for to, (one, two) in ((far_high, (own_high, other_high)), (far_low, (own_low, other_low))):
            to[:, pl.ds(pl.multiple_of(size * c, 128), size)] = jnp.concatenate([one[:, window], two[:, window]], axis=0)


def early_ladder(own, other, pieces):
    pairs = own[0].shape[1]
    amp_spec = pl.BlockSpec((None, pairs, WIDE), lambda c: (c, 0, 0))
    far = jax.ShapeDtypeStruct((2 * pairs, SIDE * WINDOW), jnp.bfloat16)
    return pl.pallas_call(
        early_kernel,
        grid=(SIDE,),
        in_specs=[amp_spec] * 4 + [pl.BlockSpec(memory_space=pl.ANY)] * len(pieces),
        out_specs=(pl.BlockSpec(memory_space=pltpu.VMEM),) * 3,
        scratch_shapes=[pltpu.VMEM((64, FRAME, 256), jnp.float32), pltpu.VMEM((WIDE, 256), jnp.float32),
                        pltpu.SemaphoreType.DMA((len(pieces),))],
        out_shape=(jax.ShapeDtypeStruct((2 * pairs, 256), jnp.float32), far, far),
        compiler_params=pltpu.CompilerParams(vmem_limit_bytes=30 * 2**20),
        cost_estimate=pl.CostEstimate(flops=6 * 10**9, bytes_accessed=25 * 10**6, transcendentals=0),
    )(*own, *other, *pieces)


def late_kernel(high_ref, low_ref, up_ref, near_ref, far_ref, total_ref, own_ref, other_ref, matrix, far):
    pairs = total_ref.shape[0] // 2
    core, at = where()
    matrix[...] = jnp.zeros_like(matrix)
    far[:8] = up_ref[...]
    far[8:12] = near_ref[...]
    far[12:] = far_ref[...]

    @pl.when(core == 0)
    def _():
        for z in range(SIDE):
            for y in range(SIDE):
                begin = CHIP_ROWS * (z * SIDE + y)
                matrix[begin:begin + FRAME, :] = far[SIDE * slot(z, at["z"]) + slot(y, at["y"])]

    for z in range(SIDE):
        @pl.when(jnp.logical_and(core == 1, (at["z"] + 2) % SIDE == z))
        def _():
            first = SIDE * CHIP_ROWS * z
            offset = first - min(first // 128, (WIDE - WINDOW) // 128) * 128
            for c in range(SIDE):
                for y in range(SIDE):
                    to = WINDOW * c + offset + CHIP_ROWS * y
                    matrix[to:to + FRAME, :] = far[SIDE * slot(y, at["y"]) + slot(c, at["x"])]

    result = jnp.dot(total_ref[...] + product(high_ref[...], low_ref[...], matrix[...]),
                     reorder(256, 16).astype(jnp.float32), precision=lax.Precision.HIGHEST,
                     preferred_element_type=jnp.float32)
    own_ref[...] = result[:pairs]
    other_ref[...] = result[pairs:]


def late_ladder(high, low, pieces, total):
    out = jax.ShapeDtypeStruct((total.shape[0] // 2, 256), jnp.float32)
    whole = pl.BlockSpec(memory_space=pltpu.VMEM)
    return pl.pallas_call(
        late_kernel,
        in_specs=[whole] * (3 + len(pieces)),
        out_specs=(whole, whole),
        scratch_shapes=[pltpu.VMEM((SIDE * WINDOW, 256), jnp.float32), pltpu.VMEM((16, FRAME, 256), jnp.float32)],
        out_shape=(out, out),
        compiler_params=pltpu.CompilerParams(vmem_limit_bytes=32 * 2**20),
        cost_estimate=pl.CostEstimate(flops=2 * 10**9, bytes_accessed=8 * 10**6, transcendentals=0),
    )(high, low, *pieces, total)


def fetch(value, axes):
    far = permute(value, 2, axes)
    return [value, permute(value, 1, axes), permute(value, -1, axes), far]


def body(ac_factors, bd_factors, amplitudes):
    barrier = lax.optimization_barrier
    bd = bd_factors.reshape(bd_factors.shape[0], bd_factors.shape[2])
    mine, sent = partial_integrals(bd, ac_factors)
    chip = mine + permute(sent, 0, None)
    amplitudes, chip = barrier((amplitudes, chip))
    other = permute(amplitudes, 0, None)
    own = arrange(amplitudes, 44)
    shard = chip[0] + permute(chip[1], 1, "xx") + permute(chip[3], -1, "xx") + permute(chip[2], 2, "xx")

    shard, own = barrier((shard, own))
    line, other = barrier((fetch(shard, STEPS[0]), other))
    halves = [jnp.concatenate(part, axis=0) for part in (line[:2], line[2:])]
    up = [permute(half, 1, STEPS[1]) for half in halves]
    down = [permute(half, -1, STEPS[1]) for half in halves]
    far = [permute(up[0], 1, STEPS[1]), permute(down[1], -1, STEPS[1])]
    first, near = jnp.concatenate(halves + up, axis=0), jnp.concatenate(down, axis=0)
    up_first, down_near = permute(first, 1, STEPS[2]), permute(near, -1, STEPS[2])
    far, other = barrier((far, other))
    far = jnp.concatenate(far, axis=0)
    second = jnp.concatenate([near, far], axis=0)
    down_far = permute(far, -1, STEPS[2])
    up_second, down_first = permute(second, 1, STEPS[2]), permute(first, -1, STEPS[2])
    other = arrange(other, 16)
    up_first, other = barrier((up_first, other))
    far_up = permute(up_first, 1, STEPS[2])
    up_first, down_near = barrier((up_first, down_near))
    far_down = [permute(down_near, -1, STEPS[2]), permute(down_far, -1, STEPS[2])]

    def runs(value):
        return value.reshape(-1, FRAME, 256)

    pieces = (first, second, up_first, up_second, down_first, down_near, down_far)
    total, high, low = early_ladder(own, other, [runs(v) for v in pieces])
    kept, given = late_ladder(high, low, [runs(v) for v in [far_up] + far_down], total)
    return kept + permute(given, 0, None)


def solution(mesh):
    placed = (P("aux", None), P("pair", "aux", None), P(("pair", "aux"), None, None))
    return jax.shard_map(
        body, mesh=mesh, in_specs=placed, out_specs=P(("pair", "aux"), None), check_vma=False
    )
```

time: 112 us -> 103 us (0.920)
  Pallas kernels: 37.1 us -> 29.2 us
  local copies, waits for them, and re-layouts: 6.53 us -> 3.12 us
  waiting for transfers between devices: 37.3 us -> 40.6 us
    pallas_call x2, Pallas kernels: 19 us -> 14.7 us  [the longest x1 11.2 us: early_ladder(): pl.pallas_call(early_kernel, grid=(SIDE,), in_specs=[amp_spec] * 4 + [pl....]
    unnamed x17 -> x10, local copies, waits for them, and re-layouts: 6.45 us -> 3 us
    ppermute x18 -> x23, waiting for transfers between devices: 37.3 us -> 40.6 us  [permute(): return lax.ppermute(value, AXES, pairs)]
    pallas_call x1 -> x2, Pallas kernels: 12.1 us -> 9.51 us  [arrange(): pl.pallas_call(arrange_kernel, grid=(pairs // rows,), out_shape=(out, out...]
    ppermute x18 -> x23, starting transfers between devices: 29.8 us -> 28.8 us  [permute(): return lax.ppermute(value, AXES, pairs)]
  transfers between devices with their start and end apart: 18 -> 23, of which waited for: 11 -> 14; matrix products, arithmetic and copies ran while one was open for 0% -> 0% of each run, Pallas kernels for 23% -> 20%
where the time goes in v3:
time: 103 us
  waiting for transfers between devices  40.6 us (39%)
  Pallas kernels  29.2 us (28%)
  starting transfers between devices  28.8 us (28%)
  local copies, waits for them, and re-layouts  3.12 us (3%)
    ppermute x23, waiting for transfers between devices, permute(): return lax.ppermute(value, AXES, pairs)  40.6 us
    ppermute x23, starting transfers between devices, permute(): return lax.ppermute(value, AXES, pairs)  28.8 us
    pallas_call x1, Pallas kernels, early_ladder(): pl.pallas_call(early_kernel, grid=(SIDE,), in_specs=[amp_spec] * 4 + [pl....  11.2 us
    pallas_call x2, Pallas kernels, arrange(): pl.pallas_call(arrange_kernel, grid=(pairs // rows,), out_shape=(out, out...  9.51 us
    pallas_call x1, Pallas kernels, partial_integrals(): pl.pallas_call(partial_kernel, grid=(2,), out_shape=(out, out), in_specs=...  4.94 us
    pallas_call x1, Pallas kernels, late_ladder(): pl.pallas_call(late_kernel, in_specs=[whole] * (3 + len(pieces)), out_spe...  3.5 us
    unnamed x10, local copies, waits for them, and re-layouts  3 us
  transfers between devices with their start and end apart: 23, of which 14 were waited for; matrix products, arithmetic and copies ran while one was open for 0% of the time, Pallas kernels for 20%

profile of v3, /device:TPU:1, one launch (start us, length us, event | category | flops | bytes accessed | tf_op | source)
XLA Modules:
  0.0 102.8 jit_solution(7227052003359641861)
XLA Ops:
  0.0 0.0 copy-start.1
  0.0 1.1 %copy-done.1 = bf16[2400,128]{1,0:T(8,128)(2,1)S(1)} copy-done((bf16[2400,128]{1,0:T(8,128)(2,1)S(1)}, bf16[2400,128]{1,0:T(8,128)(2,1)}, u32[]{:S(2)}) %copy-start.1) | copy-done | bytes 614424
  1.1 4.9 %shard_map.37 = (f32[4,152,256]{2,1,0:T(8,128)S(1)}, f32[4,152,256]{2,1,0:T(8,128)S(1)}) custom-call(bf16[75,38400]{1,0:T(8,128)(2,1)} %bitcast.33, bf16[75,38400]{1,0:T(8,128)(2,1)} %bitcast.34, bf16[2400,128]{1,0:T(8,128)(2,1)S(1)} %copy-done.1), custom_call_target="tpu_custom_call" | custom-call | flops 1000000000 | bytes 8000000 | tf_op jit(solution)/shard_map/pallas_call | solution.py:101
  6.0 1.5 %collective-permute-start = (f32[4,152,256]{2,1,0:T(8,128)S(1)}, f32[4,152,256]{2,1,0:T(8,128)S(1)}, u32[]{:S(2)}, u32[]{:S(2)}) collective-permute-start(f32[4,152,256]{2,1,0:T(8,128)S(1)} %get-tuple-element.35), channel_id=1, source_target_pairs={{0,4},{1,5},{2,6},{3,7},{4,0},{5,1},{6,2},{7,3},{8,12},{9,13},{10,... | collective-permute-start | bytes 1867784 | tf_op jit(solution)/shard_map/ppermute | solution.py:36
  7.5 1.7 %collective-permute-done = f32[4,152,256]{2,1,0:T(8,128)S(1)} collective-permute-done((f32[4,152,256]{2,1,0:T(8,128)S(1)}, f32[4,152,256]{2,1,0:T(8,128)S(1)}, u32[]{:S(2)}, u32[]{:S(2)}) %collective-permute-start) | collective-permute-done | bytes 622624 | tf_op jit(solution)/shard_map/ppermute | solution.py:36
  9.2 0.1 add.15
  9.3 0.5 collective-permute-start.7
  9.8 1.4 %collective-permute-start.1 = (f32[152,256]{1,0:T(8,128)S(1)}, f32[152,256]{1,0:T(8,128)S(1)}, u32[]{:S(2)}, u32[]{:S(2)}) collective-permute-start(f32[152,256]{1,0:T(8,128)S(1)} %get-tuple-element.63), channel_id=1, source_target_pairs={{0,1},{1,2},{2,3},{3,0},{4,5},{5,6},{6,7},{7,4},{8,9},{9,10},{10,1... | collective-permute-start | bytes 466952 | tf_op jit(solution)/shard_map/ppermute | solution.py:36
  11.1 2.5 %collective-permute-start.3 = (f32[152,256]{1,0:T(8,128)S(1)}, f32[152,256]{1,0:T(8,128)S(1)}, u32[]{:S(2)}, u32[]{:S(2)}) collective-permute-start(f32[152,256]{1,0:T(8,128)S(1)} %get-tuple-element.64), channel_id=1, source_target_pairs={{0,2},{1,3},{2,0},{3,1},{4,6},{5,7},{6,4},{7,5},{8,10},{9,11},{10,... | collective-permute-start | bytes 466952 | tf_op jit(solution)/shard_map/ppermute | solution.py:36
  13.6 1.1 %collective-permute-start.2 = (f32[152,256]{1,0:T(8,128)S(1)}, f32[152,256]{1,0:T(8,128)S(1)}, u32[]{:S(2)}, u32[]{:S(2)}) collective-permute-start(f32[152,256]{1,0:T(8,128)S(1)} %get-tuple-element.65), channel_id=1, source_target_pairs={{0,3},{1,0},{2,1},{3,2},{4,7},{5,4},{6,5},{7,6},{8,11},{9,8},{10,9... | collective-permute-start | bytes 466952 | tf_op jit(solution)/shard_map/ppermute | solution.py:36
  14.7 4.8 %shard_map.38 = (bf16[4,192,2432]{2,1,0:T(8,128)(2,1)S(1)}, bf16[4,192,2432]{2,1,0:T(8,128)(2,1)S(1)}) custom-call(f32[192,8,2400]{2,1,0:T(8,128)} %amp_ref), custom_call_target="tpu_custom_call" | custom-call | flops 1000000 | bytes 15000000 | tf_op jit(solution)/shard_map/pallas_call | solution.py:154
  19.5 0.0 collective-permute-done.1
  19.5 1.4 %collective-permute-done.3 = f32[152,256]{1,0:T(8,128)S(1)} collective-permute-done((f32[152,256]{1,0:T(8,128)S(1)}, f32[152,256]{1,0:T(8,128)S(1)}, u32[]{:S(2)}, u32[]{:S(2)}) %collective-permute-start.3) | collective-permute-done | bytes 155680 | tf_op jit(solution)/shard_map/ppermute | solution.py:36
  20.9 0.0 collective-permute-done.2
  21.0 2.1 %collective-permute-start.6 = (f32[152,256]{1,0:T(8,128)S(1)}, f32[152,256]{1,0:T(8,128)S(1)}, u32[]{:S(2)}, u32[]{:S(2)}) collective-permute-start(f32[152,256]{1,0:T(8,128)S(1)} %fusion.1), channel_id=1, source_target_pairs={{0,16},{1,17},{2,18},{3,19},{4,6},{5,7},{6,4},{7,5},{8,24},{9,25},... | collective-permute-start | bytes 466952 | tf_op jit(solution)/shard_map/ppermute | solution.py:36
  23.1 1.0 collective-permute-start.5
  24.1 0.5 collective-permute-start.4
  24.6 2.4 %collective-permute-done.6 = f32[152,256]{1,0:T(8,128)S(1)} collective-permute-done((f32[152,256]{1,0:T(8,128)S(1)}, f32[152,256]{1,0:T(8,128)S(1)}, u32[]{:S(2)}, u32[]{:S(2)}) %collective-permute-start.6) | collective-permute-done | bytes 155680 | tf_op jit(solution)/shard_map/ppermute | solution.py:36
  27.0 1.4 %collective-permute-done.5 = f32[152,256]{1,0:T(8,128)S(1)} collective-permute-done((f32[152,256]{1,0:T(8,128)S(1)}, f32[152,256]{1,0:T(8,128)S(1)}, u32[]{:S(2)}, u32[]{:S(2)}) %collective-permute-start.5) | collective-permute-done | bytes 155680 | tf_op jit(solution)/shard_map/ppermute | solution.py:36
  28.4 1.0 %collective-permute-done.4 = f32[152,256]{1,0:T(8,128)S(1)} collective-permute-done((f32[152,256]{1,0:T(8,128)S(1)}, f32[152,256]{1,0:T(8,128)S(1)}, u32[]{:S(2)}, u32[]{:S(2)}) %collective-permute-start.4) | collective-permute-done | bytes 155680 | tf_op jit(solution)/shard_map/ppermute | solution.py:36
  29.4 2.8 %collective-permute-done.7.amp_ref = f32[192,8,2400]{2,1,0:T(8,128)} collective-permute-done((f32[192,8,2400]{2,1,0:T(8,128)}, f32[192,8,2400]{2,1,0:T(8,128)}, u32[]{:S(2)}, u32[]{:S(2)}) %collective-permute-start.7) | collective-permute-done | bytes 14745632 | tf_op jit(solution)/shard_map/ppermute | solution.py:36
  32.3 1.5 %collective-permute-start.8 = (f32[304,256]{1,0:T(8,128)S(1)}, f32[304,256]{1,0:T(8,128)S(1)}, u32[]{:S(2)}, u32[]{:S(2)}) collective-permute-start(f32[304,256]{1,0:T(8,128)S(1)} %get-tuple-element.70), channel_id=1, source_target_pairs={{0,32},{1,33},{2,34},{3,35},{4,12},{5,13},{6,14},{7,15},{8,40},{9,... | collective-permute-start | bytes 933896 | tf_op jit(solution)/shard_map/ppermute | solution.py:36
  33.8 1.4 %collective-permute-start.9 = (f32[304,256]{1,0:T(8,128)S(1)}, f32[304,256]{1,0:T(8,128)S(1)}, u32[]{:S(2)}, u32[]{:S(2)}) collective-permute-start(f32[304,256]{1,0:T(8,128)S(1)} %get-tuple-element.66), channel_id=1, source_target_pairs={{0,32},{1,33},{2,34},{3,35},{4,12},{5,13},{6,14},{7,15},{8,40},{9,... | collective-permute-start | bytes 933896 | tf_op jit(solution)/shard_map/ppermute | solution.py:36
  35.2 1.4 %collective-permute-start.12 = (f32[304,256]{1,0:T(8,128)S(1)}, f32[304,256]{1,0:T(8,128)S(1)}, u32[]{:S(2)}, u32[]{:S(2)}) collective-permute-start(f32[304,256]{1,0:T(8,128)S(1)} %get-tuple-element.66), channel_id=1, source_target_pairs={{0,96},{1,97},{2,98},{3,99},{4,28},{5,29},{6,30},{7,31},{8,104},{9... | collective-permute-start | bytes 933896 | tf_op jit(solution)/shard_map/ppermute | solution.py:36
  36.5 0.3 collective-permute-start.14
  36.9 2.9 %collective-permute-done.8 = f32[304,256]{1,0:T(8,128)S(1)} collective-permute-done((f32[304,256]{1,0:T(8,128)S(1)}, f32[304,256]{1,0:T(8,128)S(1)}, u32[]{:S(2)}, u32[]{:S(2)}) %collective-permute-start.8) | collective-permute-done | bytes 311328 | tf_op jit(solution)/shard_map/ppermute | solution.py:36
  39.8 3.3 %collective-permute-done.9 = f32[304,256]{1,0:T(8,128)S(1)} collective-permute-done((f32[304,256]{1,0:T(8,128)S(1)}, f32[304,256]{1,0:T(8,128)S(1)}, u32[]{:S(2)}, u32[]{:S(2)}) %collective-permute-start.9) | collective-permute-done | bytes 311328 | tf_op jit(solution)/shard_map/ppermute | solution.py:36
  43.1 1.4 %collective-permute-start.10 = (f32[1216,256]{1,0:T(8,128)S(1)}, f32[1216,256]{1,0:T(8,128)S(1)}, u32[]{:S(2)}, u32[]{:S(2)}) collective-permute-start(f32[1216,256]{1,0:T(8,128)S(1)} %constant_dynamic-update-slice_fusion.4), channel_id=1, source_target_pairs={{0,1},{1,2},{2,3},{3,0},{4,36},{5,37},{6,38},{7,39},{8,9},{9,10},{... | collective-permute-start | bytes 3735560 | tf_op jit(solution)/shard_map/ppermute | solution.py:36
  44.5 0.0 collective-permute-done.12
  44.5 1.8 %collective-permute-start.13 = (f32[304,256]{1,0:T(8,128)S(1)}, f32[304,256]{1,0:T(8,128)S(1)}, u32[]{:S(2)}, u32[]{:S(2)}) collective-permute-start(f32[304,256]{1,0:T(8,128)S(1)} %collective-permute-done.12), channel_id=1, source_target_pairs={{0,96},{1,97},{2,98},{3,99},{4,28},{5,29},{6,30},{7,31},{8,104},{9... | collective-permute-start | bytes 933896 | tf_op jit(solution)/shard_map/ppermute | solution.py:36
  46.3 0.0 collective-permute-start.11
  46.3 2.2 %collective-permute-start.17 = (f32[1216,256]{1,0:T(8,128)S(1)}, f32[1216,256]{1,0:T(8,128)S(1)}, u32[]{:S(2)}, u32[]{:S(2)}) collective-permute-start(f32[1216,256]{1,0:T(8,128)S(1)} %constant_dynamic-update-slice_fusion.4), channel_id=1, source_target_pairs={{0,3},{1,0},{2,1},{3,2},{4,100},{5,101},{6,102},{7,103},{8,11},{9,... | collective-permute-start | bytes 3735560 | tf_op jit(solution)/shard_map/ppermute | solution.py:36
  48.5 0.0 collective-permute-done.14
  48.6 2.0 %collective-permute-done.13 = f32[304,256]{1,0:T(8,128)S(1)} collective-permute-done((f32[304,256]{1,0:T(8,128)S(1)}, f32[304,256]{1,0:T(8,128)S(1)}, u32[]{:S(2)}, u32[]{:S(2)}) %collective-permute-start.13) | collective-permute-done | bytes 311328 | tf_op jit(solution)/shard_map/ppermute | solution.py:36
  50.6 3.0 %collective-permute-done.11 = f32[304,256]{1,0:T(8,128)S(1)} collective-permute-done((f32[304,256]{1,0:T(8,128)S(1)}, f32[304,256]{1,0:T(8,128)S(1)}, u32[]{:S(2)}, u32[]{:S(2)}) %collective-permute-start.11) | collective-permute-done | bytes 311328 | tf_op jit(solution)/shard_map/ppermute | solution.py:36
  53.6 1.7 %collective-permute-start.16 = (f32[1216,256]{1,0:T(8,128)S(1)}, f32[1216,256]{1,0:T(8,128)S(1)}, u32[]{:S(2)}, u32[]{:S(2)}) collective-permute-start(f32[1216,256]{1,0:T(8,128)S(1)} %constant_dynamic-update-slice_fusion.10), channel_id=1, source_target_pairs={{0,1},{1,2},{2,3},{3,0},{4,36},{5,37},{6,38},{7,39},{8,9},{9,10},{... | collective-permute-start | bytes 3735560 | tf_op jit(solution)/shard_map/ppermute | solution.py:36
  55.4 1.1 %collective-permute-start.15 = (f32[608,256]{1,0:T(8,128)S(1)}, f32[608,256]{1,0:T(8,128)S(1)}, u32[]{:S(2)}, u32[]{:S(2)}) collective-permute-start(f32[608,256]{1,0:T(8,128)S(1)} %pad_maximum_fusion), channel_id=1, source_target_pairs={{0,3},{1,0},{2,1},{3,2},{4,100},{5,101},{6,102},{7,103},{8,11},{9,... | collective-permute-start | bytes 1867784 | tf_op jit(solution)/shard_map/ppermute | solution.py:36
  56.5 4.8 %shard_map.39 = (bf16[4,192,2432]{2,1,0:T(8,128)(2,1)S(1)}, bf16[4,192,2432]{2,1,0:T(8,128)(2,1)S(1)}) custom-call(f32[192,8,2400]{2,1,0:T(8,128)} %collective-permute-done.7.amp_ref), custom_call_target="tpu_custom_call" | custom-call | flops 1000000 | bytes 15000000 | tf_op jit(solution)/shard_map/pallas_call | solution.py:154
  61.2 0.0 copy-start
  61.2 1.8 %copy-done = bf16[4,192,2432]{2,1,0:T(8,128)(2,1)} copy-done((bf16[4,192,2432]{2,1,0:T(8,128)(2,1)}, bf16[4,192,2432]{2,1,0:T(8,128)(2,1)S(1)}, u32[]{:S(2)}) %copy-start) | copy-done | bytes 3735576
  63.1 1.1 %collective-permute-start.18 = (f32[608,256]{1,0:T(8,128)S(1)}, f32[608,256]{1,0:T(8,128)S(1)}, u32[]{:S(2)}, u32[]{:S(2)}) collective-permute-start(f32[608,256]{1,0:T(8,128)S(1)} %pad_maximum_fusion.1), channel_id=1, source_target_pairs={{0,3},{1,0},{2,1},{3,2},{4,100},{5,101},{6,102},{7,103},{8,11},{9,... | collective-permute-start | bytes 1867784 | tf_op jit(solution)/shard_map/ppermute | solution.py:36
  64.1 0.7 collective-permute-done.10
  64.9 0.0 collective-permute-start.19
  64.9 14.3 %collective-permute-done.18 = f32[608,256]{1,0:T(8,128)S(1)} collective-permute-done((f32[608,256]{1,0:T(8,128)S(1)}, f32[608,256]{1,0:T(8,128)S(1)}, u32[]{:S(2)}, u32[]{:S(2)}) %collective-permute-start.18) | collective-permute-done | bytes 622624 | tf_op jit(solution)/shard_map/ppermute | solution.py:36
  79.2 3.2 %collective-permute-start.21 = (f32[608,256]{1,0:T(8,128)S(1)}, f32[608,256]{1,0:T(8,128)S(1)}, u32[]{:S(2)}, u32[]{:S(2)}) collective-permute-start(f32[608,256]{1,0:T(8,128)S(1)} %collective-permute-done.18), channel_id=1, source_target_pairs={{0,3},{1,0},{2,1},{3,2},{4,100},{5,101},{6,102},{7,103},{8,11},{9,... | collective-permute-start | bytes 1867784 | tf_op jit(solution)/shard_map/ppermute | solution.py:36
  82.4 0.0 collective-permute-done.15
  82.5 0.0 collective-permute-start.20
  82.5 0.0 collective-permute-done.17
  82.5 0.0 collective-permute-done.16
  82.5 11.2 %shard_map.40 = (f32[384,256]{1,0:T(8,128)S(1)}, bf16[384,3072]{1,0:T(8,128)(2,1)S(1)}, bf16[384,3072]{1,0:T(8,128)(2,1)S(1)}) custom-call(bf16[4,192,2432]{2,1,0:T(8,128)(2,1)S(1)} %get-tuple-element.40.own_high, bf16[4,192,2432]{2,1,0:T(8,128)(2,1)S(1)} %get-tuple-element.41.own_low, bf16[4,192,2432]{2,1,0:T(8,128)(2,1)S(1)} %get-tuple-element.51.other_high, ...), custom_call_target="tpu_custom_call" | custom-call | flops 6000000000 | bytes 25000000 | tf_op jit(solution)/shard_map/pallas_call | solution.py:230
  93.7 0.0 collective-permute-done.21
  93.7 2.6 %collective-permute-done.20 = f32[608,256]{1,0:T(8,128)S(1)} collective-permute-done((f32[608,256]{1,0:T(8,128)S(1)}, f32[608,256]{1,0:T(8,128)S(1)}, u32[]{:S(2)}, u32[]{:S(2)}) %collective-permute-start.20) | collective-permute-done | bytes 622624 | tf_op jit(solution)/shard_map/ppermute | solution.py:36
  96.3 0.0 collective-permute-done.19
  96.3 3.5 %shard_map.41 = (f32[192,256]{1,0:T(8,128)S(1)}, f32[192,256]{1,0:T(8,128)S(1)}) custom-call(bf16[384,3072]{1,0:T(8,128)(2,1)S(1)} %get-tuple-element.58.high_ref, bf16[384,3072]{1,0:T(8,128)(2,1)S(1)} %get-tuple-element.59.low_ref, f32[8,152,256]{2,1,0:T(8,128)S(1)} %bitcast.25, f32[4,152,256]{2,1,0:T(8,128)S(1)} %bitcast.32, f32[4,152,256]{2,1,0:T(8,128)S(1)} %bitcast.31, ...), custom_call_target="tpu_custom_call" | custom-call | flops 2000000000 | bytes 8000000 | tf_op jit(solution)/shard_map/pallas_call | solution.py:278
  99.8 1.3 %collective-permute-start.22 = (f32[192,256]{1,0:T(8,128)S(1)}, f32[192,256]{1,0:T(8,128)S(1)}, u32[]{:S(2)}, u32[]{:S(2)}) collective-permute-start(f32[192,256]{1,0:T(8,128)S(1)} %get-tuple-element.62), channel_id=1, source_target_pairs={{0,4},{1,5},{2,6},{3,7},{4,0},{5,1},{6,2},{7,3},{8,12},{9,13},{10,... | collective-permute-start | bytes 589832 | tf_op jit(solution)/shard_map/ppermute | solution.py:36
  101.1 1.1 %collective-permute-done.22 = f32[192,256]{1,0:T(8,128)S(1)} collective-permute-done((f32[192,256]{1,0:T(8,128)S(1)}, f32[192,256]{1,0:T(8,128)S(1)}, u32[]{:S(2)}, u32[]{:S(2)}) %collective-permute-start.22) | collective-permute-done | bytes 196640 | tf_op jit(solution)/shard_map/ppermute | solution.py:36
  102.1 0.7 add.19
  (14 shorter events, 0.4 us)
Async XLA Ops:
  0.0 1.1 %copy-start.1 = (bf16[2400,128]{1,0:T(8,128)(2,1)S(1)}, bf16[2400,128]{1,0:T(8,128)(2,1)}, u32[]{:S(2)}) copy-start(bf16[2400,128]{1,0:T(8,128)(2,1)} %ac_ref.1) | copy-start | bytes 1843204
  6.0 3.2 %collective-permute-start = (f32[4,152,256]{2,1,0:T(8,128)S(1)}, f32[4,152,256]{2,1,0:T(8,128)S(1)}, u32[]{:S(2)}, u32[]{:S(2)}) collective-permute-start(f32[4,152,256]{2,1,0:T(8,128)S(1)} %get-tuple-element.35), channel_id=1, source_target_pairs={{0,4},{1,5},{2,6},{3,7},{4,0},{5,1},{6,2},{7,3},{8,12},{9,13},{10,... | collective-permute-start | bytes 1867784 | tf_op jit(solution)/shard_map/ppermute | solution.py:36
  9.3 23.0 %collective-permute-start.7 = (f32[192,8,2400]{2,1,0:T(8,128)}, f32[192,8,2400]{2,1,0:T(8,128)}, u32[]{:S(2)}, u32[]{:S(2)}) collective-permute-start(f32[192,8,2400]{2,1,0:T(8,128)} %amp_ref), channel_id=1, source_target_pairs={{0,4},{1,5},{2,6},{3,7},{4,0},{5,1},{6,2},{7,3},{8,12},{9,13},{10,... | collective-permute-start | bytes 44236808 | tf_op jit(solution)/shard_map/ppermute | solution.py:36
  9.8 9.7 %collective-permute-start.1 = (f32[152,256]{1,0:T(8,128)S(1)}, f32[152,256]{1,0:T(8,128)S(1)}, u32[]{:S(2)}, u32[]{:S(2)}) collective-permute-start(f32[152,256]{1,0:T(8,128)S(1)} %get-tuple-element.63), channel_id=1, source_target_pairs={{0,1},{1,2},{2,3},{3,0},{4,5},{5,6},{6,7},{7,4},{8,9},{9,10},{10,1... | collective-permute-start | bytes 466952 | tf_op jit(solution)/shard_map/ppermute | solution.py:36
  11.1 9.8 %collective-permute-start.3 = (f32[152,256]{1,0:T(8,128)S(1)}, f32[152,256]{1,0:T(8,128)S(1)}, u32[]{:S(2)}, u32[]{:S(2)}) collective-permute-start(f32[152,256]{1,0:T(8,128)S(1)} %get-tuple-element.64), channel_id=1, source_target_pairs={{0,2},{1,3},{2,0},{3,1},{4,6},{5,7},{6,4},{7,5},{8,10},{9,11},{10,... | collective-permute-start | bytes 466952 | tf_op jit(solution)/shard_map/ppermute | solution.py:36
  13.6 7.4 %collective-permute-start.2 = (f32[152,256]{1,0:T(8,128)S(1)}, f32[152,256]{1,0:T(8,128)S(1)}, u32[]{:S(2)}, u32[]{:S(2)}) collective-permute-start(f32[152,256]{1,0:T(8,128)S(1)} %get-tuple-element.65), channel_id=1, source_target_pairs={{0,3},{1,0},{2,1},{3,2},{4,7},{5,4},{6,5},{7,6},{8,11},{9,8},{10,9... | collective-permute-start | bytes 466952 | tf_op jit(solution)/shard_map/ppermute | solution.py:36
  21.0 6.0 %collective-permute-start.6 = (f32[152,256]{1,0:T(8,128)S(1)}, f32[152,256]{1,0:T(8,128)S(1)}, u32[]{:S(2)}, u32[]{:S(2)}) collective-permute-start(f32[152,256]{1,0:T(8,128)S(1)} %fusion.1), channel_id=1, source_target_pairs={{0,16},{1,17},{2,18},{3,19},{4,6},{5,7},{6,4},{7,5},{8,24},{9,25},... | collective-permute-start | bytes 466952 | tf_op jit(solution)/shard_map/ppermute | solution.py:36
  23.1 5.2 %collective-permute-start.5 = (f32[152,256]{1,0:T(8,128)S(1)}, f32[152,256]{1,0:T(8,128)S(1)}, u32[]{:S(2)}, u32[]{:S(2)}) collective-permute-start(f32[152,256]{1,0:T(8,128)S(1)} %fusion.1), channel_id=1, source_target_pairs={{0,24},{1,25},{2,26},{3,27},{4,7},{5,4},{6,5},{7,6},{8,0},{9,1},{1... | collective-permute-start | bytes 466952 | tf_op jit(solution)/shard_map/ppermute | solution.py:36
  24.1 5.3 %collective-permute-start.4 = (f32[152,256]{1,0:T(8,128)S(1)}, f32[152,256]{1,0:T(8,128)S(1)}, u32[]{:S(2)}, u32[]{:S(2)}) collective-permute-start(f32[152,256]{1,0:T(8,128)S(1)} %fusion.1), channel_id=1, source_target_pairs={{0,8},{1,9},{2,10},{3,11},{4,5},{5,6},{6,7},{7,4},{8,16},{9,17},{1... | collective-permute-start | bytes 466952 | tf_op jit(solution)/shard_map/ppermute | solution.py:36
  32.3 7.5 %collective-permute-start.8 = (f32[304,256]{1,0:T(8,128)S(1)}, f32[304,256]{1,0:T(8,128)S(1)}, u32[]{:S(2)}, u32[]{:S(2)}) collective-permute-start(f32[304,256]{1,0:T(8,128)S(1)} %get-tuple-element.70), channel_id=1, source_target_pairs={{0,32},{1,33},{2,34},{3,35},{4,12},{5,13},{6,14},{7,15},{8,40},{9,... | collective-permute-start | bytes 933896 | tf_op jit(solution)/shard_map/ppermute | solution.py:36
  33.8 9.3 %collective-permute-start.9 = (f32[304,256]{1,0:T(8,128)S(1)}, f32[304,256]{1,0:T(8,128)S(1)}, u32[]{:S(2)}, u32[]{:S(2)}) collective-permute-start(f32[304,256]{1,0:T(8,128)S(1)} %get-tuple-element.66), channel_id=1, source_target_pairs={{0,32},{1,33},{2,34},{3,35},{4,12},{5,13},{6,14},{7,15},{8,40},{9,... | collective-permute-start | bytes 933896 | tf_op jit(solution)/shard_map/ppermute | solution.py:36
  35.2 9.4 %collective-permute-start.12 = (f32[304,256]{1,0:T(8,128)S(1)}, f32[304,256]{1,0:T(8,128)S(1)}, u32[]{:S(2)}, u32[]{:S(2)}) collective-permute-start(f32[304,256]{1,0:T(8,128)S(1)} %get-tuple-element.66), channel_id=1, source_target_pairs={{0,96},{1,97},{2,98},{3,99},{4,28},{5,29},{6,30},{7,31},{8,104},{9... | collective-permute-start | bytes 933896 | tf_op jit(solution)/shard_map/ppermute | solution.py:36
  36.5 12.0 %collective-permute-start.14 = (f32[304,256]{1,0:T(8,128)S(1)}, f32[304,256]{1,0:T(8,128)S(1)}, u32[]{:S(2)}, u32[]{:S(2)}) collective-permute-start(f32[304,256]{1,0:T(8,128)S(1)} %get-tuple-element.70), channel_id=1, source_target_pairs={{0,96},{1,97},{2,98},{3,99},{4,28},{5,29},{6,30},{7,31},{8,104},{9... | collective-permute-start | bytes 933896 | tf_op jit(solution)/shard_map/ppermute | solution.py:36
  43.1 21.8 %collective-permute-start.10 = (f32[1216,256]{1,0:T(8,128)S(1)}, f32[1216,256]{1,0:T(8,128)S(1)}, u32[]{:S(2)}, u32[]{:S(2)}) collective-permute-start(f32[1216,256]{1,0:T(8,128)S(1)} %constant_dynamic-update-slice_fusion.4), channel_id=1, source_target_pairs={{0,1},{1,2},{2,3},{3,0},{4,36},{5,37},{6,38},{7,39},{8,9},{9,10},{... | collective-permute-start | bytes 3735560 | tf_op jit(solution)/shard_map/ppermute | solution.py:36
  44.5 6.0 %collective-permute-start.13 = (f32[304,256]{1,0:T(8,128)S(1)}, f32[304,256]{1,0:T(8,128)S(1)}, u32[]{:S(2)}, u32[]{:S(2)}) collective-permute-start(f32[304,256]{1,0:T(8,128)S(1)} %collective-permute-done.12), channel_id=1, source_target_pairs={{0,96},{1,97},{2,98},{3,99},{4,28},{5,29},{6,30},{7,31},{8,104},{9... | collective-permute-start | bytes 933896 | tf_op jit(solution)/shard_map/ppermute | solution.py:36
  46.3 7.3 %collective-permute-start.11 = (f32[304,256]{1,0:T(8,128)S(1)}, f32[304,256]{1,0:T(8,128)S(1)}, u32[]{:S(2)}, u32[]{:S(2)}) collective-permute-start(f32[304,256]{1,0:T(8,128)S(1)} %collective-permute-done.8), channel_id=1, source_target_pairs={{0,32},{1,33},{2,34},{3,35},{4,12},{5,13},{6,14},{7,15},{8,40},{9,... | collective-permute-start | bytes 933896 | tf_op jit(solution)/shard_map/ppermute | solution.py:36
  46.3 36.2 %collective-permute-start.17 = (f32[1216,256]{1,0:T(8,128)S(1)}, f32[1216,256]{1,0:T(8,128)S(1)}, u32[]{:S(2)}, u32[]{:S(2)}) collective-permute-start(f32[1216,256]{1,0:T(8,128)S(1)} %constant_dynamic-update-slice_fusion.4), channel_id=1, source_target_pairs={{0,3},{1,0},{2,1},{3,2},{4,100},{5,101},{6,102},{7,103},{8,11},{9,... | collective-permute-start | bytes 3735560 | tf_op jit(solution)/shard_map/ppermute | solution.py:36
  53.6 28.9 %collective-permute-start.16 = (f32[1216,256]{1,0:T(8,128)S(1)}, f32[1216,256]{1,0:T(8,128)S(1)}, u32[]{:S(2)}, u32[]{:S(2)}) collective-permute-start(f32[1216,256]{1,0:T(8,128)S(1)} %constant_dynamic-update-slice_fusion.10), channel_id=1, source_target_pairs={{0,1},{1,2},{2,3},{3,0},{4,36},{5,37},{6,38},{7,39},{8,9},{9,10},{... | collective-permute-start | bytes 3735560 | tf_op jit(solution)/shard_map/ppermute | solution.py:36
  55.4 27.1 %collective-permute-start.15 = (f32[608,256]{1,0:T(8,128)S(1)}, f32[608,256]{1,0:T(8,128)S(1)}, u32[]{:S(2)}, u32[]{:S(2)}) collective-permute-start(f32[608,256]{1,0:T(8,128)S(1)} %pad_maximum_fusion), channel_id=1, source_target_pairs={{0,3},{1,0},{2,1},{3,2},{4,100},{5,101},{6,102},{7,103},{8,11},{9,... | collective-permute-start | bytes 1867784 | tf_op jit(solution)/shard_map/ppermute | solution.py:36
  61.2 1.8 %copy-start = (bf16[4,192,2432]{2,1,0:T(8,128)(2,1)}, bf16[4,192,2432]{2,1,0:T(8,128)(2,1)S(1)}, u32[]{:S(2)}) copy-start(bf16[4,192,2432]{2,1,0:T(8,128)(2,1)S(1)} %get-tuple-element.52.other_low) | copy-start | bytes 11206660
  63.1 16.1 %collective-permute-start.18 = (f32[608,256]{1,0:T(8,128)S(1)}, f32[608,256]{1,0:T(8,128)S(1)}, u32[]{:S(2)}, u32[]{:S(2)}) collective-permute-start(f32[608,256]{1,0:T(8,128)S(1)} %pad_maximum_fusion.1), channel_id=1, source_target_pairs={{0,3},{1,0},{2,1},{3,2},{4,100},{5,101},{6,102},{7,103},{8,11},{9,... | collective-permute-start | bytes 1867784 | tf_op jit(solution)/shard_map/ppermute | solution.py:36
  64.9 31.4 %collective-permute-start.19 = (f32[1216,256]{1,0:T(8,128)S(1)}, f32[1216,256]{1,0:T(8,128)S(1)}, u32[]{:S(2)}, u32[]{:S(2)}) collective-permute-start(f32[1216,256]{1,0:T(8,128)S(1)} %collective-permute-done.10), channel_id=1, source_target_pairs={{0,1},{1,2},{2,3},{3,0},{4,36},{5,37},{6,38},{7,39},{8,9},{9,10},{... | collective-permute-start | bytes 3735560 | tf_op jit(solution)/shard_map/ppermute | solution.py:36
  79.2 14.5 %collective-permute-start.21 = (f32[608,256]{1,0:T(8,128)S(1)}, f32[608,256]{1,0:T(8,128)S(1)}, u32[]{:S(2)}, u32[]{:S(2)}) collective-permute-start(f32[608,256]{1,0:T(8,128)S(1)} %collective-permute-done.18), channel_id=1, source_target_pairs={{0,3},{1,0},{2,1},{3,2},{4,100},{5,101},{6,102},{7,103},{8,11},{9,... | collective-permute-start | bytes 1867784 | tf_op jit(solution)/shard_map/ppermute | solution.py:36
  82.5 13.8 %collective-permute-start.20 = (f32[608,256]{1,0:T(8,128)S(1)}, f32[608,256]{1,0:T(8,128)S(1)}, u32[]{:S(2)}, u32[]{:S(2)}) collective-permute-start(f32[608,256]{1,0:T(8,128)S(1)} %collective-permute-done.15), channel_id=1, source_target_pairs={{0,3},{1,0},{2,1},{3,2},{4,100},{5,101},{6,102},{7,103},{8,11},{9,... | collective-permute-start | bytes 1867784 | tf_op jit(solution)/shard_map/ppermute | solution.py:36
  99.8 2.3 %collective-permute-start.22 = (f32[192,256]{1,0:T(8,128)S(1)}, f32[192,256]{1,0:T(8,128)S(1)}, u32[]{:S(2)}, u32[]{:S(2)}) collective-permute-start(f32[192,256]{1,0:T(8,128)S(1)} %get-tuple-element.62), channel_id=1, source_target_pairs={{0,4},{1,5},{2,6},{3,7},{4,0},{5,1},{6,2},{7,3},{8,12},{9,13},{10,... | collective-permute-start | bytes 589832 | tf_op jit(solution)/shard_map/ppermute | solution.py:36

commit v4 on v3

--- a/solution.py
+++ b/solution.py
@@ -103,7 +103,8 @@
         grid=(2,),
         out_shape=(out, out),
         in_specs=[pl.BlockSpec((height, 4 * rows), lambda g: (0, 2 * g)),
-                  pl.BlockSpec((height, 4 * rows), lambda g: (0, 2 * g + 1)), whole],
+                  pl.BlockSpec((height, 4 * rows), lambda g: (0, 2 * g + 1)),
+                  pl.BlockSpec(ac.shape, lambda g: (0, 0))],
         out_specs=(whole, whole),
         scratch_shapes=[pltpu.VMEM((4, -(-(rows + 96) // 128) * 128, 128), jnp.bfloat16),
                         pltpu.VMEM((16, bd.shape[0], 128), jnp.float32)],
@@ -317,8 +318,10 @@
     other = arrange(other, 16)
     up_first, other = barrier((up_first, other))
     far_up = permute(up_first, 1, STEPS[2])
-    up_first, down_near = barrier((up_first, down_near))
-    far_down = [permute(down_near, -1, STEPS[2]), permute(down_far, -1, STEPS[2])]
+    up_first, down_far = barrier((up_first, down_far))
+    far_far = permute(down_far, -1, STEPS[2])
+    down_near, down_first, up_second = barrier((down_near, down_first, up_second))
+    far_down = [permute(down_near, -1, STEPS[2]), far_far]
 
     def runs(value):
         return value.reshape(-1, FRAME, 256)

time: 103 us -> 99.7 us (0.968)
  waiting for transfers between devices: 40.6 us -> 35.2 us
  starting transfers between devices: 28.8 us -> 30.9 us
    ppermute x23, waiting for transfers between devices: 40.6 us -> 35.2 us  [permute(): return lax.ppermute(value, AXES, pairs)]
    ppermute x23, starting transfers between devices: 28.8 us -> 30.9 us  [permute(): return lax.ppermute(value, AXES, pairs)]
  transfers between devices with their start and end apart: 23 -> 23, of which waited for: 14 -> 14; matrix products, arithmetic and copies ran while one was open for 0% -> 0% of each run, Pallas kernels for 20% -> 21%
where the time goes in v4:
time: 99.7 us; the launch traced here: 99.4 us
  waiting for transfers between devices  35.2 us (35%)
  starting transfers between devices  30.9 us (31%)
  Pallas kernels  29.2 us (29%)
  local copies, waits for them, and re-layouts  3.12 us (3%)
    ppermute x23, waiting for transfers between devices, permute(): return lax.ppermute(value, AXES, pairs)  35.2 us
    ppermute x23, starting transfers between devices, permute(): return lax.ppermute(value, AXES, pairs)  30.9 us
    pallas_call x1, Pallas kernels, early_ladder(): pl.pallas_call(early_kernel, grid=(SIDE,), in_specs=[amp_spec] * 4 + [pl....  11.2 us
    pallas_call x2, Pallas kernels, arrange(): pl.pallas_call(arrange_kernel, grid=(pairs // rows,), out_shape=(out, out...  9.51 us
    pallas_call x1, Pallas kernels, partial_integrals(): pl.pallas_call(partial_kernel, grid=(2,), out_shape=(out, out), in_specs=...  4.94 us
    pallas_call x1, Pallas kernels, late_ladder(): pl.pallas_call(late_kernel, in_specs=[whole] * (3 + len(pieces)), out_spe...  3.5 us
    unnamed x10, local copies, waits for them, and re-layouts  3 us
  transfers between devices with their start and end apart: 23, of which 14 were waited for; matrix products, arithmetic and copies ran while one was open for 0% of the time, Pallas kernels for 21%

profile of v4, /device:TPU:1, one launch (start us, length us, event | category | flops | bytes accessed | tf_op | source)
XLA Modules:
  0.0 99.4 jit_solution(1799852707613037985)
XLA Ops:
  0.0 0.0 copy-start.1
  0.0 1.1 %copy-done.1 = bf16[2400,128]{1,0:T(8,128)(2,1)S(1)} copy-done((bf16[2400,128]{1,0:T(8,128)(2,1)S(1)}, bf16[2400,128]{1,0:T(8,128)(2,1)}, u32[]{:S(2)}) %copy-start.1) | copy-done | bytes 614424
  1.1 4.9 %shard_map.37 = (f32[4,152,256]{2,1,0:T(8,128)S(1)}, f32[4,152,256]{2,1,0:T(8,128)S(1)}) custom-call(bf16[75,38400]{1,0:T(8,128)(2,1)} %bitcast.33, bf16[75,38400]{1,0:T(8,128)(2,1)} %bitcast.34, bf16[2400,128]{1,0:T(8,128)(2,1)S(1)} %copy-done.1), custom_call_target="tpu_custom_call" | custom-call | flops 1000000000 | bytes 8000000 | tf_op jit(solution)/shard_map/pallas_call | solution.py:101
  6.0 1.5 %collective-permute-start = (f32[4,152,256]{2,1,0:T(8,128)S(1)}, f32[4,152,256]{2,1,0:T(8,128)S(1)}, u32[]{:S(2)}, u32[]{:S(2)}) collective-permute-start(f32[4,152,256]{2,1,0:T(8,128)S(1)} %get-tuple-element.38), channel_id=1, source_target_pairs={{0,4},{1,5},{2,6},{3,7},{4,0},{5,1},{6,2},{7,3},{8,12},{9,13},{10,... | collective-permute-start | bytes 1867784 | tf_op jit(solution)/shard_map/ppermute | solution.py:36
  7.5 1.7 %collective-permute-done = f32[4,152,256]{2,1,0:T(8,128)S(1)} collective-permute-done((f32[4,152,256]{2,1,0:T(8,128)S(1)}, f32[4,152,256]{2,1,0:T(8,128)S(1)}, u32[]{:S(2)}, u32[]{:S(2)}) %collective-permute-start) | collective-permute-done | bytes 622624 | tf_op jit(solution)/shard_map/ppermute | solution.py:36
  9.2 0.1 add.15
  9.3 0.5 collective-permute-start.7
  9.8 1.4 %collective-permute-start.1 = (f32[152,256]{1,0:T(8,128)S(1)}, f32[152,256]{1,0:T(8,128)S(1)}, u32[]{:S(2)}, u32[]{:S(2)}) collective-permute-start(f32[152,256]{1,0:T(8,128)S(1)} %get-tuple-element.69), channel_id=1, source_target_pairs={{0,1},{1,2},{2,3},{3,0},{4,5},{5,6},{6,7},{7,4},{8,9},{9,10},{10,1... | collective-permute-start | bytes 466952 | tf_op jit(solution)/shard_map/ppermute | solution.py:36
  11.1 2.5 %collective-permute-start.3 = (f32[152,256]{1,0:T(8,128)S(1)}, f32[152,256]{1,0:T(8,128)S(1)}, u32[]{:S(2)}, u32[]{:S(2)}) collective-permute-start(f32[152,256]{1,0:T(8,128)S(1)} %get-tuple-element.70), channel_id=1, source_target_pairs={{0,2},{1,3},{2,0},{3,1},{4,6},{5,7},{6,4},{7,5},{8,10},{9,11},{10,... | collective-permute-start | bytes 466952 | tf_op jit(solution)/shard_map/ppermute | solution.py:36
  13.6 1.1 %collective-permute-start.2 = (f32[152,256]{1,0:T(8,128)S(1)}, f32[152,256]{1,0:T(8,128)S(1)}, u32[]{:S(2)}, u32[]{:S(2)}) collective-permute-start(f32[152,256]{1,0:T(8,128)S(1)} %get-tuple-element.71), channel_id=1, source_target_pairs={{0,3},{1,0},{2,1},{3,2},{4,7},{5,4},{6,5},{7,6},{8,11},{9,8},{10,9... | collective-permute-start | bytes 466952 | tf_op jit(solution)/shard_map/ppermute | solution.py:36
  14.7 4.8 %shard_map.38 = (bf16[4,192,2432]{2,1,0:T(8,128)(2,1)S(1)}, bf16[4,192,2432]{2,1,0:T(8,128)(2,1)S(1)}) custom-call(f32[192,8,2400]{2,1,0:T(8,128)} %amp_ref), custom_call_target="tpu_custom_call" | custom-call | flops 1000000 | bytes 15000000 | tf_op jit(solution)/shard_map/pallas_call | solution.py:155
  19.5 0.0 collective-permute-done.1
  19.5 1.4 %collective-permute-done.3 = f32[152,256]{1,0:T(8,128)S(1)} collective-permute-done((f32[152,256]{1,0:T(8,128)S(1)}, f32[152,256]{1,0:T(8,128)S(1)}, u32[]{:S(2)}, u32[]{:S(2)}) %collective-permute-start.3) | collective-permute-done | bytes 155680 | tf_op jit(solution)/shard_map/ppermute | solution.py:36
  20.9 0.0 collective-permute-done.2
  21.0 2.1 %collective-permute-start.6 = (f32[152,256]{1,0:T(8,128)S(1)}, f32[152,256]{1,0:T(8,128)S(1)}, u32[]{:S(2)}, u32[]{:S(2)}) collective-permute-start(f32[152,256]{1,0:T(8,128)S(1)} %fusion.1), channel_id=1, source_target_pairs={{0,16},{1,17},{2,18},{3,19},{4,6},{5,7},{6,4},{7,5},{8,24},{9,25},... | collective-permute-start | bytes 466952 | tf_op jit(solution)/shard_map/ppermute | solution.py:36
  23.1 1.0 collective-permute-start.5
  24.1 0.5 collective-permute-start.4
  24.6 2.4 %collective-permute-done.6 = f32[152,256]{1,0:T(8,128)S(1)} collective-permute-done((f32[152,256]{1,0:T(8,128)S(1)}, f32[152,256]{1,0:T(8,128)S(1)}, u32[]{:S(2)}, u32[]{:S(2)}) %collective-permute-start.6) | collective-permute-done | bytes 155680 | tf_op jit(solution)/shard_map/ppermute | solution.py:36
  27.0 1.4 %collective-permute-done.5 = f32[152,256]{1,0:T(8,128)S(1)} collective-permute-done((f32[152,256]{1,0:T(8,128)S(1)}, f32[152,256]{1,0:T(8,128)S(1)}, u32[]{:S(2)}, u32[]{:S(2)}) %collective-permute-start.5) | collective-permute-done | bytes 155680 | tf_op jit(solution)/shard_map/ppermute | solution.py:36
  28.4 1.0 %collective-permute-done.4 = f32[152,256]{1,0:T(8,128)S(1)} collective-permute-done((f32[152,256]{1,0:T(8,128)S(1)}, f32[152,256]{1,0:T(8,128)S(1)}, u32[]{:S(2)}, u32[]{:S(2)}) %collective-permute-start.4) | collective-permute-done | bytes 155680 | tf_op jit(solution)/shard_map/ppermute | solution.py:36
  29.4 2.8 %collective-permute-done.7.amp_ref = f32[192,8,2400]{2,1,0:T(8,128)} collective-permute-done((f32[192,8,2400]{2,1,0:T(8,128)}, f32[192,8,2400]{2,1,0:T(8,128)}, u32[]{:S(2)}, u32[]{:S(2)}) %collective-permute-start.7) | collective-permute-done | bytes 14745632 | tf_op jit(solution)/shard_map/ppermute | solution.py:36
  32.3 1.5 %collective-permute-start.8 = (f32[304,256]{1,0:T(8,128)S(1)}, f32[304,256]{1,0:T(8,128)S(1)}, u32[]{:S(2)}, u32[]{:S(2)}) collective-permute-start(f32[304,256]{1,0:T(8,128)S(1)} %get-tuple-element.76), channel_id=1, source_target_pairs={{0,32},{1,33},{2,34},{3,35},{4,12},{5,13},{6,14},{7,15},{8,40},{9,... | collective-permute-start | bytes 933896 | tf_op jit(solution)/shard_map/ppermute | solution.py:36
  33.8 1.4 %collective-permute-start.9 = (f32[304,256]{1,0:T(8,128)S(1)}, f32[304,256]{1,0:T(8,128)S(1)}, u32[]{:S(2)}, u32[]{:S(2)}) collective-permute-start(f32[304,256]{1,0:T(8,128)S(1)} %get-tuple-element.72), channel_id=1, source_target_pairs={{0,32},{1,33},{2,34},{3,35},{4,12},{5,13},{6,14},{7,15},{8,40},{9,... | collective-permute-start | bytes 933896 | tf_op jit(solution)/shard_map/ppermute | solution.py:36
  35.2 1.4 %collective-permute-start.12 = (f32[304,256]{1,0:T(8,128)S(1)}, f32[304,256]{1,0:T(8,128)S(1)}, u32[]{:S(2)}, u32[]{:S(2)}) collective-permute-start(f32[304,256]{1,0:T(8,128)S(1)} %get-tuple-element.72), channel_id=1, source_target_pairs={{0,96},{1,97},{2,98},{3,99},{4,28},{5,29},{6,30},{7,31},{8,104},{9... | collective-permute-start | bytes 933896 | tf_op jit(solution)/shard_map/ppermute | solution.py:36
  36.5 0.3 collective-permute-start.14
  36.9 2.9 %collective-permute-done.8 = f32[304,256]{1,0:T(8,128)S(1)} collective-permute-done((f32[304,256]{1,0:T(8,128)S(1)}, f32[304,256]{1,0:T(8,128)S(1)}, u32[]{:S(2)}, u32[]{:S(2)}) %collective-permute-start.8) | collective-permute-done | bytes 311328 | tf_op jit(solution)/shard_map/ppermute | solution.py:36
  39.8 3.3 %collective-permute-done.9 = f32[304,256]{1,0:T(8,128)S(1)} collective-permute-done((f32[304,256]{1,0:T(8,128)S(1)}, f32[304,256]{1,0:T(8,128)S(1)}, u32[]{:S(2)}, u32[]{:S(2)}) %collective-permute-start.9) | collective-permute-done | bytes 311328 | tf_op jit(solution)/shard_map/ppermute | solution.py:36
  43.1 1.4 %collective-permute-start.10 = (f32[1216,256]{1,0:T(8,128)S(1)}, f32[1216,256]{1,0:T(8,128)S(1)}, u32[]{:S(2)}, u32[]{:S(2)}) collective-permute-start(f32[1216,256]{1,0:T(8,128)S(1)} %constant_dynamic-update-slice_fusion.4), channel_id=1, source_target_pairs={{0,1},{1,2},{2,3},{3,0},{4,36},{5,37},{6,38},{7,39},{8,9},{9,10},{... | collective-permute-start | bytes 3735560 | tf_op jit(solution)/shard_map/ppermute | solution.py:36
  44.5 0.0 collective-permute-done.12
  44.5 1.8 %collective-permute-start.13 = (f32[304,256]{1,0:T(8,128)S(1)}, f32[304,256]{1,0:T(8,128)S(1)}, u32[]{:S(2)}, u32[]{:S(2)}) collective-permute-start(f32[304,256]{1,0:T(8,128)S(1)} %collective-permute-done.12), channel_id=1, source_target_pairs={{0,96},{1,97},{2,98},{3,99},{4,28},{5,29},{6,30},{7,31},{8,104},{9... | collective-permute-start | bytes 933896 | tf_op jit(solution)/shard_map/ppermute | solution.py:36
  46.3 0.0 collective-permute-start.11
  46.3 2.2 %collective-permute-start.17 = (f32[1216,256]{1,0:T(8,128)S(1)}, f32[1216,256]{1,0:T(8,128)S(1)}, u32[]{:S(2)}, u32[]{:S(2)}) collective-permute-start(f32[1216,256]{1,0:T(8,128)S(1)} %constant_dynamic-update-slice_fusion.4), channel_id=1, source_target_pairs={{0,3},{1,0},{2,1},{3,2},{4,100},{5,101},{6,102},{7,103},{8,11},{9,... | collective-permute-start | bytes 3735560 | tf_op jit(solution)/shard_map/ppermute | solution.py:36
  48.5 0.0 collective-permute-done.14
  48.6 2.0 %collective-permute-done.13 = f32[304,256]{1,0:T(8,128)S(1)} collective-permute-done((f32[304,256]{1,0:T(8,128)S(1)}, f32[304,256]{1,0:T(8,128)S(1)}, u32[]{:S(2)}, u32[]{:S(2)}) %collective-permute-start.13) | collective-permute-done | bytes 311328 | tf_op jit(solution)/shard_map/ppermute | solution.py:36
  50.6 3.0 %collective-permute-done.11 = f32[304,256]{1,0:T(8,128)S(1)} collective-permute-done((f32[304,256]{1,0:T(8,128)S(1)}, f32[304,256]{1,0:T(8,128)S(1)}, u32[]{:S(2)}, u32[]{:S(2)}) %collective-permute-start.11) | collective-permute-done | bytes 311328 | tf_op jit(solution)/shard_map/ppermute | solution.py:36
  53.6 1.7 %collective-permute-start.18 = (f32[1216,256]{1,0:T(8,128)S(1)}, f32[1216,256]{1,0:T(8,128)S(1)}, u32[]{:S(2)}, u32[]{:S(2)}) collective-permute-start(f32[1216,256]{1,0:T(8,128)S(1)} %constant_dynamic-update-slice_fusion.10), channel_id=1, source_target_pairs={{0,1},{1,2},{2,3},{3,0},{4,36},{5,37},{6,38},{7,39},{8,9},{9,10},{... | collective-permute-start | bytes 3735560 | tf_op jit(solution)/shard_map/ppermute | solution.py:36
  55.4 1.1 %collective-permute-start.15 = (f32[608,256]{1,0:T(8,128)S(1)}, f32[608,256]{1,0:T(8,128)S(1)}, u32[]{:S(2)}, u32[]{:S(2)}) collective-permute-start(f32[608,256]{1,0:T(8,128)S(1)} %pad_maximum_fusion), channel_id=1, source_target_pairs={{0,3},{1,0},{2,1},{3,2},{4,100},{5,101},{6,102},{7,103},{8,11},{9,... | collective-permute-start | bytes 1867784 | tf_op jit(solution)/shard_map/ppermute | solution.py:36
  56.5 1.1 %collective-permute-start.16 = (f32[608,256]{1,0:T(8,128)S(1)}, f32[608,256]{1,0:T(8,128)S(1)}, u32[]{:S(2)}, u32[]{:S(2)}) collective-permute-start(f32[608,256]{1,0:T(8,128)S(1)} %pad_maximum_fusion.1), channel_id=1, source_target_pairs={{0,3},{1,0},{2,1},{3,2},{4,100},{5,101},{6,102},{7,103},{8,11},{9,... | collective-permute-start | bytes 1867784 | tf_op jit(solution)/shard_map/ppermute | solution.py:36
  57.6 4.8 %shard_map.39 = (bf16[4,192,2432]{2,1,0:T(8,128)(2,1)S(1)}, bf16[4,192,2432]{2,1,0:T(8,128)(2,1)S(1)}) custom-call(f32[192,8,2400]{2,1,0:T(8,128)} %collective-permute-done.7.amp_ref), custom_call_target="tpu_custom_call" | custom-call | flops 1000000 | bytes 15000000 | tf_op jit(solution)/shard_map/pallas_call | solution.py:155
  62.3 0.0 copy-start
  62.3 1.8 %copy-done = bf16[4,192,2432]{2,1,0:T(8,128)(2,1)} copy-done((bf16[4,192,2432]{2,1,0:T(8,128)(2,1)}, bf16[4,192,2432]{2,1,0:T(8,128)(2,1)S(1)}, u32[]{:S(2)}) %copy-start) | copy-done | bytes 3735576
  64.1 0.7 collective-permute-done.10
  64.9 0.0 collective-permute-start.19
  64.9 7.6 %collective-permute-done.15 = f32[608,256]{1,0:T(8,128)S(1)} collective-permute-done((f32[608,256]{1,0:T(8,128)S(1)}, f32[608,256]{1,0:T(8,128)S(1)}, u32[]{:S(2)}, u32[]{:S(2)}) %collective-permute-start.15) | collective-permute-done | bytes 622624 | tf_op jit(solution)/shard_map/ppermute | solution.py:36
  72.5 3.2 %collective-permute-start.21 = (f32[608,256]{1,0:T(8,128)S(1)}, f32[608,256]{1,0:T(8,128)S(1)}, u32[]{:S(2)}, u32[]{:S(2)}) collective-permute-start(f32[608,256]{1,0:T(8,128)S(1)} %collective-permute-done.15), channel_id=1, source_target_pairs={{0,3},{1,0},{2,1},{3,2},{4,100},{5,101},{6,102},{7,103},{8,11},{9,... | collective-permute-start | bytes 1867784 | tf_op jit(solution)/shard_map/ppermute | solution.py:36
  75.8 3.4 %collective-permute-done.16 = f32[608,256]{1,0:T(8,128)S(1)} collective-permute-done((f32[608,256]{1,0:T(8,128)S(1)}, f32[608,256]{1,0:T(8,128)S(1)}, u32[]{:S(2)}, u32[]{:S(2)}) %collective-permute-start.16) | collective-permute-done | bytes 622624 | tf_op jit(solution)/shard_map/ppermute | solution.py:36
  79.2 0.0 collective-permute-done.17
  79.2 0.0 collective-permute-done.18
  79.2 3.3 %collective-permute-start.20 = (f32[608,256]{1,0:T(8,128)S(1)}, f32[608,256]{1,0:T(8,128)S(1)}, u32[]{:S(2)}, u32[]{:S(2)}) collective-permute-start(f32[608,256]{1,0:T(8,128)S(1)} %collective-permute-done.16), channel_id=1, source_target_pairs={{0,3},{1,0},{2,1},{3,2},{4,100},{5,101},{6,102},{7,103},{8,11},{9,... | collective-permute-start | bytes 1867784 | tf_op jit(solution)/shard_map/ppermute | solution.py:36
  82.5 11.2 %shard_map.40 = (f32[384,256]{1,0:T(8,128)S(1)}, bf16[384,3072]{1,0:T(8,128)(2,1)S(1)}, bf16[384,3072]{1,0:T(8,128)(2,1)S(1)}) custom-call(bf16[4,192,2432]{2,1,0:T(8,128)(2,1)S(1)} %get-tuple-element.43.own_high, bf16[4,192,2432]{2,1,0:T(8,128)(2,1)S(1)} %get-tuple-element.44.own_low, bf16[4,192,2432]{2,1,0:T(8,128)(2,1)S(1)} %get-tuple-element.54.other_high, ...), custom_call_target="tpu_custom_call" | custom-call | flops 6000000000 | bytes 25000000 | tf_op jit(solution)/shard_map/pallas_call | solution.py:231
  93.7 0.0 collective-permute-done.21
  93.7 0.0 collective-permute-done.20
  93.7 0.0 collective-permute-done.19
  93.7 3.5 %shard_map.41 = (f32[192,256]{1,0:T(8,128)S(1)}, f32[192,256]{1,0:T(8,128)S(1)}) custom-call(bf16[384,3072]{1,0:T(8,128)(2,1)S(1)} %get-tuple-element.64.high_ref, bf16[384,3072]{1,0:T(8,128)(2,1)S(1)} %get-tuple-element.65.low_ref, f32[8,152,256]{2,1,0:T(8,128)S(1)} %bitcast.25, f32[4,152,256]{2,1,0:T(8,128)S(1)} %bitcast.32, f32[4,152,256]{2,1,0:T(8,128)S(1)} %bitcast.31, ...), custom_call_target="tpu_custom_call" | custom-call | flops 2000000000 | bytes 8000000 | tf_op jit(solution)/shard_map/pallas_call | solution.py:279
  97.2 0.1 collective-permute-start.22
  97.3 1.4 %collective-permute-done.22 = f32[192,256]{1,0:T(8,128)S(1)} collective-permute-done((f32[192,256]{1,0:T(8,128)S(1)}, f32[192,256]{1,0:T(8,128)S(1)}, u32[]{:S(2)}, u32[]{:S(2)}) %collective-permute-start.22) | collective-permute-done | bytes 196640 | tf_op jit(solution)/shard_map/ppermute | solution.py:36
  98.7 0.7 add.19
  (14 shorter events, 0.4 us)
Async XLA Ops:
  0.0 1.1 %copy-start.1 = (bf16[2400,128]{1,0:T(8,128)(2,1)S(1)}, bf16[2400,128]{1,0:T(8,128)(2,1)}, u32[]{:S(2)}) copy-start(bf16[2400,128]{1,0:T(8,128)(2,1)} %ac_ref.1) | copy-start | bytes 1843204
  6.0 3.2 %collective-permute-start = (f32[4,152,256]{2,1,0:T(8,128)S(1)}, f32[4,152,256]{2,1,0:T(8,128)S(1)}, u32[]{:S(2)}, u32[]{:S(2)}) collective-permute-start(f32[4,152,256]{2,1,0:T(8,128)S(1)} %get-tuple-element.38), channel_id=1, source_target_pairs={{0,4},{1,5},{2,6},{3,7},{4,0},{5,1},{6,2},{7,3},{8,12},{9,13},{10,... | collective-permute-start | bytes 1867784 | tf_op jit(solution)/shard_map/ppermute | solution.py:36
  9.3 23.0 %collective-permute-start.7 = (f32[192,8,2400]{2,1,0:T(8,128)}, f32[192,8,2400]{2,1,0:T(8,128)}, u32[]{:S(2)}, u32[]{:S(2)}) collective-permute-start(f32[192,8,2400]{2,1,0:T(8,128)} %amp_ref), channel_id=1, source_target_pairs={{0,4},{1,5},{2,6},{3,7},{4,0},{5,1},{6,2},{7,3},{8,12},{9,13},{10,... | collective-permute-start | bytes 44236808 | tf_op jit(solution)/shard_map/ppermute | solution.py:36
  9.8 9.7 %collective-permute-start.1 = (f32[152,256]{1,0:T(8,128)S(1)}, f32[152,256]{1,0:T(8,128)S(1)}, u32[]{:S(2)}, u32[]{:S(2)}) collective-permute-start(f32[152,256]{1,0:T(8,128)S(1)} %get-tuple-element.69), channel_id=1, source_target_pairs={{0,1},{1,2},{2,3},{3,0},{4,5},{5,6},{6,7},{7,4},{8,9},{9,10},{10,1... | collective-permute-start | bytes 466952 | tf_op jit(solution)/shard_map/ppermute | solution.py:36
  11.1 9.8 %collective-permute-start.3 = (f32[152,256]{1,0:T(8,128)S(1)}, f32[152,256]{1,0:T(8,128)S(1)}, u32[]{:S(2)}, u32[]{:S(2)}) collective-permute-start(f32[152,256]{1,0:T(8,128)S(1)} %get-tuple-element.70), channel_id=1, source_target_pairs={{0,2},{1,3},{2,0},{3,1},{4,6},{5,7},{6,4},{7,5},{8,10},{9,11},{10,... | collective-permute-start | bytes 466952 | tf_op jit(solution)/shard_map/ppermute | solution.py:36
  13.6 7.4 %collective-permute-start.2 = (f32[152,256]{1,0:T(8,128)S(1)}, f32[152,256]{1,0:T(8,128)S(1)}, u32[]{:S(2)}, u32[]{:S(2)}) collective-permute-start(f32[152,256]{1,0:T(8,128)S(1)} %get-tuple-element.71), channel_id=1, source_target_pairs={{0,3},{1,0},{2,1},{3,2},{4,7},{5,4},{6,5},{7,6},{8,11},{9,8},{10,9... | collective-permute-start | bytes 466952 | tf_op jit(solution)/shard_map/ppermute | solution.py:36
  21.0 6.0 %collective-permute-start.6 = (f32[152,256]{1,0:T(8,128)S(1)}, f32[152,256]{1,0:T(8,128)S(1)}, u32[]{:S(2)}, u32[]{:S(2)}) collective-permute-start(f32[152,256]{1,0:T(8,128)S(1)} %fusion.1), channel_id=1, source_target_pairs={{0,16},{1,17},{2,18},{3,19},{4,6},{5,7},{6,4},{7,5},{8,24},{9,25},... | collective-permute-start | bytes 466952 | tf_op jit(solution)/shard_map/ppermute | solution.py:36
  23.1 5.2 %collective-permute-start.5 = (f32[152,256]{1,0:T(8,128)S(1)}, f32[152,256]{1,0:T(8,128)S(1)}, u32[]{:S(2)}, u32[]{:S(2)}) collective-permute-start(f32[152,256]{1,0:T(8,128)S(1)} %fusion.1), channel_id=1, source_target_pairs={{0,24},{1,25},{2,26},{3,27},{4,7},{5,4},{6,5},{7,6},{8,0},{9,1},{1... | collective-permute-start | bytes 466952 | tf_op jit(solution)/shard_map/ppermute | solution.py:36
  24.1 5.3 %collective-permute-start.4 = (f32[152,256]{1,0:T(8,128)S(1)}, f32[152,256]{1,0:T(8,128)S(1)}, u32[]{:S(2)}, u32[]{:S(2)}) collective-permute-start(f32[152,256]{1,0:T(8,128)S(1)} %fusion.1), channel_id=1, source_target_pairs={{0,8},{1,9},{2,10},{3,11},{4,5},{5,6},{6,7},{7,4},{8,16},{9,17},{1... | collective-permute-start | bytes 466952 | tf_op jit(solution)/shard_map/ppermute | solution.py:36
  32.3 7.5 %collective-permute-start.8 = (f32[304,256]{1,0:T(8,128)S(1)}, f32[304,256]{1,0:T(8,128)S(1)}, u32[]{:S(2)}, u32[]{:S(2)}) collective-permute-start(f32[304,256]{1,0:T(8,128)S(1)} %get-tuple-element.76), channel_id=1, source_target_pairs={{0,32},{1,33},{2,34},{3,35},{4,12},{5,13},{6,14},{7,15},{8,40},{9,... | collective-permute-start | bytes 933896 | tf_op jit(solution)/shard_map/ppermute | solution.py:36
  33.8 9.3 %collective-permute-start.9 = (f32[304,256]{1,0:T(8,128)S(1)}, f32[304,256]{1,0:T(8,128)S(1)}, u32[]{:S(2)}, u32[]{:S(2)}) collective-permute-start(f32[304,256]{1,0:T(8,128)S(1)} %get-tuple-element.72), channel_id=1, source_target_pairs={{0,32},{1,33},{2,34},{3,35},{4,12},{5,13},{6,14},{7,15},{8,40},{9,... | collective-permute-start | bytes 933896 | tf_op jit(solution)/shard_map/ppermute | solution.py:36
  35.2 9.4 %collective-permute-start.12 = (f32[304,256]{1,0:T(8,128)S(1)}, f32[304,256]{1,0:T(8,128)S(1)}, u32[]{:S(2)}, u32[]{:S(2)}) collective-permute-start(f32[304,256]{1,0:T(8,128)S(1)} %get-tuple-element.72), channel_id=1, source_target_pairs={{0,96},{1,97},{2,98},{3,99},{4,28},{5,29},{6,30},{7,31},{8,104},{9... | collective-permute-start | bytes 933896 | tf_op jit(solution)/shard_map/ppermute | solution.py:36
  36.5 12.0 %collective-permute-start.14 = (f32[304,256]{1,0:T(8,128)S(1)}, f32[304,256]{1,0:T(8,128)S(1)}, u32[]{:S(2)}, u32[]{:S(2)}) collective-permute-start(f32[304,256]{1,0:T(8,128)S(1)} %get-tuple-element.76), channel_id=1, source_target_pairs={{0,96},{1,97},{2,98},{3,99},{4,28},{5,29},{6,30},{7,31},{8,104},{9... | collective-permute-start | bytes 933896 | tf_op jit(solution)/shard_map/ppermute | solution.py:36
  43.1 21.8 %collective-permute-start.10 = (f32[1216,256]{1,0:T(8,128)S(1)}, f32[1216,256]{1,0:T(8,128)S(1)}, u32[]{:S(2)}, u32[]{:S(2)}) collective-permute-start(f32[1216,256]{1,0:T(8,128)S(1)} %constant_dynamic-update-slice_fusion.4), channel_id=1, source_target_pairs={{0,1},{1,2},{2,3},{3,0},{4,36},{5,37},{6,38},{7,39},{8,9},{9,10},{... | collective-permute-start | bytes 3735560 | tf_op jit(solution)/shard_map/ppermute | solution.py:36
  44.5 6.0 %collective-permute-start.13 = (f32[304,256]{1,0:T(8,128)S(1)}, f32[304,256]{1,0:T(8,128)S(1)}, u32[]{:S(2)}, u32[]{:S(2)}) collective-permute-start(f32[304,256]{1,0:T(8,128)S(1)} %collective-permute-done.12), channel_id=1, source_target_pairs={{0,96},{1,97},{2,98},{3,99},{4,28},{5,29},{6,30},{7,31},{8,104},{9... | collective-permute-start | bytes 933896 | tf_op jit(solution)/shard_map/ppermute | solution.py:36
  46.3 7.3 %collective-permute-start.11 = (f32[304,256]{1,0:T(8,128)S(1)}, f32[304,256]{1,0:T(8,128)S(1)}, u32[]{:S(2)}, u32[]{:S(2)}) collective-permute-start(f32[304,256]{1,0:T(8,128)S(1)} %collective-permute-done.8), channel_id=1, source_target_pairs={{0,32},{1,33},{2,34},{3,35},{4,12},{5,13},{6,14},{7,15},{8,40},{9,... | collective-permute-start | bytes 933896 | tf_op jit(solution)/shard_map/ppermute | solution.py:36
  46.3 32.9 %collective-permute-start.17 = (f32[1216,256]{1,0:T(8,128)S(1)}, f32[1216,256]{1,0:T(8,128)S(1)}, u32[]{:S(2)}, u32[]{:S(2)}) collective-permute-start(f32[1216,256]{1,0:T(8,128)S(1)} %constant_dynamic-update-slice_fusion.4), channel_id=1, source_target_pairs={{0,3},{1,0},{2,1},{3,2},{4,100},{5,101},{6,102},{7,103},{8,11},{9,... | collective-permute-start | bytes 3735560 | tf_op jit(solution)/shard_map/ppermute | solution.py:36
  53.6 25.6 %collective-permute-start.18 = (f32[1216,256]{1,0:T(8,128)S(1)}, f32[1216,256]{1,0:T(8,128)S(1)}, u32[]{:S(2)}, u32[]{:S(2)}) collective-permute-start(f32[1216,256]{1,0:T(8,128)S(1)} %constant_dynamic-update-slice_fusion.10), channel_id=1, source_target_pairs={{0,1},{1,2},{2,3},{3,0},{4,36},{5,37},{6,38},{7,39},{8,9},{9,10},{... | collective-permute-start | bytes 3735560 | tf_op jit(solution)/shard_map/ppermute | solution.py:36
  55.4 17.2 %collective-permute-start.15 = (f32[608,256]{1,0:T(8,128)S(1)}, f32[608,256]{1,0:T(8,128)S(1)}, u32[]{:S(2)}, u32[]{:S(2)}) collective-permute-start(f32[608,256]{1,0:T(8,128)S(1)} %pad_maximum_fusion), channel_id=1, source_target_pairs={{0,3},{1,0},{2,1},{3,2},{4,100},{5,101},{6,102},{7,103},{8,11},{9,... | collective-permute-start | bytes 1867784 | tf_op jit(solution)/shard_map/ppermute | solution.py:36
  56.5 22.7 %collective-permute-start.16 = (f32[608,256]{1,0:T(8,128)S(1)}, f32[608,256]{1,0:T(8,128)S(1)}, u32[]{:S(2)}, u32[]{:S(2)}) collective-permute-start(f32[608,256]{1,0:T(8,128)S(1)} %pad_maximum_fusion.1), channel_id=1, source_target_pairs={{0,3},{1,0},{2,1},{3,2},{4,100},{5,101},{6,102},{7,103},{8,11},{9,... | collective-permute-start | bytes 1867784 | tf_op jit(solution)/shard_map/ppermute | solution.py:36
  62.3 1.8 %copy-start = (bf16[4,192,2432]{2,1,0:T(8,128)(2,1)}, bf16[4,192,2432]{2,1,0:T(8,128)(2,1)S(1)}, u32[]{:S(2)}) copy-start(bf16[4,192,2432]{2,1,0:T(8,128)(2,1)S(1)} %get-tuple-element.55.other_low) | copy-start | bytes 11206660
  64.9 28.8 %collective-permute-start.19 = (f32[1216,256]{1,0:T(8,128)S(1)}, f32[1216,256]{1,0:T(8,128)S(1)}, u32[]{:S(2)}, u32[]{:S(2)}) collective-permute-start(f32[1216,256]{1,0:T(8,128)S(1)} %collective-permute-done.10), channel_id=1, source_target_pairs={{0,1},{1,2},{2,3},{3,0},{4,36},{5,37},{6,38},{7,39},{8,9},{9,10},{... | collective-permute-start | bytes 3735560 | tf_op jit(solution)/shard_map/ppermute | solution.py:36
  72.5 21.2 %collective-permute-start.21 = (f32[608,256]{1,0:T(8,128)S(1)}, f32[608,256]{1,0:T(8,128)S(1)}, u32[]{:S(2)}, u32[]{:S(2)}) collective-permute-start(f32[608,256]{1,0:T(8,128)S(1)} %collective-permute-done.15), channel_id=1, source_target_pairs={{0,3},{1,0},{2,1},{3,2},{4,100},{5,101},{6,102},{7,103},{8,11},{9,... | collective-permute-start | bytes 1867784 | tf_op jit(solution)/shard_map/ppermute | solution.py:36
  79.2 14.5 %collective-permute-start.20 = (f32[608,256]{1,0:T(8,128)S(1)}, f32[608,256]{1,0:T(8,128)S(1)}, u32[]{:S(2)}, u32[]{:S(2)}) collective-permute-start(f32[608,256]{1,0:T(8,128)S(1)} %collective-permute-done.16), channel_id=1, source_target_pairs={{0,3},{1,0},{2,1},{3,2},{4,100},{5,101},{6,102},{7,103},{8,11},{9,... | collective-permute-start | bytes 1867784 | tf_op jit(solution)/shard_map/ppermute | solution.py:36
  97.2 1.5 %collective-permute-start.22 = (f32[192,256]{1,0:T(8,128)S(1)}, f32[192,256]{1,0:T(8,128)S(1)}, u32[]{:S(2)}, u32[]{:S(2)}) collective-permute-start(f32[192,256]{1,0:T(8,128)S(1)} %get-tuple-element.68), channel_id=1, source_target_pairs={{0,4},{1,5},{2,6},{3,7},{4,0},{5,1},{6,2},{7,3},{8,12},{9,13},{10,... | collective-permute-start | bytes 589832 | tf_op jit(solution)/shard_map/ppermute | solution.py:36

commit v5 on v4

--- a/solution.py
+++ b/solution.py
@@ -59,15 +59,13 @@
         for k in range(4):
             shifted[k, pl.ds((rows * k) % 128, rows), :] = ordered.astype(jnp.bfloat16)
 
-    height = first_ref.shape[0]
     for k in range(4):
         offset = (rows * k) % 128
         start = rows * k - offset
         length = -(-(offset + rows) // 128) * 128
-        both = jnp.concatenate([ref[:, start:start + length] for ref in (first_ref, second_ref)], axis=0)
-        both = jnp.dot(both, shifted[k, :length, :], preferred_element_type=jnp.float32)
-        products[8 * group + k] = both[:count_d]
-        products[8 * group + 4 + k] = both[height:height + count_d]
+        for j, bd_ref in enumerate((first_ref, second_ref)):
+            products[8 * group + 4 * j + k] = jnp.dot(bd_ref[:, start:start + length], shifted[k, :length, :],
+                                                      preferred_element_type=jnp.float32)
 
     @pl.when(group == pl.num_programs(0) - 1)
     def _():
@@ -95,15 +93,14 @@
 
 def partial_integrals(bd, ac):
     rows = ac.shape[0]
-    height = -(-bd.shape[0] // 16) * 16
     out = jax.ShapeDtypeStruct((SIDE, FRAME, 256), jnp.float32)
     whole = pl.BlockSpec(memory_space=pltpu.VMEM)
     return pl.pallas_call(
         partial_kernel,
         grid=(2,),
         out_shape=(out, out),
-        in_specs=[pl.BlockSpec((height, 4 * rows), lambda g: (0, 2 * g)),
-                  pl.BlockSpec((height, 4 * rows), lambda g: (0, 2 * g + 1)),
+        in_specs=[pl.BlockSpec((bd.shape[0], 4 * rows), lambda g: (0, 2 * g)),
+                  pl.BlockSpec((bd.shape[0], 4 * rows), lambda g: (0, 2 * g + 1)),
                   pl.BlockSpec(ac.shape, lambda g: (0, 0))],
         out_specs=(whole, whole),
         scratch_shapes=[pltpu.VMEM((4, -(-(rows + 96) // 128) * 128, 128), jnp.bfloat16),

time: 99.7 us -> 99.9 us (level)
  no operation moved by 1% of the time
where the time goes in v5:
time: 99.9 us; the launch traced here: 99.6 us
  waiting for transfers between devices  35.2 us (35%)
  starting transfers between devices  30.9 us (31%)
  Pallas kernels  29.3 us (29%)
  local copies, waits for them, and re-layouts  3.12 us (3%)
    ppermute x23, waiting for transfers between devices, permute(): return lax.ppermute(value, AXES, pairs)  35.2 us
    ppermute x23, starting transfers between devices, permute(): return lax.ppermute(value, AXES, pairs)  30.9 us
    pallas_call x1, Pallas kernels, early_ladder(): pl.pallas_call(early_kernel, grid=(SIDE,), in_specs=[amp_spec] * 4 + [pl....  11.2 us
    pallas_call x2, Pallas kernels, arrange(): pl.pallas_call(arrange_kernel, grid=(pairs // rows,), out_shape=(out, out...  9.51 us
    pallas_call x1, Pallas kernels, partial_integrals(): pl.pallas_call(partial_kernel, grid=(2,), out_shape=(out, out), in_specs=...  5.11 us
    pallas_call x1, Pallas kernels, late_ladder(): pl.pallas_call(late_kernel, in_specs=[whole] * (3 + len(pieces)), out_spe...  3.5 us
    unnamed x10, local copies, waits for them, and re-layouts  3 us
  transfers between devices with their start and end apart: 23, of which 14 were waited for; matrix products, arithmetic and copies ran while one was open for 0% of the time, Pallas kernels for 21%

profile of v5, /device:TPU:1, one launch (start us, length us, event | category | flops | bytes accessed | tf_op | source)
XLA Modules:
  0.0 99.6 jit_solution(4947708734785345873)
XLA Ops:
  0.0 0.0 copy-start.1
  0.0 1.1 %copy-done.1 = bf16[2400,128]{1,0:T(8,128)(2,1)S(1)} copy-done((bf16[2400,128]{1,0:T(8,128)(2,1)S(1)}, bf16[2400,128]{1,0:T(8,128)(2,1)}, u32[]{:S(2)}) %copy-start.1) | copy-done | bytes 614424
  1.1 5.1 %shard_map.37 = (f32[4,152,256]{2,1,0:T(8,128)S(1)}, f32[4,152,256]{2,1,0:T(8,128)S(1)}) custom-call(bf16[75,38400]{1,0:T(8,128)(2,1)} %bitcast.33, bf16[75,38400]{1,0:T(8,128)(2,1)} %bitcast.34, bf16[2400,128]{1,0:T(8,128)(2,1)S(1)} %copy-done.1), custom_call_target="tpu_custom_call" | custom-call | flops 1000000000 | bytes 8000000 | tf_op jit(solution)/shard_map/pallas_call | solution.py:98
  6.2 1.5 %collective-permute-start = (f32[4,152,256]{2,1,0:T(8,128)S(1)}, f32[4,152,256]{2,1,0:T(8,128)S(1)}, u32[]{:S(2)}, u32[]{:S(2)}) collective-permute-start(f32[4,152,256]{2,1,0:T(8,128)S(1)} %get-tuple-element.38), channel_id=1, source_target_pairs={{0,4},{1,5},{2,6},{3,7},{4,0},{5,1},{6,2},{7,3},{8,12},{9,13},{10,... | collective-permute-start | bytes 1867784 | tf_op jit(solution)/shard_map/ppermute | solution.py:36
  7.7 1.7 %collective-permute-done = f32[4,152,256]{2,1,0:T(8,128)S(1)} collective-permute-done((f32[4,152,256]{2,1,0:T(8,128)S(1)}, f32[4,152,256]{2,1,0:T(8,128)S(1)}, u32[]{:S(2)}, u32[]{:S(2)}) %collective-permute-start) | collective-permute-done | bytes 622624 | tf_op jit(solution)/shard_map/ppermute | solution.py:36
  9.4 0.1 add.15
  9.5 0.5 collective-permute-start.7
  9.9 1.4 %collective-permute-start.1 = (f32[152,256]{1,0:T(8,128)S(1)}, f32[152,256]{1,0:T(8,128)S(1)}, u32[]{:S(2)}, u32[]{:S(2)}) collective-permute-start(f32[152,256]{1,0:T(8,128)S(1)} %get-tuple-element.69), channel_id=1, source_target_pairs={{0,1},{1,2},{2,3},{3,0},{4,5},{5,6},{6,7},{7,4},{8,9},{9,10},{10,1... | collective-permute-start | bytes 466952 | tf_op jit(solution)/shard_map/ppermute | solution.py:36
  11.3 2.5 %collective-permute-start.3 = (f32[152,256]{1,0:T(8,128)S(1)}, f32[152,256]{1,0:T(8,128)S(1)}, u32[]{:S(2)}, u32[]{:S(2)}) collective-permute-start(f32[152,256]{1,0:T(8,128)S(1)} %get-tuple-element.70), channel_id=1, source_target_pairs={{0,2},{1,3},{2,0},{3,1},{4,6},{5,7},{6,4},{7,5},{8,10},{9,11},{10,... | collective-permute-start | bytes 466952 | tf_op jit(solution)/shard_map/ppermute | solution.py:36
  13.8 1.1 %collective-permute-start.2 = (f32[152,256]{1,0:T(8,128)S(1)}, f32[152,256]{1,0:T(8,128)S(1)}, u32[]{:S(2)}, u32[]{:S(2)}) collective-permute-start(f32[152,256]{1,0:T(8,128)S(1)} %get-tuple-element.71), channel_id=1, source_target_pairs={{0,3},{1,0},{2,1},{3,2},{4,7},{5,4},{6,5},{7,6},{8,11},{9,8},{10,9... | collective-permute-start | bytes 466952 | tf_op jit(solution)/shard_map/ppermute | solution.py:36
  14.9 4.8 %shard_map.38 = (bf16[4,192,2432]{2,1,0:T(8,128)(2,1)S(1)}, bf16[4,192,2432]{2,1,0:T(8,128)(2,1)S(1)}) custom-call(f32[192,8,2400]{2,1,0:T(8,128)} %amp_ref), custom_call_target="tpu_custom_call" | custom-call | flops 1000000 | bytes 15000000 | tf_op jit(solution)/shard_map/pallas_call | solution.py:152
  19.7 0.0 collective-permute-done.1
  19.7 1.4 %collective-permute-done.3 = f32[152,256]{1,0:T(8,128)S(1)} collective-permute-done((f32[152,256]{1,0:T(8,128)S(1)}, f32[152,256]{1,0:T(8,128)S(1)}, u32[]{:S(2)}, u32[]{:S(2)}) %collective-permute-start.3) | collective-permute-done | bytes 155680 | tf_op jit(solution)/shard_map/ppermute | solution.py:36
  21.1 0.0 collective-permute-done.2
  21.2 2.1 %collective-permute-start.6 = (f32[152,256]{1,0:T(8,128)S(1)}, f32[152,256]{1,0:T(8,128)S(1)}, u32[]{:S(2)}, u32[]{:S(2)}) collective-permute-start(f32[152,256]{1,0:T(8,128)S(1)} %fusion.1), channel_id=1, source_target_pairs={{0,16},{1,17},{2,18},{3,19},{4,6},{5,7},{6,4},{7,5},{8,24},{9,25},... | collective-permute-start | bytes 466952 | tf_op jit(solution)/shard_map/ppermute | solution.py:36
  23.3 1.0 %collective-permute-start.5 = (f32[152,256]{1,0:T(8,128)S(1)}, f32[152,256]{1,0:T(8,128)S(1)}, u32[]{:S(2)}, u32[]{:S(2)}) collective-permute-start(f32[152,256]{1,0:T(8,128)S(1)} %fusion.1), channel_id=1, source_target_pairs={{0,24},{1,25},{2,26},{3,27},{4,7},{5,4},{6,5},{7,6},{8,0},{9,1},{1... | collective-permute-start | bytes 466952 | tf_op jit(solution)/shard_map/ppermute | solution.py:36
  24.3 0.5 collective-permute-start.4
  24.8 2.4 %collective-permute-done.6 = f32[152,256]{1,0:T(8,128)S(1)} collective-permute-done((f32[152,256]{1,0:T(8,128)S(1)}, f32[152,256]{1,0:T(8,128)S(1)}, u32[]{:S(2)}, u32[]{:S(2)}) %collective-permute-start.6) | collective-permute-done | bytes 155680 | tf_op jit(solution)/shard_map/ppermute | solution.py:36
  27.1 1.4 %collective-permute-done.5 = f32[152,256]{1,0:T(8,128)S(1)} collective-permute-done((f32[152,256]{1,0:T(8,128)S(1)}, f32[152,256]{1,0:T(8,128)S(1)}, u32[]{:S(2)}, u32[]{:S(2)}) %collective-permute-start.5) | collective-permute-done | bytes 155680 | tf_op jit(solution)/shard_map/ppermute | solution.py:36
  28.5 1.1 %collective-permute-done.4 = f32[152,256]{1,0:T(8,128)S(1)} collective-permute-done((f32[152,256]{1,0:T(8,128)S(1)}, f32[152,256]{1,0:T(8,128)S(1)}, u32[]{:S(2)}, u32[]{:S(2)}) %collective-permute-start.4) | collective-permute-done | bytes 155680 | tf_op jit(solution)/shard_map/ppermute | solution.py:36
  29.6 2.8 %collective-permute-done.7.amp_ref = f32[192,8,2400]{2,1,0:T(8,128)} collective-permute-done((f32[192,8,2400]{2,1,0:T(8,128)}, f32[192,8,2400]{2,1,0:T(8,128)}, u32[]{:S(2)}, u32[]{:S(2)}) %collective-permute-start.7) | collective-permute-done | bytes 14745632 | tf_op jit(solution)/shard_map/ppermute | solution.py:36
  32.5 1.4 %collective-permute-start.8 = (f32[304,256]{1,0:T(8,128)S(1)}, f32[304,256]{1,0:T(8,128)S(1)}, u32[]{:S(2)}, u32[]{:S(2)}) collective-permute-start(f32[304,256]{1,0:T(8,128)S(1)} %get-tuple-element.76), channel_id=1, source_target_pairs={{0,32},{1,33},{2,34},{3,35},{4,12},{5,13},{6,14},{7,15},{8,40},{9,... | collective-permute-start | bytes 933896 | tf_op jit(solution)/shard_map/ppermute | solution.py:36
  34.0 1.4 %collective-permute-start.9 = (f32[304,256]{1,0:T(8,128)S(1)}, f32[304,256]{1,0:T(8,128)S(1)}, u32[]{:S(2)}, u32[]{:S(2)}) collective-permute-start(f32[304,256]{1,0:T(8,128)S(1)} %get-tuple-element.72), channel_id=1, source_target_pairs={{0,32},{1,33},{2,34},{3,35},{4,12},{5,13},{6,14},{7,15},{8,40},{9,... | collective-permute-start | bytes 933896 | tf_op jit(solution)/shard_map/ppermute | solution.py:36
  35.3 1.4 %collective-permute-start.12 = (f32[304,256]{1,0:T(8,128)S(1)}, f32[304,256]{1,0:T(8,128)S(1)}, u32[]{:S(2)}, u32[]{:S(2)}) collective-permute-start(f32[304,256]{1,0:T(8,128)S(1)} %get-tuple-element.72), channel_id=1, source_target_pairs={{0,96},{1,97},{2,98},{3,99},{4,28},{5,29},{6,30},{7,31},{8,104},{9... | collective-permute-start | bytes 933896 | tf_op jit(solution)/shard_map/ppermute | solution.py:36
  36.7 0.3 collective-permute-start.14
  37.0 2.9 %collective-permute-done.8 = f32[304,256]{1,0:T(8,128)S(1)} collective-permute-done((f32[304,256]{1,0:T(8,128)S(1)}, f32[304,256]{1,0:T(8,128)S(1)}, u32[]{:S(2)}, u32[]{:S(2)}) %collective-permute-start.8) | collective-permute-done | bytes 311328 | tf_op jit(solution)/shard_map/ppermute | solution.py:36
  40.0 3.3 %collective-permute-done.9 = f32[304,256]{1,0:T(8,128)S(1)} collective-permute-done((f32[304,256]{1,0:T(8,128)S(1)}, f32[304,256]{1,0:T(8,128)S(1)}, u32[]{:S(2)}, u32[]{:S(2)}) %collective-permute-start.9) | collective-permute-done | bytes 311328 | tf_op jit(solution)/shard_map/ppermute | solution.py:36
  43.3 1.4 %collective-permute-start.10 = (f32[1216,256]{1,0:T(8,128)S(1)}, f32[1216,256]{1,0:T(8,128)S(1)}, u32[]{:S(2)}, u32[]{:S(2)}) collective-permute-start(f32[1216,256]{1,0:T(8,128)S(1)} %constant_dynamic-update-slice_fusion.4), channel_id=1, source_target_pairs={{0,1},{1,2},{2,3},{3,0},{4,36},{5,37},{6,38},{7,39},{8,9},{9,10},{... | collective-permute-start | bytes 3735560 | tf_op jit(solution)/shard_map/ppermute | solution.py:36
  44.7 0.0 collective-permute-done.12
  44.7 1.8 %collective-permute-start.13 = (f32[304,256]{1,0:T(8,128)S(1)}, f32[304,256]{1,0:T(8,128)S(1)}, u32[]{:S(2)}, u32[]{:S(2)}) collective-permute-start(f32[304,256]{1,0:T(8,128)S(1)} %collective-permute-done.12), channel_id=1, source_target_pairs={{0,96},{1,97},{2,98},{3,99},{4,28},{5,29},{6,30},{7,31},{8,104},{9... | collective-permute-start | bytes 933896 | tf_op jit(solution)/shard_map/ppermute | solution.py:36
  46.5 0.0 collective-permute-start.11
  46.5 2.2 %collective-permute-start.17 = (f32[1216,256]{1,0:T(8,128)S(1)}, f32[1216,256]{1,0:T(8,128)S(1)}, u32[]{:S(2)}, u32[]{:S(2)}) collective-permute-start(f32[1216,256]{1,0:T(8,128)S(1)} %constant_dynamic-update-slice_fusion.4), channel_id=1, source_target_pairs={{0,3},{1,0},{2,1},{3,2},{4,100},{5,101},{6,102},{7,103},{8,11},{9,... | collective-permute-start | bytes 3735560 | tf_op jit(solution)/shard_map/ppermute | solution.py:36
  48.7 0.0 collective-permute-done.14
  48.7 2.0 %collective-permute-done.13 = f32[304,256]{1,0:T(8,128)S(1)} collective-permute-done((f32[304,256]{1,0:T(8,128)S(1)}, f32[304,256]{1,0:T(8,128)S(1)}, u32[]{:S(2)}, u32[]{:S(2)}) %collective-permute-start.13) | collective-permute-done | bytes 311328 | tf_op jit(solution)/shard_map/ppermute | solution.py:36
  50.8 3.0 %collective-permute-done.11 = f32[304,256]{1,0:T(8,128)S(1)} collective-permute-done((f32[304,256]{1,0:T(8,128)S(1)}, f32[304,256]{1,0:T(8,128)S(1)}, u32[]{:S(2)}, u32[]{:S(2)}) %collective-permute-start.11) | collective-permute-done | bytes 311328 | tf_op jit(solution)/shard_map/ppermute | solution.py:36
  53.8 1.7 %collective-permute-start.18 = (f32[1216,256]{1,0:T(8,128)S(1)}, f32[1216,256]{1,0:T(8,128)S(1)}, u32[]{:S(2)}, u32[]{:S(2)}) collective-permute-start(f32[1216,256]{1,0:T(8,128)S(1)} %constant_dynamic-update-slice_fusion.10), channel_id=1, source_target_pairs={{0,1},{1,2},{2,3},{3,0},{4,36},{5,37},{6,38},{7,39},{8,9},{9,10},{... | collective-permute-start | bytes 3735560 | tf_op jit(solution)/shard_map/ppermute | solution.py:36
  55.5 1.1 %collective-permute-start.15 = (f32[608,256]{1,0:T(8,128)S(1)}, f32[608,256]{1,0:T(8,128)S(1)}, u32[]{:S(2)}, u32[]{:S(2)}) collective-permute-start(f32[608,256]{1,0:T(8,128)S(1)} %pad_maximum_fusion), channel_id=1, source_target_pairs={{0,3},{1,0},{2,1},{3,2},{4,100},{5,101},{6,102},{7,103},{8,11},{9,... | collective-permute-start | bytes 1867784 | tf_op jit(solution)/shard_map/ppermute | solution.py:36
  56.7 1.1 %collective-permute-start.16 = (f32[608,256]{1,0:T(8,128)S(1)}, f32[608,256]{1,0:T(8,128)S(1)}, u32[]{:S(2)}, u32[]{:S(2)}) collective-permute-start(f32[608,256]{1,0:T(8,128)S(1)} %pad_maximum_fusion.1), channel_id=1, source_target_pairs={{0,3},{1,0},{2,1},{3,2},{4,100},{5,101},{6,102},{7,103},{8,11},{9,... | collective-permute-start | bytes 1867784 | tf_op jit(solution)/shard_map/ppermute | solution.py:36
  57.7 4.8 %shard_map.39 = (bf16[4,192,2432]{2,1,0:T(8,128)(2,1)S(1)}, bf16[4,192,2432]{2,1,0:T(8,128)(2,1)S(1)}) custom-call(f32[192,8,2400]{2,1,0:T(8,128)} %collective-permute-done.7.amp_ref), custom_call_target="tpu_custom_call" | custom-call | flops 1000000 | bytes 15000000 | tf_op jit(solution)/shard_map/pallas_call | solution.py:152
  62.5 0.0 copy-start
  62.5 1.8 %copy-done = bf16[4,192,2432]{2,1,0:T(8,128)(2,1)} copy-done((bf16[4,192,2432]{2,1,0:T(8,128)(2,1)}, bf16[4,192,2432]{2,1,0:T(8,128)(2,1)S(1)}, u32[]{:S(2)}) %copy-start) | copy-done | bytes 3735576
  64.3 0.7 collective-permute-done.10
  65.0 0.0 collective-permute-start.19
  65.1 7.6 %collective-permute-done.15 = f32[608,256]{1,0:T(8,128)S(1)} collective-permute-done((f32[608,256]{1,0:T(8,128)S(1)}, f32[608,256]{1,0:T(8,128)S(1)}, u32[]{:S(2)}, u32[]{:S(2)}) %collective-permute-start.15) | collective-permute-done | bytes 622624 | tf_op jit(solution)/shard_map/ppermute | solution.py:36
  72.7 3.2 %collective-permute-start.21 = (f32[608,256]{1,0:T(8,128)S(1)}, f32[608,256]{1,0:T(8,128)S(1)}, u32[]{:S(2)}, u32[]{:S(2)}) collective-permute-start(f32[608,256]{1,0:T(8,128)S(1)} %collective-permute-done.15), channel_id=1, source_target_pairs={{0,3},{1,0},{2,1},{3,2},{4,100},{5,101},{6,102},{7,103},{8,11},{9,... | collective-permute-start | bytes 1867784 | tf_op jit(solution)/shard_map/ppermute | solution.py:36
  76.0 3.4 %collective-permute-done.16 = f32[608,256]{1,0:T(8,128)S(1)} collective-permute-done((f32[608,256]{1,0:T(8,128)S(1)}, f32[608,256]{1,0:T(8,128)S(1)}, u32[]{:S(2)}, u32[]{:S(2)}) %collective-permute-start.16) | collective-permute-done | bytes 622624 | tf_op jit(solution)/shard_map/ppermute | solution.py:36
  79.4 0.0 collective-permute-done.17
  79.4 0.0 collective-permute-done.18
  79.4 3.3 %collective-permute-start.20 = (f32[608,256]{1,0:T(8,128)S(1)}, f32[608,256]{1,0:T(8,128)S(1)}, u32[]{:S(2)}, u32[]{:S(2)}) collective-permute-start(f32[608,256]{1,0:T(8,128)S(1)} %collective-permute-done.16), channel_id=1, source_target_pairs={{0,3},{1,0},{2,1},{3,2},{4,100},{5,101},{6,102},{7,103},{8,11},{9,... | collective-permute-start | bytes 1867784 | tf_op jit(solution)/shard_map/ppermute | solution.py:36
  82.6 11.2 %shard_map.40 = (f32[384,256]{1,0:T(8,128)S(1)}, bf16[384,3072]{1,0:T(8,128)(2,1)S(1)}, bf16[384,3072]{1,0:T(8,128)(2,1)S(1)}) custom-call(bf16[4,192,2432]{2,1,0:T(8,128)(2,1)S(1)} %get-tuple-element.43.own_high, bf16[4,192,2432]{2,1,0:T(8,128)(2,1)S(1)} %get-tuple-element.44.own_low, bf16[4,192,2432]{2,1,0:T(8,128)(2,1)S(1)} %get-tuple-element.54.other_high, ...), custom_call_target="tpu_custom_call" | custom-call | flops 6000000000 | bytes 25000000 | tf_op jit(solution)/shard_map/pallas_call | solution.py:228
  93.8 0.0 collective-permute-done.21
  93.9 0.0 collective-permute-done.20
  93.9 0.0 collective-permute-done.19
  93.9 3.5 %shard_map.41 = (f32[192,256]{1,0:T(8,128)S(1)}, f32[192,256]{1,0:T(8,128)S(1)}) custom-call(bf16[384,3072]{1,0:T(8,128)(2,1)S(1)} %get-tuple-element.64.high_ref, bf16[384,3072]{1,0:T(8,128)(2,1)S(1)} %get-tuple-element.65.low_ref, f32[8,152,256]{2,1,0:T(8,128)S(1)} %bitcast.25, f32[4,152,256]{2,1,0:T(8,128)S(1)} %bitcast.32, f32[4,152,256]{2,1,0:T(8,128)S(1)} %bitcast.31, ...), custom_call_target="tpu_custom_call" | custom-call | flops 2000000000 | bytes 8000000 | tf_op jit(solution)/shard_map/pallas_call | solution.py:276
  97.4 0.1 collective-permute-start.22
  97.5 1.4 %collective-permute-done.22 = f32[192,256]{1,0:T(8,128)S(1)} collective-permute-done((f32[192,256]{1,0:T(8,128)S(1)}, f32[192,256]{1,0:T(8,128)S(1)}, u32[]{:S(2)}, u32[]{:S(2)}) %collective-permute-start.22) | collective-permute-done | bytes 196640 | tf_op jit(solution)/shard_map/ppermute | solution.py:36
  98.9 0.7 add.19
  (14 shorter events, 0.4 us)
Async XLA Ops:
  0.0 1.1 %copy-start.1 = (bf16[2400,128]{1,0:T(8,128)(2,1)S(1)}, bf16[2400,128]{1,0:T(8,128)(2,1)}, u32[]{:S(2)}) copy-start(bf16[2400,128]{1,0:T(8,128)(2,1)} %ac_ref.1) | copy-start | bytes 1843204
  6.2 3.2 %collective-permute-start = (f32[4,152,256]{2,1,0:T(8,128)S(1)}, f32[4,152,256]{2,1,0:T(8,128)S(1)}, u32[]{:S(2)}, u32[]{:S(2)}) collective-permute-start(f32[4,152,256]{2,1,0:T(8,128)S(1)} %get-tuple-element.38), channel_id=1, source_target_pairs={{0,4},{1,5},{2,6},{3,7},{4,0},{5,1},{6,2},{7,3},{8,12},{9,13},{10,... | collective-permute-start | bytes 1867784 | tf_op jit(solution)/shard_map/ppermute | solution.py:36
  9.5 23.0 %collective-permute-start.7 = (f32[192,8,2400]{2,1,0:T(8,128)}, f32[192,8,2400]{2,1,0:T(8,128)}, u32[]{:S(2)}, u32[]{:S(2)}) collective-permute-start(f32[192,8,2400]{2,1,0:T(8,128)} %amp_ref), channel_id=1, source_target_pairs={{0,4},{1,5},{2,6},{3,7},{4,0},{5,1},{6,2},{7,3},{8,12},{9,13},{10,... | collective-permute-start | bytes 44236808 | tf_op jit(solution)/shard_map/ppermute | solution.py:36
  9.9 9.7 %collective-permute-start.1 = (f32[152,256]{1,0:T(8,128)S(1)}, f32[152,256]{1,0:T(8,128)S(1)}, u32[]{:S(2)}, u32[]{:S(2)}) collective-permute-start(f32[152,256]{1,0:T(8,128)S(1)} %get-tuple-element.69), channel_id=1, source_target_pairs={{0,1},{1,2},{2,3},{3,0},{4,5},{5,6},{6,7},{7,4},{8,9},{9,10},{10,1... | collective-permute-start | bytes 466952 | tf_op jit(solution)/shard_map/ppermute | solution.py:36
  11.3 9.8 %collective-permute-start.3 = (f32[152,256]{1,0:T(8,128)S(1)}, f32[152,256]{1,0:T(8,128)S(1)}, u32[]{:S(2)}, u32[]{:S(2)}) collective-permute-start(f32[152,256]{1,0:T(8,128)S(1)} %get-tuple-element.70), channel_id=1, source_target_pairs={{0,2},{1,3},{2,0},{3,1},{4,6},{5,7},{6,4},{7,5},{8,10},{9,11},{10,... | collective-permute-start | bytes 466952 | tf_op jit(solution)/shard_map/ppermute | solution.py:36
  13.8 7.4 %collective-permute-start.2 = (f32[152,256]{1,0:T(8,128)S(1)}, f32[152,256]{1,0:T(8,128)S(1)}, u32[]{:S(2)}, u32[]{:S(2)}) collective-permute-start(f32[152,256]{1,0:T(8,128)S(1)} %get-tuple-element.71), channel_id=1, source_target_pairs={{0,3},{1,0},{2,1},{3,2},{4,7},{5,4},{6,5},{7,6},{8,11},{9,8},{10,9... | collective-permute-start | bytes 466952 | tf_op jit(solution)/shard_map/ppermute | solution.py:36
  21.2 6.0 %collective-permute-start.6 = (f32[152,256]{1,0:T(8,128)S(1)}, f32[152,256]{1,0:T(8,128)S(1)}, u32[]{:S(2)}, u32[]{:S(2)}) collective-permute-start(f32[152,256]{1,0:T(8,128)S(1)} %fusion.1), channel_id=1, source_target_pairs={{0,16},{1,17},{2,18},{3,19},{4,6},{5,7},{6,4},{7,5},{8,24},{9,25},... | collective-permute-start | bytes 466952 | tf_op jit(solution)/shard_map/ppermute | solution.py:36
  23.3 5.2 %collective-permute-start.5 = (f32[152,256]{1,0:T(8,128)S(1)}, f32[152,256]{1,0:T(8,128)S(1)}, u32[]{:S(2)}, u32[]{:S(2)}) collective-permute-start(f32[152,256]{1,0:T(8,128)S(1)} %fusion.1), channel_id=1, source_target_pairs={{0,24},{1,25},{2,26},{3,27},{4,7},{5,4},{6,5},{7,6},{8,0},{9,1},{1... | collective-permute-start | bytes 466952 | tf_op jit(solution)/shard_map/ppermute | solution.py:36
  24.3 5.3 %collective-permute-start.4 = (f32[152,256]{1,0:T(8,128)S(1)}, f32[152,256]{1,0:T(8,128)S(1)}, u32[]{:S(2)}, u32[]{:S(2)}) collective-permute-start(f32[152,256]{1,0:T(8,128)S(1)} %fusion.1), channel_id=1, source_target_pairs={{0,8},{1,9},{2,10},{3,11},{4,5},{5,6},{6,7},{7,4},{8,16},{9,17},{1... | collective-permute-start | bytes 466952 | tf_op jit(solution)/shard_map/ppermute | solution.py:36
  32.5 7.5 %collective-permute-start.8 = (f32[304,256]{1,0:T(8,128)S(1)}, f32[304,256]{1,0:T(8,128)S(1)}, u32[]{:S(2)}, u32[]{:S(2)}) collective-permute-start(f32[304,256]{1,0:T(8,128)S(1)} %get-tuple-element.76), channel_id=1, source_target_pairs={{0,32},{1,33},{2,34},{3,35},{4,12},{5,13},{6,14},{7,15},{8,40},{9,... | collective-permute-start | bytes 933896 | tf_op jit(solution)/shard_map/ppermute | solution.py:36
  34.0 9.3 %collective-permute-start.9 = (f32[304,256]{1,0:T(8,128)S(1)}, f32[304,256]{1,0:T(8,128)S(1)}, u32[]{:S(2)}, u32[]{:S(2)}) collective-permute-start(f32[304,256]{1,0:T(8,128)S(1)} %get-tuple-element.72), channel_id=1, source_target_pairs={{0,32},{1,33},{2,34},{3,35},{4,12},{5,13},{6,14},{7,15},{8,40},{9,... | collective-permute-start | bytes 933896 | tf_op jit(solution)/shard_map/ppermute | solution.py:36
  35.3 9.4 %collective-permute-start.12 = (f32[304,256]{1,0:T(8,128)S(1)}, f32[304,256]{1,0:T(8,128)S(1)}, u32[]{:S(2)}, u32[]{:S(2)}) collective-permute-start(f32[304,256]{1,0:T(8,128)S(1)} %get-tuple-element.72), channel_id=1, source_target_pairs={{0,96},{1,97},{2,98},{3,99},{4,28},{5,29},{6,30},{7,31},{8,104},{9... | collective-permute-start | bytes 933896 | tf_op jit(solution)/shard_map/ppermute | solution.py:36
  36.7 12.0 %collective-permute-start.14 = (f32[304,256]{1,0:T(8,128)S(1)}, f32[304,256]{1,0:T(8,128)S(1)}, u32[]{:S(2)}, u32[]{:S(2)}) collective-permute-start(f32[304,256]{1,0:T(8,128)S(1)} %get-tuple-element.76), channel_id=1, source_target_pairs={{0,96},{1,97},{2,98},{3,99},{4,28},{5,29},{6,30},{7,31},{8,104},{9... | collective-permute-start | bytes 933896 | tf_op jit(solution)/shard_map/ppermute | solution.py:36
  43.3 21.8 %collective-permute-start.10 = (f32[1216,256]{1,0:T(8,128)S(1)}, f32[1216,256]{1,0:T(8,128)S(1)}, u32[]{:S(2)}, u32[]{:S(2)}) collective-permute-start(f32[1216,256]{1,0:T(8,128)S(1)} %constant_dynamic-update-slice_fusion.4), channel_id=1, source_target_pairs={{0,1},{1,2},{2,3},{3,0},{4,36},{5,37},{6,38},{7,39},{8,9},{9,10},{... | collective-permute-start | bytes 3735560 | tf_op jit(solution)/shard_map/ppermute | solution.py:36
  44.7 6.0 %collective-permute-start.13 = (f32[304,256]{1,0:T(8,128)S(1)}, f32[304,256]{1,0:T(8,128)S(1)}, u32[]{:S(2)}, u32[]{:S(2)}) collective-permute-start(f32[304,256]{1,0:T(8,128)S(1)} %collective-permute-done.12), channel_id=1, source_target_pairs={{0,96},{1,97},{2,98},{3,99},{4,28},{5,29},{6,30},{7,31},{8,104},{9... | collective-permute-start | bytes 933896 | tf_op jit(solution)/shard_map/ppermute | solution.py:36
  46.5 7.3 %collective-permute-start.11 = (f32[304,256]{1,0:T(8,128)S(1)}, f32[304,256]{1,0:T(8,128)S(1)}, u32[]{:S(2)}, u32[]{:S(2)}) collective-permute-start(f32[304,256]{1,0:T(8,128)S(1)} %collective-permute-done.8), channel_id=1, source_target_pairs={{0,32},{1,33},{2,34},{3,35},{4,12},{5,13},{6,14},{7,15},{8,40},{9,... | collective-permute-start | bytes 933896 | tf_op jit(solution)/shard_map/ppermute | solution.py:36
  46.5 32.9 %collective-permute-start.17 = (f32[1216,256]{1,0:T(8,128)S(1)}, f32[1216,256]{1,0:T(8,128)S(1)}, u32[]{:S(2)}, u32[]{:S(2)}) collective-permute-start(f32[1216,256]{1,0:T(8,128)S(1)} %constant_dynamic-update-slice_fusion.4), channel_id=1, source_target_pairs={{0,3},{1,0},{2,1},{3,2},{4,100},{5,101},{6,102},{7,103},{8,11},{9,... | collective-permute-start | bytes 3735560 | tf_op jit(solution)/shard_map/ppermute | solution.py:36
  53.8 25.6 %collective-permute-start.18 = (f32[1216,256]{1,0:T(8,128)S(1)}, f32[1216,256]{1,0:T(8,128)S(1)}, u32[]{:S(2)}, u32[]{:S(2)}) collective-permute-start(f32[1216,256]{1,0:T(8,128)S(1)} %constant_dynamic-update-slice_fusion.10), channel_id=1, source_target_pairs={{0,1},{1,2},{2,3},{3,0},{4,36},{5,37},{6,38},{7,39},{8,9},{9,10},{... | collective-permute-start | bytes 3735560 | tf_op jit(solution)/shard_map/ppermute | solution.py:36
  55.5 17.2 %collective-permute-start.15 = (f32[608,256]{1,0:T(8,128)S(1)}, f32[608,256]{1,0:T(8,128)S(1)}, u32[]{:S(2)}, u32[]{:S(2)}) collective-permute-start(f32[608,256]{1,0:T(8,128)S(1)} %pad_maximum_fusion), channel_id=1, source_target_pairs={{0,3},{1,0},{2,1},{3,2},{4,100},{5,101},{6,102},{7,103},{8,11},{9,... | collective-permute-start | bytes 1867784 | tf_op jit(solution)/shard_map/ppermute | solution.py:36
  56.7 22.7 %collective-permute-start.16 = (f32[608,256]{1,0:T(8,128)S(1)}, f32[608,256]{1,0:T(8,128)S(1)}, u32[]{:S(2)}, u32[]{:S(2)}) collective-permute-start(f32[608,256]{1,0:T(8,128)S(1)} %pad_maximum_fusion.1), channel_id=1, source_target_pairs={{0,3},{1,0},{2,1},{3,2},{4,100},{5,101},{6,102},{7,103},{8,11},{9,... | collective-permute-start | bytes 1867784 | tf_op jit(solution)/shard_map/ppermute | solution.py:36
  62.5 1.8 %copy-start = (bf16[4,192,2432]{2,1,0:T(8,128)(2,1)}, bf16[4,192,2432]{2,1,0:T(8,128)(2,1)S(1)}, u32[]{:S(2)}) copy-start(bf16[4,192,2432]{2,1,0:T(8,128)(2,1)S(1)} %get-tuple-element.55.other_low) | copy-start | bytes 11206660
  65.0 28.8 %collective-permute-start.19 = (f32[1216,256]{1,0:T(8,128)S(1)}, f32[1216,256]{1,0:T(8,128)S(1)}, u32[]{:S(2)}, u32[]{:S(2)}) collective-permute-start(f32[1216,256]{1,0:T(8,128)S(1)} %collective-permute-done.10), channel_id=1, source_target_pairs={{0,1},{1,2},{2,3},{3,0},{4,36},{5,37},{6,38},{7,39},{8,9},{9,10},{... | collective-permute-start | bytes 3735560 | tf_op jit(solution)/shard_map/ppermute | solution.py:36
  72.7 21.1 %collective-permute-start.21 = (f32[608,256]{1,0:T(8,128)S(1)}, f32[608,256]{1,0:T(8,128)S(1)}, u32[]{:S(2)}, u32[]{:S(2)}) collective-permute-start(f32[608,256]{1,0:T(8,128)S(1)} %collective-permute-done.15), channel_id=1, source_target_pairs={{0,3},{1,0},{2,1},{3,2},{4,100},{5,101},{6,102},{7,103},{8,11},{9,... | collective-permute-start | bytes 1867784 | tf_op jit(solution)/shard_map/ppermute | solution.py:36
  79.4 14.5 %collective-permute-start.20 = (f32[608,256]{1,0:T(8,128)S(1)}, f32[608,256]{1,0:T(8,128)S(1)}, u32[]{:S(2)}, u32[]{:S(2)}) collective-permute-start(f32[608,256]{1,0:T(8,128)S(1)} %collective-permute-done.16), channel_id=1, source_target_pairs={{0,3},{1,0},{2,1},{3,2},{4,100},{5,101},{6,102},{7,103},{8,11},{9,... | collective-permute-start | bytes 1867784 | tf_op jit(solution)/shard_map/ppermute | solution.py:36
  97.4 1.5 %collective-permute-start.22 = (f32[192,256]{1,0:T(8,128)S(1)}, f32[192,256]{1,0:T(8,128)S(1)}, u32[]{:S(2)}, u32[]{:S(2)}) collective-permute-start(f32[192,256]{1,0:T(8,128)S(1)} %get-tuple-element.68), channel_id=1, source_target_pairs={{0,4},{1,5},{2,6},{3,7},{4,0},{5,1},{6,2},{7,3},{8,12},{9,13},{10,... | collective-permute-start | bytes 589832 | tf_op jit(solution)/shard_map/ppermute | solution.py:36

commit v6 on v5

--- a/solution.py
+++ b/solution.py
@@ -305,9 +305,9 @@
     up = [permute(half, 1, STEPS[1]) for half in halves]
     down = [permute(half, -1, STEPS[1]) for half in halves]
     far = [permute(up[0], 1, STEPS[1]), permute(down[1], -1, STEPS[1])]
+    down, other = barrier((down, other))
     first, near = jnp.concatenate(halves + up, axis=0), jnp.concatenate(down, axis=0)
     up_first, down_near = permute(first, 1, STEPS[2]), permute(near, -1, STEPS[2])
-    far, other = barrier((far, other))
     far = jnp.concatenate(far, axis=0)
     second = jnp.concatenate([near, far], axis=0)
     down_far = permute(far, -1, STEPS[2])

time: 99.9 us -> 99 us (level)
  waiting for transfers between devices: 35.2 us -> 33.5 us
    ppermute x23, waiting for transfers between devices: 35.2 us -> 33.5 us  [permute(): return lax.ppermute(value, AXES, pairs)]
  transfers between devices with their start and end apart: 23 -> 23, of which waited for: 14 -> 15; matrix products, arithmetic and copies ran while one was open for 0% -> 0% of each run, Pallas kernels for 21% -> 21%
where the time goes in v6:
time: 99 us; the launch traced here: 98.7 us
  waiting for transfers between devices  33.5 us (34%)
  starting transfers between devices  31.6 us (32%)
  Pallas kernels  29.4 us (30%)
  local copies, waits for them, and re-layouts  3.12 us (3%)
    ppermute x23, waiting for transfers between devices, permute(): return lax.ppermute(value, AXES, pairs)  33.5 us
    ppermute x23, starting transfers between devices, permute(): return lax.ppermute(value, AXES, pairs)  31.6 us
    pallas_call x1, Pallas kernels, early_ladder(): pl.pallas_call(early_kernel, grid=(SIDE,), in_specs=[amp_spec] * 4 + [pl....  11.2 us
    pallas_call x2, Pallas kernels, arrange(): pl.pallas_call(arrange_kernel, grid=(pairs // rows,), out_shape=(out, out...  9.54 us
    pallas_call x1, Pallas kernels, partial_integrals(): pl.pallas_call(partial_kernel, grid=(2,), out_shape=(out, out), in_specs=...  5.11 us
    pallas_call x1, Pallas kernels, late_ladder(): pl.pallas_call(late_kernel, in_specs=[whole] * (3 + len(pieces)), out_spe...  3.5 us
    unnamed x10, local copies, waits for them, and re-layouts  3 us
  transfers between devices with their start and end apart: 23, of which 15 were waited for; matrix products, arithmetic and copies ran while one was open for 0% of the time, Pallas kernels for 21%

profile of v6, /device:TPU:1, one launch (start us, length us, event | category | flops | bytes accessed | tf_op | source)
XLA Modules:
  0.0 98.7 jit_solution(9970399803929345836)
XLA Ops:
  0.0 0.0 copy-start.1
  0.0 1.1 %copy-done.1 = bf16[2400,128]{1,0:T(8,128)(2,1)S(1)} copy-done((bf16[2400,128]{1,0:T(8,128)(2,1)S(1)}, bf16[2400,128]{1,0:T(8,128)(2,1)}, u32[]{:S(2)}) %copy-start.1) | copy-done | bytes 614424
  1.1 5.1 %shard_map.37 = (f32[4,152,256]{2,1,0:T(8,128)S(1)}, f32[4,152,256]{2,1,0:T(8,128)S(1)}) custom-call(bf16[75,38400]{1,0:T(8,128)(2,1)} %bitcast.33, bf16[75,38400]{1,0:T(8,128)(2,1)} %bitcast.34, bf16[2400,128]{1,0:T(8,128)(2,1)S(1)} %copy-done.1), custom_call_target="tpu_custom_call" | custom-call | flops 1000000000 | bytes 8000000 | tf_op jit(solution)/shard_map/pallas_call | solution.py:98
  6.2 1.5 %collective-permute-start = (f32[4,152,256]{2,1,0:T(8,128)S(1)}, f32[4,152,256]{2,1,0:T(8,128)S(1)}, u32[]{:S(2)}, u32[]{:S(2)}) collective-permute-start(f32[4,152,256]{2,1,0:T(8,128)S(1)} %get-tuple-element.38), channel_id=1, source_target_pairs={{0,4},{1,5},{2,6},{3,7},{4,0},{5,1},{6,2},{7,3},{8,12},{9,13},{10,... | collective-permute-start | bytes 1867784 | tf_op jit(solution)/shard_map/ppermute | solution.py:36
  7.7 1.7 %collective-permute-done = f32[4,152,256]{2,1,0:T(8,128)S(1)} collective-permute-done((f32[4,152,256]{2,1,0:T(8,128)S(1)}, f32[4,152,256]{2,1,0:T(8,128)S(1)}, u32[]{:S(2)}, u32[]{:S(2)}) %collective-permute-start) | collective-permute-done | bytes 622624 | tf_op jit(solution)/shard_map/ppermute | solution.py:36
  9.4 0.1 add.15
  9.5 0.5 collective-permute-start.7
  9.9 1.4 %collective-permute-start.1 = (f32[152,256]{1,0:T(8,128)S(1)}, f32[152,256]{1,0:T(8,128)S(1)}, u32[]{:S(2)}, u32[]{:S(2)}) collective-permute-start(f32[152,256]{1,0:T(8,128)S(1)} %get-tuple-element.69), channel_id=1, source_target_pairs={{0,1},{1,2},{2,3},{3,0},{4,5},{5,6},{6,7},{7,4},{8,9},{9,10},{10,1... | collective-permute-start | bytes 466952 | tf_op jit(solution)/shard_map/ppermute | solution.py:36
  11.3 2.5 %collective-permute-start.3 = (f32[152,256]{1,0:T(8,128)S(1)}, f32[152,256]{1,0:T(8,128)S(1)}, u32[]{:S(2)}, u32[]{:S(2)}) collective-permute-start(f32[152,256]{1,0:T(8,128)S(1)} %get-tuple-element.70), channel_id=1, source_target_pairs={{0,2},{1,3},{2,0},{3,1},{4,6},{5,7},{6,4},{7,5},{8,10},{9,11},{10,... | collective-permute-start | bytes 466952 | tf_op jit(solution)/shard_map/ppermute | solution.py:36
  13.8 1.1 %collective-permute-start.2 = (f32[152,256]{1,0:T(8,128)S(1)}, f32[152,256]{1,0:T(8,128)S(1)}, u32[]{:S(2)}, u32[]{:S(2)}) collective-permute-start(f32[152,256]{1,0:T(8,128)S(1)} %get-tuple-element.71), channel_id=1, source_target_pairs={{0,3},{1,0},{2,1},{3,2},{4,7},{5,4},{6,5},{7,6},{8,11},{9,8},{10,9... | collective-permute-start | bytes 466952 | tf_op jit(solution)/shard_map/ppermute | solution.py:36
  14.9 4.8 %shard_map.38 = (bf16[4,192,2432]{2,1,0:T(8,128)(2,1)S(1)}, bf16[4,192,2432]{2,1,0:T(8,128)(2,1)S(1)}) custom-call(f32[192,8,2400]{2,1,0:T(8,128)} %amp_ref), custom_call_target="tpu_custom_call" | custom-call | flops 1000000 | bytes 15000000 | tf_op jit(solution)/shard_map/pallas_call | solution.py:152
  19.7 0.0 collective-permute-done.1
  19.7 1.4 %collective-permute-done.3 = f32[152,256]{1,0:T(8,128)S(1)} collective-permute-done((f32[152,256]{1,0:T(8,128)S(1)}, f32[152,256]{1,0:T(8,128)S(1)}, u32[]{:S(2)}, u32[]{:S(2)}) %collective-permute-start.3) | collective-permute-done | bytes 155680 | tf_op jit(solution)/shard_map/ppermute | solution.py:36
  21.1 0.0 collective-permute-done.2
  21.2 2.1 %collective-permute-start.6 = (f32[152,256]{1,0:T(8,128)S(1)}, f32[152,256]{1,0:T(8,128)S(1)}, u32[]{:S(2)}, u32[]{:S(2)}) collective-permute-start(f32[152,256]{1,0:T(8,128)S(1)} %fusion.1), channel_id=1, source_target_pairs={{0,16},{1,17},{2,18},{3,19},{4,6},{5,7},{6,4},{7,5},{8,24},{9,25},... | collective-permute-start | bytes 466952 | tf_op jit(solution)/shard_map/ppermute | solution.py:36
  23.3 1.0 %collective-permute-start.5 = (f32[152,256]{1,0:T(8,128)S(1)}, f32[152,256]{1,0:T(8,128)S(1)}, u32[]{:S(2)}, u32[]{:S(2)}) collective-permute-start(f32[152,256]{1,0:T(8,128)S(1)} %fusion.1), channel_id=1, source_target_pairs={{0,24},{1,25},{2,26},{3,27},{4,7},{5,4},{6,5},{7,6},{8,0},{9,1},{1... | collective-permute-start | bytes 466952 | tf_op jit(solution)/shard_map/ppermute | solution.py:36
  24.3 0.5 collective-permute-start.4
  24.8 2.4 %collective-permute-done.6 = f32[152,256]{1,0:T(8,128)S(1)} collective-permute-done((f32[152,256]{1,0:T(8,128)S(1)}, f32[152,256]{1,0:T(8,128)S(1)}, u32[]{:S(2)}, u32[]{:S(2)}) %collective-permute-start.6) | collective-permute-done | bytes 155680 | tf_op jit(solution)/shard_map/ppermute | solution.py:36
  27.1 1.4 %collective-permute-done.5 = f32[152,256]{1,0:T(8,128)S(1)} collective-permute-done((f32[152,256]{1,0:T(8,128)S(1)}, f32[152,256]{1,0:T(8,128)S(1)}, u32[]{:S(2)}, u32[]{:S(2)}) %collective-permute-start.5) | collective-permute-done | bytes 155680 | tf_op jit(solution)/shard_map/ppermute | solution.py:36
  28.5 1.1 %collective-permute-done.4 = f32[152,256]{1,0:T(8,128)S(1)} collective-permute-done((f32[152,256]{1,0:T(8,128)S(1)}, f32[152,256]{1,0:T(8,128)S(1)}, u32[]{:S(2)}, u32[]{:S(2)}) %collective-permute-start.4) | collective-permute-done | bytes 155680 | tf_op jit(solution)/shard_map/ppermute | solution.py:36
  29.6 2.8 %collective-permute-done.7.amp_ref = f32[192,8,2400]{2,1,0:T(8,128)} collective-permute-done((f32[192,8,2400]{2,1,0:T(8,128)}, f32[192,8,2400]{2,1,0:T(8,128)}, u32[]{:S(2)}, u32[]{:S(2)}) %collective-permute-start.7) | collective-permute-done | bytes 14745632 | tf_op jit(solution)/shard_map/ppermute | solution.py:36
  32.5 1.4 %collective-permute-start.8 = (f32[304,256]{1,0:T(8,128)S(1)}, f32[304,256]{1,0:T(8,128)S(1)}, u32[]{:S(2)}, u32[]{:S(2)}) collective-permute-start(f32[304,256]{1,0:T(8,128)S(1)} %get-tuple-element.76), channel_id=1, source_target_pairs={{0,32},{1,33},{2,34},{3,35},{4,12},{5,13},{6,14},{7,15},{8,40},{9,... | collective-permute-start | bytes 933896 | tf_op jit(solution)/shard_map/ppermute | solution.py:36
  34.0 1.4 %collective-permute-start.9 = (f32[304,256]{1,0:T(8,128)S(1)}, f32[304,256]{1,0:T(8,128)S(1)}, u32[]{:S(2)}, u32[]{:S(2)}) collective-permute-start(f32[304,256]{1,0:T(8,128)S(1)} %get-tuple-element.72), channel_id=1, source_target_pairs={{0,32},{1,33},{2,34},{3,35},{4,12},{5,13},{6,14},{7,15},{8,40},{9,... | collective-permute-start | bytes 933896 | tf_op jit(solution)/shard_map/ppermute | solution.py:36
  35.3 1.4 %collective-permute-start.12 = (f32[304,256]{1,0:T(8,128)S(1)}, f32[304,256]{1,0:T(8,128)S(1)}, u32[]{:S(2)}, u32[]{:S(2)}) collective-permute-start(f32[304,256]{1,0:T(8,128)S(1)} %get-tuple-element.72), channel_id=1, source_target_pairs={{0,96},{1,97},{2,98},{3,99},{4,28},{5,29},{6,30},{7,31},{8,104},{9... | collective-permute-start | bytes 933896 | tf_op jit(solution)/shard_map/ppermute | solution.py:36
  36.7 0.3 collective-permute-start.11
  37.0 2.9 %collective-permute-done.8 = f32[304,256]{1,0:T(8,128)S(1)} collective-permute-done((f32[304,256]{1,0:T(8,128)S(1)}, f32[304,256]{1,0:T(8,128)S(1)}, u32[]{:S(2)}, u32[]{:S(2)}) %collective-permute-start.8) | collective-permute-done | bytes 311328 | tf_op jit(solution)/shard_map/ppermute | solution.py:36
  40.0 3.3 %collective-permute-done.9 = f32[304,256]{1,0:T(8,128)S(1)} collective-permute-done((f32[304,256]{1,0:T(8,128)S(1)}, f32[304,256]{1,0:T(8,128)S(1)}, u32[]{:S(2)}, u32[]{:S(2)}) %collective-permute-start.9) | collective-permute-done | bytes 311328 | tf_op jit(solution)/shard_map/ppermute | solution.py:36
  43.3 1.4 %collective-permute-start.10 = (f32[1216,256]{1,0:T(8,128)S(1)}, f32[1216,256]{1,0:T(8,128)S(1)}, u32[]{:S(2)}, u32[]{:S(2)}) collective-permute-start(f32[1216,256]{1,0:T(8,128)S(1)} %constant_dynamic-update-slice_fusion.4), channel_id=1, source_target_pairs={{0,1},{1,2},{2,3},{3,0},{4,36},{5,37},{6,38},{7,39},{8,9},{9,10},{... | collective-permute-start | bytes 3735560 | tf_op jit(solution)/shard_map/ppermute | solution.py:36
  44.7 0.3 collective-permute-start.13
  45.0 2.3 %collective-permute-start.17 = (f32[1216,256]{1,0:T(8,128)S(1)}, f32[1216,256]{1,0:T(8,128)S(1)}, u32[]{:S(2)}, u32[]{:S(2)}) collective-permute-start(f32[1216,256]{1,0:T(8,128)S(1)} %constant_dynamic-update-slice_fusion.4), channel_id=1, source_target_pairs={{0,3},{1,0},{2,1},{3,2},{4,100},{5,101},{6,102},{7,103},{8,11},{9,... | collective-permute-start | bytes 3735560 | tf_op jit(solution)/shard_map/ppermute | solution.py:36
  47.3 0.0 collective-permute-done.12
  47.3 0.0 collective-permute-done.11
  47.3 2.6 %collective-permute-start.14 = (f32[304,256]{1,0:T(8,128)S(1)}, f32[304,256]{1,0:T(8,128)S(1)}, u32[]{:S(2)}, u32[]{:S(2)}) collective-permute-start(f32[304,256]{1,0:T(8,128)S(1)} %collective-permute-done.12), channel_id=1, source_target_pairs={{0,96},{1,97},{2,98},{3,99},{4,28},{5,29},{6,30},{7,31},{8,104},{9... | collective-permute-start | bytes 933896 | tf_op jit(solution)/shard_map/ppermute | solution.py:36
  49.9 2.0 %collective-permute-done.13 = f32[304,256]{1,0:T(8,128)S(1)} collective-permute-done((f32[304,256]{1,0:T(8,128)S(1)}, f32[304,256]{1,0:T(8,128)S(1)}, u32[]{:S(2)}, u32[]{:S(2)}) %collective-permute-start.13) | collective-permute-done | bytes 311328 | tf_op jit(solution)/shard_map/ppermute | solution.py:36
  52.0 1.7 %collective-permute-done.14 = f32[304,256]{1,0:T(8,128)S(1)} collective-permute-done((f32[304,256]{1,0:T(8,128)S(1)}, f32[304,256]{1,0:T(8,128)S(1)}, u32[]{:S(2)}, u32[]{:S(2)}) %collective-permute-start.14) | collective-permute-done | bytes 311328 | tf_op jit(solution)/shard_map/ppermute | solution.py:36
  53.8 0.1 collective-permute-start.18
  53.9 2.7 %collective-permute-start.15 = (f32[608,256]{1,0:T(8,128)S(1)}, f32[608,256]{1,0:T(8,128)S(1)}, u32[]{:S(2)}, u32[]{:S(2)}) collective-permute-start(f32[608,256]{1,0:T(8,128)S(1)} %pad_maximum_fusion), channel_id=1, source_target_pairs={{0,3},{1,0},{2,1},{3,2},{4,100},{5,101},{6,102},{7,103},{8,11},{9,... | collective-permute-start | bytes 1867784 | tf_op jit(solution)/shard_map/ppermute | solution.py:36
  56.7 4.8 %shard_map.39 = (bf16[4,192,2432]{2,1,0:T(8,128)(2,1)S(1)}, bf16[4,192,2432]{2,1,0:T(8,128)(2,1)S(1)}) custom-call(f32[192,8,2400]{2,1,0:T(8,128)} %collective-permute-done.7.amp_ref), custom_call_target="tpu_custom_call" | custom-call | flops 1000000 | bytes 15000000 | tf_op jit(solution)/shard_map/pallas_call | solution.py:152
  61.5 0.0 copy-start
  61.5 1.8 %copy-done = bf16[4,192,2432]{2,1,0:T(8,128)(2,1)} copy-done((bf16[4,192,2432]{2,1,0:T(8,128)(2,1)}, bf16[4,192,2432]{2,1,0:T(8,128)(2,1)S(1)}, u32[]{:S(2)}) %copy-start) | copy-done | bytes 3735576
  63.3 0.2 collective-permute-start.16
  63.4 1.6 %collective-permute-done.10 = f32[1216,256]{1,0:T(8,128)S(1)} collective-permute-done((f32[1216,256]{1,0:T(8,128)S(1)}, f32[1216,256]{1,0:T(8,128)S(1)}, u32[]{:S(2)}, u32[]{:S(2)}) %collective-permute-start.10) | collective-permute-done | bytes 1245216 | tf_op jit(solution)/shard_map/ppermute | solution.py:36
  65.0 0.0 collective-permute-start.19
  65.1 6.2 %collective-permute-done.15 = f32[608,256]{1,0:T(8,128)S(1)} collective-permute-done((f32[608,256]{1,0:T(8,128)S(1)}, f32[608,256]{1,0:T(8,128)S(1)}, u32[]{:S(2)}, u32[]{:S(2)}) %collective-permute-start.15) | collective-permute-done | bytes 622624 | tf_op jit(solution)/shard_map/ppermute | solution.py:36
  71.3 3.3 %collective-permute-start.21 = (f32[608,256]{1,0:T(8,128)S(1)}, f32[608,256]{1,0:T(8,128)S(1)}, u32[]{:S(2)}, u32[]{:S(2)}) collective-permute-start(f32[608,256]{1,0:T(8,128)S(1)} %collective-permute-done.15), channel_id=1, source_target_pairs={{0,3},{1,0},{2,1},{3,2},{4,100},{5,101},{6,102},{7,103},{8,11},{9,... | collective-permute-start | bytes 1867784 | tf_op jit(solution)/shard_map/ppermute | solution.py:36
  74.6 3.4 %collective-permute-done.16 = f32[608,256]{1,0:T(8,128)S(1)} collective-permute-done((f32[608,256]{1,0:T(8,128)S(1)}, f32[608,256]{1,0:T(8,128)S(1)}, u32[]{:S(2)}, u32[]{:S(2)}) %collective-permute-start.16) | collective-permute-done | bytes 622624 | tf_op jit(solution)/shard_map/ppermute | solution.py:36
  77.9 0.0 collective-permute-done.17
  77.9 0.5 collective-permute-done.18
  78.4 2.8 %collective-permute-start.20 = (f32[608,256]{1,0:T(8,128)S(1)}, f32[608,256]{1,0:T(8,128)S(1)}, u32[]{:S(2)}, u32[]{:S(2)}) collective-permute-start(f32[608,256]{1,0:T(8,128)S(1)} %collective-permute-done.16), channel_id=1, source_target_pairs={{0,3},{1,0},{2,1},{3,2},{4,100},{5,101},{6,102},{7,103},{8,11},{9,... | collective-permute-start | bytes 1867784 | tf_op jit(solution)/shard_map/ppermute | solution.py:36
  81.2 11.2 %shard_map.40 = (f32[384,256]{1,0:T(8,128)S(1)}, bf16[384,3072]{1,0:T(8,128)(2,1)S(1)}, bf16[384,3072]{1,0:T(8,128)(2,1)S(1)}) custom-call(bf16[4,192,2432]{2,1,0:T(8,128)(2,1)S(1)} %get-tuple-element.43.own_high, bf16[4,192,2432]{2,1,0:T(8,128)(2,1)S(1)} %get-tuple-element.44.own_low, bf16[4,192,2432]{2,1,0:T(8,128)(2,1)S(1)} %get-tuple-element.54.other_high, ...), custom_call_target="tpu_custom_call" | custom-call | flops 6000000000 | bytes 25000000 | tf_op jit(solution)/shard_map/pallas_call | solution.py:228
  92.5 0.0 collective-permute-done.21
  92.5 0.0 collective-permute-done.20
  92.5 0.0 collective-permute-done.19
  92.5 3.5 %shard_map.41 = (f32[192,256]{1,0:T(8,128)S(1)}, f32[192,256]{1,0:T(8,128)S(1)}) custom-call(bf16[384,3072]{1,0:T(8,128)(2,1)S(1)} %get-tuple-element.64.high_ref, bf16[384,3072]{1,0:T(8,128)(2,1)S(1)} %get-tuple-element.65.low_ref, f32[8,152,256]{2,1,0:T(8,128)S(1)} %bitcast.25, f32[4,152,256]{2,1,0:T(8,128)S(1)} %bitcast.32, f32[4,152,256]{2,1,0:T(8,128)S(1)} %bitcast.31, ...), custom_call_target="tpu_custom_call" | custom-call | flops 2000000000 | bytes 8000000 | tf_op jit(solution)/shard_map/pallas_call | solution.py:276
  96.0 0.9 collective-permute-start.22
  96.9 1.1 %collective-permute-done.22 = f32[192,256]{1,0:T(8,128)S(1)} collective-permute-done((f32[192,256]{1,0:T(8,128)S(1)}, f32[192,256]{1,0:T(8,128)S(1)}, u32[]{:S(2)}, u32[]{:S(2)}) %collective-permute-start.22) | collective-permute-done | bytes 196640 | tf_op jit(solution)/shard_map/ppermute | solution.py:36
  98.0 0.7 add.19
  (14 shorter events, 0.4 us)
Async XLA Ops:
  0.0 1.1 %copy-start.1 = (bf16[2400,128]{1,0:T(8,128)(2,1)S(1)}, bf16[2400,128]{1,0:T(8,128)(2,1)}, u32[]{:S(2)}) copy-start(bf16[2400,128]{1,0:T(8,128)(2,1)} %ac_ref.1) | copy-start | bytes 1843204
  6.2 3.2 %collective-permute-start = (f32[4,152,256]{2,1,0:T(8,128)S(1)}, f32[4,152,256]{2,1,0:T(8,128)S(1)}, u32[]{:S(2)}, u32[]{:S(2)}) collective-permute-start(f32[4,152,256]{2,1,0:T(8,128)S(1)} %get-tuple-element.38), channel_id=1, source_target_pairs={{0,4},{1,5},{2,6},{3,7},{4,0},{5,1},{6,2},{7,3},{8,12},{9,13},{10,... | collective-permute-start | bytes 1867784 | tf_op jit(solution)/shard_map/ppermute | solution.py:36
  9.5 23.0 %collective-permute-start.7 = (f32[192,8,2400]{2,1,0:T(8,128)}, f32[192,8,2400]{2,1,0:T(8,128)}, u32[]{:S(2)}, u32[]{:S(2)}) collective-permute-start(f32[192,8,2400]{2,1,0:T(8,128)} %amp_ref), channel_id=1, source_target_pairs={{0,4},{1,5},{2,6},{3,7},{4,0},{5,1},{6,2},{7,3},{8,12},{9,13},{10,... | collective-permute-start | bytes 44236808 | tf_op jit(solution)/shard_map/ppermute | solution.py:36
  9.9 9.7 %collective-permute-start.1 = (f32[152,256]{1,0:T(8,128)S(1)}, f32[152,256]{1,0:T(8,128)S(1)}, u32[]{:S(2)}, u32[]{:S(2)}) collective-permute-start(f32[152,256]{1,0:T(8,128)S(1)} %get-tuple-element.69), channel_id=1, source_target_pairs={{0,1},{1,2},{2,3},{3,0},{4,5},{5,6},{6,7},{7,4},{8,9},{9,10},{10,1... | collective-permute-start | bytes 466952 | tf_op jit(solution)/shard_map/ppermute | solution.py:36
  11.3 9.8 %collective-permute-start.3 = (f32[152,256]{1,0:T(8,128)S(1)}, f32[152,256]{1,0:T(8,128)S(1)}, u32[]{:S(2)}, u32[]{:S(2)}) collective-permute-start(f32[152,256]{1,0:T(8,128)S(1)} %get-tuple-element.70), channel_id=1, source_target_pairs={{0,2},{1,3},{2,0},{3,1},{4,6},{5,7},{6,4},{7,5},{8,10},{9,11},{10,... | collective-permute-start | bytes 466952 | tf_op jit(solution)/shard_map/ppermute | solution.py:36
  13.8 7.4 %collective-permute-start.2 = (f32[152,256]{1,0:T(8,128)S(1)}, f32[152,256]{1,0:T(8,128)S(1)}, u32[]{:S(2)}, u32[]{:S(2)}) collective-permute-start(f32[152,256]{1,0:T(8,128)S(1)} %get-tuple-element.71), channel_id=1, source_target_pairs={{0,3},{1,0},{2,1},{3,2},{4,7},{5,4},{6,5},{7,6},{8,11},{9,8},{10,9... | collective-permute-start | bytes 466952 | tf_op jit(solution)/shard_map/ppermute | solution.py:36
  21.2 6.0 %collective-permute-start.6 = (f32[152,256]{1,0:T(8,128)S(1)}, f32[152,256]{1,0:T(8,128)S(1)}, u32[]{:S(2)}, u32[]{:S(2)}) collective-permute-start(f32[152,256]{1,0:T(8,128)S(1)} %fusion.1), channel_id=1, source_target_pairs={{0,16},{1,17},{2,18},{3,19},{4,6},{5,7},{6,4},{7,5},{8,24},{9,25},... | collective-permute-start | bytes 466952 | tf_op jit(solution)/shard_map/ppermute | solution.py:36
  23.3 5.2 %collective-permute-start.5 = (f32[152,256]{1,0:T(8,128)S(1)}, f32[152,256]{1,0:T(8,128)S(1)}, u32[]{:S(2)}, u32[]{:S(2)}) collective-permute-start(f32[152,256]{1,0:T(8,128)S(1)} %fusion.1), channel_id=1, source_target_pairs={{0,24},{1,25},{2,26},{3,27},{4,7},{5,4},{6,5},{7,6},{8,0},{9,1},{1... | collective-permute-start | bytes 466952 | tf_op jit(solution)/shard_map/ppermute | solution.py:36
  24.3 5.3 %collective-permute-start.4 = (f32[152,256]{1,0:T(8,128)S(1)}, f32[152,256]{1,0:T(8,128)S(1)}, u32[]{:S(2)}, u32[]{:S(2)}) collective-permute-start(f32[152,256]{1,0:T(8,128)S(1)} %fusion.1), channel_id=1, source_target_pairs={{0,8},{1,9},{2,10},{3,11},{4,5},{5,6},{6,7},{7,4},{8,16},{9,17},{1... | collective-permute-start | bytes 466952 | tf_op jit(solution)/shard_map/ppermute | solution.py:36
  32.5 7.5 %collective-permute-start.8 = (f32[304,256]{1,0:T(8,128)S(1)}, f32[304,256]{1,0:T(8,128)S(1)}, u32[]{:S(2)}, u32[]{:S(2)}) collective-permute-start(f32[304,256]{1,0:T(8,128)S(1)} %get-tuple-element.76), channel_id=1, source_target_pairs={{0,32},{1,33},{2,34},{3,35},{4,12},{5,13},{6,14},{7,15},{8,40},{9,... | collective-permute-start | bytes 933896 | tf_op jit(solution)/shard_map/ppermute | solution.py:36
  34.0 9.3 %collective-permute-start.9 = (f32[304,256]{1,0:T(8,128)S(1)}, f32[304,256]{1,0:T(8,128)S(1)}, u32[]{:S(2)}, u32[]{:S(2)}) collective-permute-start(f32[304,256]{1,0:T(8,128)S(1)} %get-tuple-element.72), channel_id=1, source_target_pairs={{0,32},{1,33},{2,34},{3,35},{4,12},{5,13},{6,14},{7,15},{8,40},{9,... | collective-permute-start | bytes 933896 | tf_op jit(solution)/shard_map/ppermute | solution.py:36
  35.3 12.0 %collective-permute-start.12 = (f32[304,256]{1,0:T(8,128)S(1)}, f32[304,256]{1,0:T(8,128)S(1)}, u32[]{:S(2)}, u32[]{:S(2)}) collective-permute-start(f32[304,256]{1,0:T(8,128)S(1)} %get-tuple-element.72), channel_id=1, source_target_pairs={{0,96},{1,97},{2,98},{3,99},{4,28},{5,29},{6,30},{7,31},{8,104},{9... | collective-permute-start | bytes 933896 | tf_op jit(solution)/shard_map/ppermute | solution.py:36
  36.7 10.6 %collective-permute-start.11 = (f32[304,256]{1,0:T(8,128)S(1)}, f32[304,256]{1,0:T(8,128)S(1)}, u32[]{:S(2)}, u32[]{:S(2)}) collective-permute-start(f32[304,256]{1,0:T(8,128)S(1)} %get-tuple-element.76), channel_id=1, source_target_pairs={{0,96},{1,97},{2,98},{3,99},{4,28},{5,29},{6,30},{7,31},{8,104},{9... | collective-permute-start | bytes 933896 | tf_op jit(solution)/shard_map/ppermute | solution.py:36
  43.3 21.8 %collective-permute-start.10 = (f32[1216,256]{1,0:T(8,128)S(1)}, f32[1216,256]{1,0:T(8,128)S(1)}, u32[]{:S(2)}, u32[]{:S(2)}) collective-permute-start(f32[1216,256]{1,0:T(8,128)S(1)} %constant_dynamic-update-slice_fusion.4), channel_id=1, source_target_pairs={{0,1},{1,2},{2,3},{3,0},{4,36},{5,37},{6,38},{7,39},{8,9},{9,10},{... | collective-permute-start | bytes 3735560 | tf_op jit(solution)/shard_map/ppermute | solution.py:36
  44.7 7.3 %collective-permute-start.13 = (f32[304,256]{1,0:T(8,128)S(1)}, f32[304,256]{1,0:T(8,128)S(1)}, u32[]{:S(2)}, u32[]{:S(2)}) collective-permute-start(f32[304,256]{1,0:T(8,128)S(1)} %collective-permute-done.8), channel_id=1, source_target_pairs={{0,32},{1,33},{2,34},{3,35},{4,12},{5,13},{6,14},{7,15},{8,40},{9,... | collective-permute-start | bytes 933896 | tf_op jit(solution)/shard_map/ppermute | solution.py:36
  45.0 32.9 %collective-permute-start.17 = (f32[1216,256]{1,0:T(8,128)S(1)}, f32[1216,256]{1,0:T(8,128)S(1)}, u32[]{:S(2)}, u32[]{:S(2)}) collective-permute-start(f32[1216,256]{1,0:T(8,128)S(1)} %constant_dynamic-update-slice_fusion.4), channel_id=1, source_target_pairs={{0,3},{1,0},{2,1},{3,2},{4,100},{5,101},{6,102},{7,103},{8,11},{9,... | collective-permute-start | bytes 3735560 | tf_op jit(solution)/shard_map/ppermute | solution.py:36
  47.3 6.4 %collective-permute-start.14 = (f32[304,256]{1,0:T(8,128)S(1)}, f32[304,256]{1,0:T(8,128)S(1)}, u32[]{:S(2)}, u32[]{:S(2)}) collective-permute-start(f32[304,256]{1,0:T(8,128)S(1)} %collective-permute-done.12), channel_id=1, source_target_pairs={{0,96},{1,97},{2,98},{3,99},{4,28},{5,29},{6,30},{7,31},{8,104},{9... | collective-permute-start | bytes 933896 | tf_op jit(solution)/shard_map/ppermute | solution.py:36
  53.8 24.6 %collective-permute-start.18 = (f32[1216,256]{1,0:T(8,128)S(1)}, f32[1216,256]{1,0:T(8,128)S(1)}, u32[]{:S(2)}, u32[]{:S(2)}) collective-permute-start(f32[1216,256]{1,0:T(8,128)S(1)} %constant_dynamic-update-slice_fusion.10), channel_id=1, source_target_pairs={{0,1},{1,2},{2,3},{3,0},{4,36},{5,37},{6,38},{7,39},{8,9},{9,10},{... | collective-permute-start | bytes 3735560 | tf_op jit(solution)/shard_map/ppermute | solution.py:36
  53.9 17.4 %collective-permute-start.15 = (f32[608,256]{1,0:T(8,128)S(1)}, f32[608,256]{1,0:T(8,128)S(1)}, u32[]{:S(2)}, u32[]{:S(2)}) collective-permute-start(f32[608,256]{1,0:T(8,128)S(1)} %pad_maximum_fusion), channel_id=1, source_target_pairs={{0,3},{1,0},{2,1},{3,2},{4,100},{5,101},{6,102},{7,103},{8,11},{9,... | collective-permute-start | bytes 1867784 | tf_op jit(solution)/shard_map/ppermute | solution.py:36
  61.5 1.8 %copy-start = (bf16[4,192,2432]{2,1,0:T(8,128)(2,1)}, bf16[4,192,2432]{2,1,0:T(8,128)(2,1)S(1)}, u32[]{:S(2)}) copy-start(bf16[4,192,2432]{2,1,0:T(8,128)(2,1)S(1)} %get-tuple-element.55.other_low) | copy-start | bytes 11206660
  63.3 14.7 %collective-permute-start.16 = (f32[608,256]{1,0:T(8,128)S(1)}, f32[608,256]{1,0:T(8,128)S(1)}, u32[]{:S(2)}, u32[]{:S(2)}) collective-permute-start(f32[608,256]{1,0:T(8,128)S(1)} %pad_maximum_fusion.1), channel_id=1, source_target_pairs={{0,3},{1,0},{2,1},{3,2},{4,100},{5,101},{6,102},{7,103},{8,11},{9,... | collective-permute-start | bytes 1867784 | tf_op jit(solution)/shard_map/ppermute | solution.py:36
  65.0 27.4 %collective-permute-start.19 = (f32[1216,256]{1,0:T(8,128)S(1)}, f32[1216,256]{1,0:T(8,128)S(1)}, u32[]{:S(2)}, u32[]{:S(2)}) collective-permute-start(f32[1216,256]{1,0:T(8,128)S(1)} %collective-permute-done.10), channel_id=1, source_target_pairs={{0,1},{1,2},{2,3},{3,0},{4,36},{5,37},{6,38},{7,39},{8,9},{9,10},{... | collective-permute-start | bytes 3735560 | tf_op jit(solution)/shard_map/ppermute | solution.py:36
  71.3 21.2 %collective-permute-start.21 = (f32[608,256]{1,0:T(8,128)S(1)}, f32[608,256]{1,0:T(8,128)S(1)}, u32[]{:S(2)}, u32[]{:S(2)}) collective-permute-start(f32[608,256]{1,0:T(8,128)S(1)} %collective-permute-done.15), channel_id=1, source_target_pairs={{0,3},{1,0},{2,1},{3,2},{4,100},{5,101},{6,102},{7,103},{8,11},{9,... | collective-permute-start | bytes 1867784 | tf_op jit(solution)/shard_map/ppermute | solution.py:36
  78.4 14.1 %collective-permute-start.20 = (f32[608,256]{1,0:T(8,128)S(1)}, f32[608,256]{1,0:T(8,128)S(1)}, u32[]{:S(2)}, u32[]{:S(2)}) collective-permute-start(f32[608,256]{1,0:T(8,128)S(1)} %collective-permute-done.16), channel_id=1, source_target_pairs={{0,3},{1,0},{2,1},{3,2},{4,100},{5,101},{6,102},{7,103},{8,11},{9,... | collective-permute-start | bytes 1867784 | tf_op jit(solution)/shard_map/ppermute | solution.py:36
  96.0 2.0 %collective-permute-start.22 = (f32[192,256]{1,0:T(8,128)S(1)}, f32[192,256]{1,0:T(8,128)S(1)}, u32[]{:S(2)}, u32[]{:S(2)}) collective-permute-start(f32[192,256]{1,0:T(8,128)S(1)} %get-tuple-element.68), channel_id=1, source_target_pairs={{0,4},{1,5},{2,6},{3,7},{4,0},{5,1},{6,2},{7,3},{8,12},{9,13},{10,... | collective-permute-start | bytes 589832 | tf_op jit(solution)/shard_map/ppermute | solution.py:36
